TPU v7x, 32 devices: a whole 2x2x4 slice. The times are simulated.
32 devices in a mesh: feat: 16 (over z, y, x), rows: 2 (over core).
Axes of the slice: x: 2, y: 2, z: 4, core: 2. Of those that a mesh axis runs over, the one named last changes fastest.
Arguments:
- embeddings: bfloat16 [256, 512], P('rows'), may hold values from -6 to 6
- sign_flips: float32 [524288], P('feat'), may hold values from -1 to 1, as said below
- gaussian: float32 [524288], P('feat'), may hold values from -5 to 5
- scales: float32 [524288], P('feat'), may hold values from 0.5 to 2
- phases: float32 [524288], P('feat'), may hold values from 0 to 6.2831855
- source_blocks: int32 [4096], P('feat'), may hold values from 0 to 4095, as said below
- block_permutations: bfloat16 [4096, 128, 128], P('feat'), may hold values from 0 to 1, as said below
- weights: float32 [524288], P('feat'), may hold values from -6 to 6
- targets: float32 [256], P('rows'), may hold values from -6 to 6
Outputs:
- predictions: float32 [256], P('rows')
- feature_grad: float32 [524288], P(('feat', 'rows'))
Inputs may be any that keep to these rules, and one draw needn't show every extreme that they name: `sign_flips`: each entry is -1 or 1. `source_blocks`: A permutation of the 4096 block numbers. The 256 entries of each aligned run of 256 entries name exactly 16 blocks from every aligned run of 256 blocks. Each block_permutations[b] is a permutation matrix.
All inputs are finite; a program needn't handle non-finite values.
Results may differ from a plain program's by a relative error of at most 0.0003.
Values sent between devices are 32-bit elements; how exact they have to be, the bound alone decides.
No kernel may reach another device: no remote copies, remote signals or barrier semaphores. Data moves between devices by JAX's collectives and lax.ppermute only.
A program may use at most 128 MiB of HBM per device.

v0:
```python
import math

import jax
import jax.numpy as jnp
from jax import lax
from jax.sharding import PartitionSpec as P

FEATURE_COUNT = 524288


def rademacher_signs(length):
    indices = jnp.arange(length, dtype=jnp.int32)
    joined = jnp.bitwise_and(indices[:, None], indices[None, :])
    parity = jnp.zeros((length, length), jnp.int32)
    for bit_number in range(length.bit_length() - 1):
        parity = parity + jnp.bitwise_and(jnp.right_shift(joined, bit_number), 1)
    return (1 - 2 * jnp.bitwise_and(parity, 1)).astype(jnp.float32)


def transform(field, block):
    row_count = field.shape[0]
    feat_here = field.shape[1]
    outer = feat_here // block
    values = field.reshape(row_count, outer, block)
    values = jnp.einsum(
        "rac,dc->rad", values, rademacher_signs(block), precision=lax.Precision.HIGHEST
    )
    values = jnp.einsum(
        "rac,ba->rbc", values, rademacher_signs(outer), precision=lax.Precision.HIGHEST
    )
    device_shards = lax.axis_size("feat")
    spread = values.reshape(row_count, device_shards, feat_here // device_shards)
    across_devices = lax.all_to_all(spread, "feat", split_axis=1, concat_axis=1, tiled=True)
    combined = jnp.einsum(
        "gwf,aw->gaf",
        across_devices,
        rademacher_signs(device_shards),
        precision=lax.Precision.HIGHEST,
    )
    returned = lax.all_to_all(combined, "feat", split_axis=1, concat_axis=1, tiled=True)
    values = returned.reshape(row_count, feat_here)
    return values * (1.0 / math.sqrt(FEATURE_COUNT))


def local(
    embeddings,
    sign_flips,
    gaussian,
    scales,
    phases,
    source_blocks,
    block_permutations,
    weights,
    targets,
):
    row_count = embeddings.shape[0]
    width = embeddings.shape[1]
    feat_here = sign_flips.shape[0]
    blk_here = block_permutations.shape[0]
    block = block_permutations.shape[1]
    device_shards = lax.axis_size("feat")
    per_pair = blk_here // device_shards
    tiled = jnp.tile(embeddings.astype(jnp.float32), (1, feat_here // width)) * sign_flips[None, :]
    first = transform(tiled, block)
    source_dev = source_blocks // blk_here
    source_local = source_blocks % blk_here
    slot_keys = source_dev * blk_here + jnp.arange(blk_here, dtype=jnp.int32)
    ordering = jnp.argsort(slot_keys)
    inverse = jnp.argsort(ordering)
    wanted = jnp.take(source_local, ordering).reshape(device_shards, per_pair)
    asked = lax.all_to_all(wanted, "feat", split_axis=0, concat_axis=0, tiled=True)
    first_blocks = first.reshape(row_count, blk_here, block)
    outgoing = jnp.take(first_blocks, asked.reshape(-1), axis=1)
    incoming = lax.all_to_all(outgoing, "feat", split_axis=1, concat_axis=1, tiled=True)
    placed = jnp.take(incoming, inverse, axis=1)
    mixed = jnp.einsum(
        "rbj,bij->rbi",
        placed,
        block_permutations.astype(jnp.float32),
        precision=lax.Precision.HIGHEST,
    )
    mixed = mixed.reshape(row_count, feat_here) * gaussian[None, :]
    second = transform(mixed, block)
    features = jnp.cos(scales[None, :] * second + phases[None, :])
    local_sum = jnp.dot(features, weights, precision=lax.Precision.HIGHEST)
    predictions = lax.psum(local_sum, "feat") * (1.0 / math.sqrt(FEATURE_COUNT))
    residual = predictions - targets
    total_rows = row_count * lax.axis_size("rows")
    grad_terms = jnp.dot(residual, features, precision=lax.Precision.HIGHEST) * (
        1.0 / math.sqrt(total_rows)
    )
    feature_grad = lax.psum_scatter(grad_terms, "rows", scatter_dimension=0, tiled=True)
    return (predictions, feature_grad)


def solution(mesh):
    in_specs = (
        P("rows", None),
        P("feat"),
        P("feat"),
        P("feat"),
        P("feat"),
        P("feat"),
        P("feat", None, None),
        P("feat"),
        P("rows"),
    )
    out_specs = (P("rows"), P(("feat", "rows")))
    return jax.shard_map(local, mesh=mesh, in_specs=in_specs, out_specs=out_specs, check_vma=False)
```

profile of v0, /device:TPU:0, one launch (start us, length us, event | category | flops | bytes accessed | tf_op | source)
XLA Modules:
  0.0 2493.8 jit_solution(17697195913247625538)
XLA Ops:
  16.0 17.4 tile.10
  33.4 18.3 fusion.11
  51.8 22.1 convolution_bitcast_fusion.1
  73.9 18.5 reshape.78
  92.4 17.7 copy.19
  124.4 309.5 %all-to-all-done = f32[128,16,2048]{2,0,1:T(8,128)} async-done(((f32[128,16,2048]{2,0,1:T(8,128)}), f32[128,16,2048]{2,0,1:T(8,128)}, u32[]{:S(2)}, u32[]{:S(2)}) %all-to-all-start) | async-done | bytes 16777248 | tf_op jit(solution)/shard_map/all_to_all | solution.py:33
  433.9 73.0 %all-to-all-start.2 = ((s32[16,1,16]{2,1,0:T(1,128)}), s32[16,1,16]{2,1,0:T(1,128)S(1)}, u32[]{:S(2)}, u32[]{:S(2)}) async-start(s32[16,1,16]{2,1,0:T(1,128)} %select_n.41), calls=%async_computation.2 | async-start | bytes 16384 | tf_op jit(solution)/shard_map/all_to_all | solution.py:71
  506.9 31.6 %fusion.18 = f32[128,16,2048]{2,1,0:T(8,128)} fusion(f32[128,16,2048]{2,0,1:T(8,128)} %all-to-all-done), kind=kOutput, calls=%fused_computation.25 | convolution fusion | flops 805310464 | bytes 33554432 | tf_op jit(solution)/shard_map/gwf,aw->gaf/dot_general | solution.py:34
  538.6 17.7 copy.21
  564.5 309.7 %all-to-all-done.1 = f32[128,16,2048]{2,0,1:T(8,128)} async-done(((f32[128,16,2048]{2,0,1:T(8,128)}), f32[128,16,2048]{2,0,1:T(8,128)}, u32[]{:S(2)}, u32[]{:S(2)}) %all-to-all-start.1) | async-done | bytes 16777248 | tf_op jit(solution)/shard_map/all_to_all | solution.py:40
  874.2 17.6 copy.22
  891.8 11.4 broadcast_multiply_fusion
  903.2 17.5 copy.23
  920.6 17.7 gather_fusion.1
  938.3 11.6 select_bitcast_fusion
  949.9 73.7 %all-to-all-start.3 = ((f32[128,256,128]{2,0,1:T(8,128)}), f32[128,256,128]{2,0,1:T(8,128)}, u32[]{:S(2)}, u32[]{:S(2)}) async-start(f32[128,256,128]{2,0,1:T(8,128)} %select_bitcast_fusion), calls=%async_computation.3 | async-start | bytes 33554432 | tf_op jit(solution)/shard_map/all_to_all | solution.py:74
  1026.8 304.9 %all-to-all-done.3 = f32[128,256,128]{2,0,1:T(8,128)} async-done(((f32[128,256,128]{2,0,1:T(8,128)}), f32[128,256,128]{2,0,1:T(8,128)}, u32[]{:S(2)}, u32[]{:S(2)}) %all-to-all-start.3) | async-done | bytes 16777248 | tf_op jit(solution)/shard_map/all_to_all | solution.py:74
  1331.7 17.7 gather_fusion.2
  1349.4 25.3 %multiply_bitcast_fusion = f32[128,256,128]{2,0,1:T(8,128)} fusion(bf16[256,128,128]{2,1,0:T(8,128)(2,1)} %param.17, f32[256,128,128]{2,1,0:T(8,128)} %gather_fusion.2, f32[256,128]{1,0:T(8,128)S(1)} %bitcast.59, pred[256]{0:T(512)(128)(4,1)S(1)} %compare_and_fusion), kind=kOutput, calls=%fused_computation.16 | convolution fusion | flops 6450839552 | bytes 42074368 | tf_op jit(solution)/shard_map/rbj,bij->rbi/dot_general | solution.py:76
  1374.7 29.8 %fusion.6 = f32[128,256,128]{2,1,0:T(8,128)} fusion(f32[128,256,128]{2,0,1:T(8,128)} %multiply_bitcast_fusion), kind=kOutput, calls=%fused_computation.10 | convolution fusion | flops 6442860544 | bytes 33554432 | tf_op jit(solution)/shard_map/rac,dc->rad/dot_general | solution.py:25
  1404.4 22.3 convolution_bitcast_fusion
  1426.7 18.0 reshape.80
  1444.7 15.2 copy.25
  1460.0 433.5 %all_to_all.31 = f32[128,16,2048]{2,0,1:T(8,128)} all-to-all(f32[128,16,2048]{2,0,1:T(8,128)S(1)} %copy.25), channel_id=1, replica_groups=mesh['feat'=16,'rows'=2] {'feat'}, dimensions={1} | all-to-all | bytes 33554432 | tf_op jit(solution)/shard_map/all_to_all | solution.py:33
  1893.4 32.0 %fusion.21 = f32[128,16,2048]{2,1,0:T(8,128)} fusion(f32[128,16,2048]{2,0,1:T(8,128)} %all_to_all.31), kind=kOutput, calls=%fused_computation.26 | convolution fusion | flops 805310464 | bytes 33554432 | tf_op jit(solution)/shard_map/gwf,aw->gaf/dot_general | solution.py:34
  1925.5 17.7 copy.27
  1948.6 307.5 %all-to-all-done.5 = f32[128,16,2048]{2,0,1:T(8,128)} async-done(((f32[128,16,2048]{2,0,1:T(8,128)}), f32[128,16,2048]{2,0,1:T(8,128)}, u32[]{:S(2)}, u32[]{:S(2)}) %all-to-all-start.5) | async-done | bytes 16777248 | tf_op jit(solution)/shard_map/all_to_all | solution.py:40
  2256.0 17.6 copy.28
  2273.6 58.5 %fusion.1 = f32[128,32768]{0,1:T(8,128)S(1)} fusion(f32[128,16,2048]{0,2,1:T(8,128)} %copy.28, f32[32768]{0:T(1024)S(1)} %copy-done.4, f32[32768]{0:T(1024)S(1)} %broadcast_multiply_fusion.2), kind=kLoop, calls=%fused_computation.5 | loop fusion | flops 8388608 | bytes 33816576 | tf_op jit(solution)/shard_map/cos | solution.py:84
  2347.1 105.2 %psum.7 = f32[128]{0:T(128)S(1)} all-reduce(f32[128]{0:T(128)S(1)} %convolution_bitcast_fusion.2), channel_id=1, replica_groups=mesh['feat'=16,'rows'=2] {'feat'}, use_global_device_ids=true, to_apply=%region_2.4 | all-reduce | flops 128 | bytes 1024 | tf_op jit(solution)/shard_map/psum | solution.py:86
  2452.3 16.5 fusion.44
  2470.7 14.6 all-reduce.3.cloned.1.call-done
  (52 shorter events, 57.6 us)
Async XLA Ops:
  7.2 2324.9 %copy-start = (f32[32768]{0:T(1024)S(1)}, f32[32768]{0:T(1024)}, u32[]{:S(2)}) copy-start(f32[32768]{0:T(1024)} %param.18) | copy-start | bytes 393220
  16.0 17.4 copy-start.2
  110.0 8.5 copy-start.6
  110.0 323.9 %all-to-all-start = ((f32[128,16,2048]{2,0,1:T(8,128)}), f32[128,16,2048]{2,0,1:T(8,128)}, u32[]{:S(2)}, u32[]{:S(2)}) async-start(f32[128,16,2048]{2,0,1:T(8,128)} %copy.19), calls=%async_computation | async-start | bytes 33554432 | tf_op jit(solution)/shard_map/all_to_all | solution.py:33
  433.9 122.3 %all-to-all-start.2 = ((s32[16,1,16]{2,1,0:T(1,128)}), s32[16,1,16]{2,1,0:T(1,128)S(1)}, u32[]{:S(2)}, u32[]{:S(2)}) async-start(s32[16,1,16]{2,1,0:T(1,128)} %select_n.41), calls=%async_computation.2 | async-start | bytes 16384 | tf_op jit(solution)/shard_map/all_to_all | solution.py:71
  556.3 317.9 %all-to-all-start.1 = ((f32[128,16,2048]{2,0,1:T(8,128)}), f32[128,16,2048]{2,0,1:T(8,128)}, u32[]{:S(2)}, u32[]{:S(2)}) async-start(f32[128,16,2048]{2,0,1:T(8,128)} %copy.21), calls=%async_computation.1 | async-start | bytes 33554432 | tf_op jit(solution)/shard_map/all_to_all | solution.py:40
  949.9 381.8 %all-to-all-start.3 = ((f32[128,256,128]{2,0,1:T(8,128)}), f32[128,256,128]{2,0,1:T(8,128)}, u32[]{:S(2)}, u32[]{:S(2)}) async-start(f32[128,256,128]{2,0,1:T(8,128)} %select_bitcast_fusion), calls=%async_computation.3 | async-start | bytes 33554432 | tf_op jit(solution)/shard_map/all_to_all | solution.py:74
  1026.8 322.6 %copy-start.3 = (f32[32768]{0:T(1024)S(1)}, f32[32768]{0:T(1024)}, u32[]{:S(2)}) copy-start(f32[32768]{0:T(1024)} %param.13) | copy-start | bytes 393220
  1943.2 5.3 copy-start.5
  1943.2 312.8 %all-to-all-start.5 = ((f32[128,16,2048]{2,0,1:T(8,128)}), f32[128,16,2048]{2,0,1:T(8,128)}, u32[]{:S(2)}, u32[]{:S(2)}) async-start(f32[128,16,2048]{2,0,1:T(8,128)} %copy.27), calls=%async_computation.5 | async-start | bytes 33554432 | tf_op jit(solution)/shard_map/all_to_all | solution.py:40
  1948.5 536.8 %all-reduce.3.cloned.1.call-start = ((), (), s32[]{:S(2)}) async-start(), calls=%async_computation.6 | async-start | bytes 262144
  1948.6 325.0 %copy-start.4 = (f32[32768]{0:T(1024)S(1)}, f32[32768]{0:T(1024)}, u32[]{:S(2)}) copy-start(f32[32768]{0:T(1024)} %param.15) | copy-start | bytes 393220
  2332.1 5.7 copy-start.1
  2332.1 120.2 %copy-start.7 = (f32[128]{0:T(128)S(1)}, f32[128]{0:T(128)}, u32[]{:S(2)}) copy-start(f32[128]{0:T(128)} %param.19) | copy-start | bytes 1540
  2337.8 131.7 %copy-start.9 = (u32[32]{0:T(128)S(1)}, u32[32]{0:T(128)}, u32[]{:S(2)}) copy-start(u32[32]{0:T(128)} %constant.84) | copy-start | bytes 388
  2452.3 34.5 %copy-start.8 = (f32[128]{0:T(128)}, f32[128]{0:T(128)S(1)}, u32[]{:S(2)}) copy-start(f32[128]{0:T(128)S(1)} %broadcast_multiply_fusion.3) | copy-start | bytes 1540
Sparse Core Ops, SparseCore 0:
  2469.6 15.6 all-reduce.2
where the time goes:
time: 2510 us; the launch traced here: 2490 us
  waiting for transfers between devices  1250 us (50%)
  blocking collectives  539 us (21%)
  local copies, waits for them, and re-layouts  230 us (9%)
  matrix products  207 us (8%)
  starting transfers between devices  168 us (7%)
  other arithmetic  89.2 us (4%)
    all_to_all x2, waiting for transfers between devices, transform(): lax.all_to_all(combined, 'feat', split_axis=1, concat_axis=1, tiled=True)  617 us
    all_to_all x1, blocking collectives, transform(): lax.all_to_all(spread, 'feat', split_axis=1, concat_axis=1, tiled=True)  433 us
    all_to_all x1, waiting for transfers between devices, transform(): lax.all_to_all(spread, 'feat', split_axis=1, concat_axis=1, tiled=True)  309 us
    all_to_all x1, waiting for transfers between devices, local(): lax.all_to_all(outgoing, 'feat', split_axis=1, concat_axis=1, tiled=True)  305 us
    psum x1, blocking collectives, local(): predictions = lax.psum(local_sum, 'feat') * (1.0 / math.sqrt(FEATURE_COUNT))  105 us
    all_to_all x1, starting transfers between devices, local(): lax.all_to_all(outgoing, 'feat', split_axis=1, concat_axis=1, tiled=True)  73.7 us
    all_to_all x1, starting transfers between devices, local(): lax.all_to_all(wanted, 'feat', split_axis=0, concat_axis=0, tiled=True)  73 us
    reshape x4, local copies, waits for them, and re-layouts, transform(): values.reshape(row_count, device_shards, feat_here // device_shards)  69.4 us
  transfers between devices with their start and end apart: 6, of which 5 were waited for; matrix products, arithmetic and copies ran while one was open for 2% of the time, Pallas kernels for 0%

commit v1 on v0

v1 whole, which is shorter than its diff:
```python
import functools
import math

import jax
import jax.numpy as jnp
import numpy as np
from jax import lax
from jax.experimental import pallas as pl
from jax.experimental.pallas import tpu as pltpu
from jax.sharding import PartitionSpec as P

LANES = 128
CHUNK = 256
BOTH = ("feat", "rows")
MIB = 1024 * 1024


def hadamard(length):
    matrix = np.ones((1, 1), np.float32)
    while matrix.shape[0] < length:
        matrix = np.block([[matrix, matrix], [matrix, -matrix]])
    return matrix


def halves(values):
    high = values.astype(jnp.bfloat16)
    low = (values - high.astype(jnp.float32)).astype(jnp.bfloat16)
    return high, low


def swap(values, axis_name, bit):
    size = lax.axis_size(axis_name)
    return lax.ppermute(values, axis_name, [(i, i ^ bit) for i in range(size)])


def descending_bits(axis_name):
    bit = lax.axis_size(axis_name) // 2
    while bit:
        yield bit
        bit //= 2


def gather_all(piece, axes=BOTH):
    shape = piece.shape
    held = piece[None]
    for axis_name in axes:
        index = lax.axis_index(axis_name)
        for bit in descending_bits(axis_name):
            other = swap(held, axis_name, bit)
            upper = (index & bit) != 0
            held = jnp.where(
                upper, jnp.stack([other, held], 1), jnp.stack([held, other], 1)
            ).reshape((-1,) + shape)
    return held


def scatter_sum(terms):
    core = lax.axis_index("rows")
    for bit in descending_bits("rows"):
        count = terms.shape[1] // 2
        pair = terms.reshape((terms.shape[0], 2, count) + terms.shape[2:])
        mine = (core & bit) // bit
        keep = lax.dynamic_index_in_dim(pair, mine, 1, False)
        send = lax.dynamic_index_in_dim(pair, 1 - mine, 1, False)
        terms = keep + swap(send, "rows", bit)
    terms = terms[:, 0]
    place = lax.axis_index("feat")
    done = 1
    size = lax.axis_size("feat")
    bit = 1
    while bit < size:
        pair = terms.reshape((size // (2 * bit), 2) + terms.shape[1:])
        mine = (place & bit) // bit
        keep = lax.dynamic_index_in_dim(pair, mine, 1, False)
        send = lax.dynamic_index_in_dim(pair, 1 - mine, 1, False)
        terms = keep + swap(send, "feat", bit)
        bit *= 2
    return terms.reshape(terms.shape[1:])


def mix_kernel(rows, src_ref, sign_ref, order_ref, gain_ref, emb_ref, lane_ref, block_ref, out_ref, spread_ref):
    f32 = jnp.float32
    source = jnp.concatenate(
        [
            jnp.broadcast_to(src_ref[0, pl.ds(half, 1), :], (LANES, LANES)).T
            for half in range(CHUNK // LANES)
        ],
        axis=0,
    )
    source = source.astype(jnp.int32)
    lane = lax.broadcasted_iota(jnp.int32, (CHUNK, LANES), 1)
    major = source >> 2

    def flip(bits):
        return (1 - 2 * (bits & 1)).astype(f32)

    tiles = [flip(lax.population_count(major & lane))]
    for shift in range(7, 10):
        turn = flip(major >> shift)
        tiles = tiles + [tile * turn for tile in tiles]
    signs = jnp.concatenate([tile.astype(jnp.bfloat16) for tile in tiles], axis=1)
    sums = jnp.dot(signs, sign_ref[...], preferred_element_type=f32)
    first_flip = flip(source)
    second_flip = flip(source >> 1)
    quarter = [
        sums[:, 0:128],
        sums[:, 128:256] * first_flip,
        sums[:, 256:384] * second_flip,
        sums[:, 384:512] * (first_flip * second_flip),
    ]
    order = order_ref[...].reshape(CHUNK, LANES).astype(jnp.int32)
    gain = gain_ref[...].reshape(CHUNK, LANES)
    for r in range(rows):
        total = quarter[0] * emb_ref[pl.ds(r, 1), 0:128]
        for q in range(1, 4):
            total = total + quarter[q] * emb_ref[pl.ds(r, 1), 128 * q : 128 * (q + 1)]
        first = jnp.dot(
            jnp.concatenate(halves(total), axis=1), lane_ref[...], preferred_element_type=f32
        )
        mixed = jnp.take_along_axis(first, order, axis=1) * gain
        across = jnp.dot(
            jnp.concatenate(halves(mixed), axis=1), lane_ref[...], preferred_element_type=f32
        )
        high, low = halves(across)
        spread_ref[0:CHUNK, r * LANES : (r + 1) * LANES] = high
        spread_ref[CHUNK:, r * LANES : (r + 1) * LANES] = low
    result = jnp.dot(block_ref[...], spread_ref[...], preferred_element_type=f32)
    for r in range(rows):
        out_ref[0, r] = result[:, r * LANES : (r + 1) * LANES]


def turn_cosine_coefficients(degree):
    points = np.cos(np.pi * (np.arange(400) + 0.5) / 400)
    u = 0.5 * points
    fit = np.polynomial.chebyshev.Chebyshev.fit(u * u, np.cos(2 * np.pi * u), degree, domain=[0, 0.25])
    return [float(c) for c in fit.convert(kind=np.polynomial.Polynomial).coef]


def head_kernel(rows, chunks, tile, coefs, y_ref, scale_ref, phase_ref, weight_ref, target_ref, pred_ref, grad_ref, feat_ref, acc_ref, *, grad_scale):
    f32 = jnp.float32
    step = pl.program_id(0)
    steps = pl.num_programs(0)

    @pl.when(step == 0)
    def _():
        acc_ref[...] = jnp.zeros_like(acc_ref)

    for part in range(tile // 8):
        here = slice(part * 8, part * 8 + 8)
        for r in range(rows):
            values = [y_ref[k, r, here, :] for k in range(chunks)]
            width = 1
            while width < chunks:
                for k in range(chunks):
                    if not k & width:
                        a, b = values[k], values[k | width]
                        values[k], values[k | width] = a + b, a - b
                width *= 2
            acc = acc_ref[r]
            for k in range(chunks):
                turns = values[k] * scale_ref[k, 0, here, :] + phase_ref[k, 0, here, :]
                u = turns - jnp.round(turns)
                square = u * u
                cosine = jnp.full_like(square, coefs[-1])
                for c in coefs[-2::-1]:
                    cosine = cosine * square + c
                feat_ref[k, r, pl.ds(pl.multiple_of(step * tile + part * 8, 8), 8), :] = cosine
                acc = acc + cosine * weight_ref[k, 0, here, :]
            acc_ref[r] = acc

    @pl.when(step == steps - 1)
    def _():
        residuals = []
        for r in range(rows):
            total = jnp.sum(jnp.sum(acc_ref[r], axis=0, keepdims=True), axis=1, keepdims=True)
            pred_ref[pl.ds(r, 1), :] = jnp.broadcast_to(total, (1, LANES))
            residuals.append(jnp.broadcast_to((total - target_ref[r]) * grad_scale, (8, LANES)))

        for k in range(chunks):

            @pl.loop(0, CHUNK // 8)
            def _(i):
                rows_here = pl.ds(pl.multiple_of(i * 8, 8), 8)
                total = feat_ref[k, 0, rows_here, :] * residuals[0]
                for r in range(1, rows):
                    total = total + feat_ref[k, r, rows_here, :] * residuals[r]
                grad_ref[k, rows_here, :] = total


def local(
    embeddings,
    sign_flips,
    gaussian,
    scales,
    phases,
    source_blocks,
    block_permutations,
    weights,
    targets,
):
    f32 = jnp.float32
    feat_size = lax.axis_size("feat")
    rows_size = lax.axis_size("rows")
    place = lax.axis_index("feat")
    core = lax.axis_index("rows")
    devices = feat_size * rows_size
    width = embeddings.shape[1]
    rows = embeddings.shape[0] // feat_size
    total_rows = embeddings.shape[0] * rows_size
    features = sign_flips.shape[0] * feat_size
    blocks = features // LANES
    mine = blocks // devices
    quarters = width // LANES
    chunks = blocks // CHUNK
    per_chunk = CHUNK // mine

    def half(values):
        parts = values.reshape((rows_size, values.shape[0] // rows_size) + values.shape[1:])
        return lax.dynamic_index_in_dim(parts, core, 0, False)

    def rows_of(values):
        return half(values).reshape(mine, LANES)

    positions = jnp.einsum(
        "bij,j->bi", half(block_permutations), jnp.arange(LANES).astype(jnp.bfloat16), preferred_element_type=f32
    )
    early = jnp.concatenate([rows_of(sign_flips), positions, rows_of(gaussian)], axis=0)
    late = jnp.concatenate(
        [
            rows_of(scales) * f32(1.0 / (2.0 * math.pi * features)),
            rows_of(phases) * f32(1.0 / (2.0 * math.pi)),
            rows_of(weights) * f32(1.0 / math.sqrt(features)),
        ],
        axis=0,
    )
    numbers = gather_all(half(source_blocks).astype(f32))
    early = gather_all(early)
    late = gather_all(late)

    numbers = numbers.reshape(chunks, CHUNK // LANES, LANES)
    signs = early[:, :mine].reshape(blocks // quarters, width).astype(jnp.bfloat16)
    emb = lax.dynamic_slice_in_dim(embeddings, place * rows, rows, 0).astype(f32)
    lane_matrix = jnp.asarray(np.concatenate([hadamard(LANES)] * 2, 0), jnp.bfloat16)
    block_matrix = jnp.asarray(np.concatenate([hadamard(CHUNK)] * 2, 1), jnp.bfloat16)

    def early_part(which):
        return pl.BlockSpec((per_chunk, mine, LANES), lambda k: (k, which, 0))

    spread = pl.pallas_call(
        functools.partial(mix_kernel, rows),
        grid=(chunks,),
        in_specs=[
            pl.BlockSpec((1, CHUNK // LANES, LANES), lambda k: (k, 0, 0)),
            pl.BlockSpec((blocks // quarters, width), lambda k: (0, 0)),
            early_part(1),
            early_part(2),
            pl.BlockSpec((rows, width), lambda k: (0, 0)),
            pl.BlockSpec((2 * LANES, LANES), lambda k: (0, 0)),
            pl.BlockSpec((CHUNK, 2 * CHUNK), lambda k: (0, 0)),
        ],
        out_specs=pl.BlockSpec((1, rows, CHUNK, LANES), lambda k: (k, 0, 0, 0)),
        out_shape=jax.ShapeDtypeStruct((chunks, rows, CHUNK, LANES), f32),
        scratch_shapes=[pltpu.VMEM((2 * CHUNK, rows * LANES), jnp.bfloat16)],
        compiler_params=pltpu.CompilerParams(vmem_limit_bytes=48 * MIB),
        name="mix",
    )(numbers, signs, early, early, emb, lane_matrix, block_matrix)

    tile = min(16, mine)
    tiles_here = mine // tile
    late = late.reshape(chunks, per_chunk, 3 * mine, LANES)

    def late_part(which):
        return pl.BlockSpec(
            (chunks, 1, tile, LANES), lambda i: (0, i // tiles_here, which * tiles_here + i % tiles_here, 0)
        )

    my_targets = lax.dynamic_slice_in_dim(targets, place * rows, rows, 0)
    preds, grads = pl.pallas_call(
        functools.partial(
            head_kernel, rows, chunks, tile, turn_cosine_coefficients(6), grad_scale=1.0 / math.sqrt(total_rows)
        ),
        grid=(CHUNK // tile,),
        in_specs=[
            pl.BlockSpec((chunks, rows, tile, LANES), lambda i: (0, 0, i, 0)),
            late_part(0),
            late_part(1),
            late_part(2),
            pl.BlockSpec(memory_space=pltpu.SMEM),
        ],
        out_specs=[
            pl.BlockSpec((rows, LANES), lambda i: (0, 0)),
            pl.BlockSpec((chunks, CHUNK, LANES), lambda i: (0, 0, 0)),
        ],
        out_shape=[
            jax.ShapeDtypeStruct((rows, LANES), f32),
            jax.ShapeDtypeStruct((chunks, CHUNK, LANES), f32),
        ],
        scratch_shapes=[
            pltpu.VMEM((chunks, rows, CHUNK, LANES), f32),
            pltpu.VMEM((rows, 8, LANES), f32),
        ],
        compiler_params=pltpu.CompilerParams(vmem_limit_bytes=48 * MIB),
        name="head",
    )(spread, late, late, late, my_targets)

    predictions = gather_all(preds[:, 0], ("feat",)).reshape(-1)
    feature_grad = scatter_sum(grads.reshape(feat_size, rows_size, mine, LANES))
    return predictions, feature_grad.reshape(-1)


def solution(mesh):
    in_specs = (
        P("rows", None),
        P("feat"),
        P("feat"),
        P("feat"),
        P("feat"),
        P("feat"),
        P("feat", None, None),
        P("feat"),
        P("rows"),
    )
    out_specs = (P("rows"), P(("feat", "rows")))
    return jax.shard_map(local, mesh=mesh, in_specs=in_specs, out_specs=out_specs, check_vma=False)
```

time: 2510 us -> 262 us (0.10)
  waiting for transfers between devices: 1250 us -> 130 us
  blocking collectives: 539 us -> 0 us
  local copies, waits for them, and re-layouts: 230 us -> 8.65 us
  matrix products: 207 us -> 3.37 us
  starting transfers between devices: 168 us -> 34 us
  other arithmetic: 89.2 us -> 28.4 us
  Pallas kernels: 0 us -> 56.4 us
    all_to_all x5 -> x0, waiting for transfers between devices: 1230 us -> none  [the longest x2 617 us: transform(): lax.all_to_all(combined, 'feat', split_axis=1, concat_axis=1, tiled=True)]
    all_to_all x1 -> x0, blocking collectives: 433 us -> none  [transform(): lax.all_to_all(spread, 'feat', split_axis=1, concat_axis=1, tiled=True)]
    dot_general x9 -> x1, matrix products: 207 us -> 3.37 us  [local(): jnp.einsum('bij,j->bi', half(block_permutations), jnp.arange(LANES).astyp...]
    all_to_all x5 -> x0, starting transfers between devices: 167 us -> none  [the longest x1 73.7 us: local(): lax.all_to_all(outgoing, 'feat', split_axis=1, concat_axis=1, tiled=True)]
    ppermute x0 -> x24, waiting for transfers between devices: none -> 130 us  [swap(): return lax.ppermute(values, axis_name, [(i, i ^ bit) for i in range(size)])]
    psum x1 -> x0, blocking collectives: 105 us -> none  [local(): predictions = lax.psum(local_sum, 'feat') * (1.0 / math.sqrt(FEATURE_COUNT))]
    reshape x5, local copies, waits for them, and re-layouts: 69.4 us -> 3.13 us  [half(): values.reshape((rows_size, values.shape[0] // rows_size) + values.shape[1:])]
    cos x1 -> x0, other arithmetic: 58.5 us -> none  [local(): features = jnp.cos(scales[None, :] * second + phases[None, :])]
  transfers between devices with their start and end apart: 6 -> 24, of which waited for: 5 -> 19; matrix products, arithmetic and copies ran while one was open for 2% -> 8% of each run, Pallas kernels for 0% -> 0%
where the time goes in v1:
time: 262 us
  waiting for transfers between devices  130 us (50%)
  Pallas kernels  56.4 us (22%)
  starting transfers between devices  34 us (13%)
  other arithmetic  28.4 us (11%)
  local copies, waits for them, and re-layouts  8.65 us (3%)
  matrix products  3.37 us (1%)
    ppermute x24, waiting for transfers between devices, swap(): return lax.ppermute(values, axis_name, [(i, i ^ bit) for i in range(size)])  130 us
    ppermute x24, starting transfers between devices, swap(): return lax.ppermute(values, axis_name, [(i, i ^ bit) for i in range(size)])  34 us
    pallas_call x1, Pallas kernels, local(): pl.pallas_call(functools.partial(mix_kernel, rows), grid=(chunks,), in_sp...  32.1 us
    select_n x23, other arithmetic, gather_all(): jnp.where(upper, jnp.stack([other, held], 1), jnp.stack([held, other], 1))  25.2 us
    pallas_call x1, Pallas kernels, local(): pl.pallas_call(functools.partial(head_kernel, rows, chunks, tile, turn_co...  24.2 us
  transfers between devices with their start and end apart: 24, of which 19 were waited for; matrix products, arithmetic and copies ran while one was open for 8% of the time, Pallas kernels for 0%

profile of v1, /device:TPU:0, one launch (start us, length us, event | category | flops | bytes accessed | tf_op | source)
XLA Modules:
  0.0 261.6 jit_solution(11909765087447794598)
XLA Ops:
  3.7 3.4 %fusion = f32[1,128,128]{2,0,1:T(1,128)S(1)} fusion(bf16[2,128,128,128]{3,2,1,0:T(8,128)(2,1)} %bitcast.114, s32[]{:T(128)S(6)} %select_n.421), kind=kOutput, calls=%fused_computation.2 | convolution fusion | flops 4194432 | bytes 4259844 | tf_op jit(solution)/shard_map/bij,j->bi/dot_general | solution.py:224
  7.3 4.1 %collective-permute-start.5 = (f32[1,384,128]{2,1,0:T(8,128)S(1)}, f32[1,384,128]{2,1,0:T(8,128)S(1)}, u32[]{:S(2)}, u32[]{:S(2)}) collective-permute-start(f32[1,384,128]{2,1,0:T(8,128)S(1)} %get-tuple-element.8), channel_id=1, source_target_pairs={{0,16},{2,18},{4,20},{6,22},{8,24},{10,26},{12,28},{14,30},{16,0},... | collective-permute-start | bytes 589832 | tf_op jit(solution)/shard_map/ppermute | solution.py:33
  11.9 13.7 %collective-permute-done.5 = f32[1,384,128]{2,1,0:T(8,128)S(1)} collective-permute-done((f32[1,384,128]{2,1,0:T(8,128)S(1)}, f32[1,384,128]{2,1,0:T(8,128)S(1)}, u32[]{:S(2)}, u32[]{:S(2)}) %collective-permute-start.5) | collective-permute-done | bytes 196640 | tf_op jit(solution)/shard_map/ppermute | solution.py:33
  25.7 3.4 %collective-permute-done.10 = f32[1,384,128]{2,1,0:T(8,128)S(1)} collective-permute-done((f32[1,384,128]{2,1,0:T(8,128)S(1)}, f32[1,384,128]{2,1,0:T(8,128)S(1)}, u32[]{:S(2)}, u32[]{:S(2)}) %collective-permute-start.10) | collective-permute-done | bytes 196640 | tf_op jit(solution)/shard_map/ppermute | solution.py:33
  29.8 7.8 %collective-permute-done.6 = f32[2,384,128]{2,1,0:T(8,128)S(1)} collective-permute-done((f32[2,384,128]{2,1,0:T(8,128)S(1)}, f32[2,384,128]{2,1,0:T(8,128)S(1)}, u32[]{:S(2)}, u32[]{:S(2)}) %collective-permute-start.6) | collective-permute-done | bytes 393248 | tf_op jit(solution)/shard_map/ppermute | solution.py:33
  37.8 2.0 collective-permute-start.7
  39.8 6.0 %collective-permute-done.11 = f32[2,384,128]{2,1,0:T(8,128)S(1)} collective-permute-done((f32[2,384,128]{2,1,0:T(8,128)S(1)}, f32[2,384,128]{2,1,0:T(8,128)S(1)}, u32[]{:S(2)}, u32[]{:S(2)}) %collective-permute-start.11) | collective-permute-done | bytes 393248 | tf_op jit(solution)/shard_map/ppermute | solution.py:33
  47.5 10.8 %collective-permute-done.7 = f32[4,384,128]{2,1,0:T(8,128)S(1)} collective-permute-done((f32[4,384,128]{2,1,0:T(8,128)S(1)}, f32[4,384,128]{2,1,0:T(8,128)S(1)}, u32[]{:S(2)}, u32[]{:S(2)}) %collective-permute-start.7) | collective-permute-done | bytes 786464 | tf_op jit(solution)/shard_map/ppermute | solution.py:33
  60.8 2.0 collective-permute-start.8
  62.8 11.0 %collective-permute-done.12 = f32[4,384,128]{2,1,0:T(8,128)} collective-permute-done((f32[4,384,128]{2,1,0:T(8,128)S(1)}, f32[4,384,128]{2,1,0:T(8,128)}, u32[]{:S(2)}, u32[]{:S(2)}) %collective-permute-start.12) | collective-permute-done | bytes 786464 | tf_op jit(solution)/shard_map/ppermute | solution.py:33
  73.8 2.0 maximum_select_fusion.5
  77.1 21.2 %collective-permute-done.8 = f32[8,384,128]{2,1,0:T(8,128)} collective-permute-done((f32[8,384,128]{2,1,0:T(8,128)S(1)}, f32[8,384,128]{2,1,0:T(8,128)}, u32[]{:S(2)}, u32[]{:S(2)}) %collective-permute-start.8) | collective-permute-done | bytes 1572896 | tf_op jit(solution)/shard_map/ppermute | solution.py:33
  98.3 3.8 %maximum_select_fusion.2 = f32[8,2,384,128]{3,2,1,0:T(8,128)} fusion(f32[8,1,384,128]{3,2,1,0:T(8,128)S(1)} %bitcast.105, f32[8,1,384,128]{3,2,1,0:T(8,128)} %bitcast.28, pred[]{:T(512)S(6)} %ne.53), kind=kLoop, calls=%fused_computation.5 | loop fusion | flops 2359296 | bytes 6291457 | tf_op jit(solution)/shard_map/jit(_where)/select_n | solution.py:51
  102.1 26.0 %collective-permute-done.13 = f32[8,384,128]{2,1,0:T(8,128)} collective-permute-done((f32[8,384,128]{2,1,0:T(8,128)S(1)}, f32[8,384,128]{2,1,0:T(8,128)}, u32[]{:S(2)}, u32[]{:S(2)}) %collective-permute-start.13) | collective-permute-done | bytes 1572896 | tf_op jit(solution)/shard_map/ppermute | solution.py:33
  128.2 3.8 %maximum_select_fusion.3 = f32[8,2,384,128]{3,2,1,0:T(8,128)} fusion(f32[8,1,384,128]{3,2,1,0:T(8,128)S(1)} %bitcast.107, f32[8,1,384,128]{3,2,1,0:T(8,128)} %bitcast.46, pred[]{:T(512)S(6)} %ne.53), kind=kLoop, calls=%fused_computation.6 | loop fusion | flops 2359296 | bytes 6291457 | tf_op jit(solution)/shard_map/jit(_where)/select_n | solution.py:51
  132.0 2.3 collective-permute-start
  134.3 2.2 collective-permute-done
  136.5 1.8 collective-permute-start.1
  138.3 1.8 collective-permute-done.1
  141.5 2.3 collective-permute-done.2
  145.1 2.4 collective-permute-done.3
  148.8 5.8 %maximum_select_fusion = f32[16,2,384,128]{3,2,1,0:T(8,128)S(1)} fusion(f32[16,1,384,128]{3,2,1,0:T(8,128)} %bitcast.32, f32[16,1,384,128]{3,2,1,0:T(8,128)} %bitcast.31, pred[]{:T(512)S(6)} %ne.57), kind=kLoop, calls=%fused_computation | loop fusion | flops 4718592 | bytes 12582913 | tf_op jit(solution)/shard_map/jit(_where)/select_n | solution.py:51
  154.6 2.6 %copy-done.2 = f32[16,2,384,128]{3,2,1,0:T(8,128)} copy-done((f32[16,2,384,128]{3,2,1,0:T(8,128)}, f32[16,2,384,128]{3,2,1,0:T(8,128)S(1)}, u32[]{:S(2)}) %copy-start.2) | copy-done | bytes 6291480
  158.1 7.8 %maximum_select_fusion.1.scale_ref.phase_ref.weight_ref = f32[16,2,384,128]{3,2,1,0:T(8,128)} fusion(f32[16,1,384,128]{3,2,1,0:T(8,128)} %bitcast.50, f32[16,1,384,128]{3,2,1,0:T(8,128)} %bitcast.49, pred[]{:T(512)S(6)} %ne.57), kind=kLoop, calls=%fused_computation.1 | loop fusion | flops 4718592 | bytes 12582913 | tf_op jit(solution)/shard_map/jit(_where)/select_n | solution.py:51
  165.9 32.1 %mix.1.y_ref = f32[16,8,256,128]{3,2,1,0:T(8,128)} custom-call(f32[16,2,128]{2,1,0:T(2,128)S(1)} %maximum_select_fusion.12.src_ref, bf16[1024,512]{1,0:T(8,128)(2,1)S(1)} %convert_element_type.18.sign_ref, f32[32,384,128]{2,1,0:T(8,128)} %bitcast.102, f32[32,384,128]{2,1,0:T(8,128)} %bitcast.103, f32[8,512]{1,0:T(8,128)S(1)} %dynamic-slice_convert_fusion.emb_ref, ...), custom_call_target="tpu_custom_call" | custom-call | tf_op jit(solution)/shard_map/mix/pallas_call | solution.py:249
  198.1 24.2 %head.1 = (f32[8,128]{1,0:T(8,128)S(1)}, f32[16,256,128]{2,1,0:T(8,128)S(1)}) custom-call(f32[16,8,256,128]{3,2,1,0:T(8,128)} %mix.1.y_ref, f32[16,2,384,128]{3,2,1,0:T(8,128)} %maximum_select_fusion.1.scale_ref.phase_ref.weight_ref, f32[16,2,384,128]{3,2,1,0:T(8,128)} %maximum_select_fusion.1.scale_ref.phase_ref.weight_ref, ...), custom_call_target="tpu_custom_call" | custom-call | tf_op jit(solution)/shard_map/head/pallas_call | solution.py:278
  222.6 2.6 %collective-permute-done.19 = f32[16,1,128,128]{3,2,0,1:T(8,128)} collective-permute-done((f32[16,1,128,128]{3,2,0,1:T(8,128)S(1)}, f32[16,1,128,128]{3,2,0,1:T(8,128)}, u32[]{:S(2)}, u32[]{:S(2)}) %collective-permute-start.19) | collective-permute-done | bytes 1048608 | tf_op jit(solution)/shard_map/ppermute | solution.py:33
  228.0 12.7 %collective-permute-done.20 = f32[8,128,128]{2,1,0:T(8,128)S(1)} collective-permute-done((f32[8,128,128]{2,1,0:T(8,128)S(1)}, f32[8,128,128]{2,1,0:T(8,128)S(1)}, u32[]{:S(2)}, u32[]{:S(2)}) %collective-permute-start.20) | collective-permute-done | bytes 524320 | tf_op jit(solution)/shard_map/ppermute | solution.py:33
  242.3 3.0 %collective-permute-start.15 = (f32[1,8]{1,0:T(1,128)S(1)}, f32[1,8]{1,0:T(1,128)S(1)}, u32[]{:S(2)}, u32[]{:S(2)}) collective-permute-start(f32[1,8]{1,0:T(1,128)S(1)} %bitcast.141), channel_id=1, source_target_pairs={{0,16},{2,18},{4,20},{6,22},{8,24},{10,26},{12,28},{14,30},{16,0},... | collective-permute-start | bytes 104 | tf_op jit(solution)/shard_map/ppermute | solution.py:33
  246.8 2.1 collective-permute-start.16
  252.0 2.1 collective-permute-done.17
  255.7 3.0 %collective-permute-start.23 = (f32[1,128,128]{2,1,0:T(8,128)S(1)}, f32[1,128,128]{2,1,0:T(8,128)S(1)}, u32[]{:S(2)}, u32[]{:S(2)}) collective-permute-start(f32[1,128,128]{2,1,0:T(8,128)S(1)} %constant_dynamic-slice_fusion), channel_id=1, source_target_pairs={{0,16},{2,18},{4,20},{6,22},{8,24},{10,26},{12,28},{14,30},{16,0},... | collective-permute-start | bytes 196616 | tf_op jit(solution)/shard_map/ppermute | solution.py:33
  (93 shorter events, 28.6 us)
Async XLA Ops:
  0.6 10.8 %copy-start.5 = (f32[32768]{0:T(1024)S(1)}, f32[32768]{0:T(1024)}, u32[]{:S(2)}) copy-start(f32[32768]{0:T(1024)} %param.18) | copy-start | bytes 393220
  0.6 10.9 %copy-start.6 = (f32[32768]{0:T(1024)S(1)}, f32[32768]{0:T(1024)}, u32[]{:S(2)}) copy-start(f32[32768]{0:T(1024)} %param.15) | copy-start | bytes 393220
  7.3 18.3 %collective-permute-start.5 = (f32[1,384,128]{2,1,0:T(8,128)S(1)}, f32[1,384,128]{2,1,0:T(8,128)S(1)}, u32[]{:S(2)}, u32[]{:S(2)}) collective-permute-start(f32[1,384,128]{2,1,0:T(8,128)S(1)} %get-tuple-element.8), channel_id=1, source_target_pairs={{0,16},{2,18},{4,20},{6,22},{8,24},{10,26},{12,28},{14,30},{16,0},... | collective-permute-start | bytes 589832 | tf_op jit(solution)/shard_map/ppermute | solution.py:33
  11.8 17.2 %collective-permute-start.10 = (f32[1,384,128]{2,1,0:T(8,128)S(1)}, f32[1,384,128]{2,1,0:T(8,128)S(1)}, u32[]{:S(2)}, u32[]{:S(2)}) collective-permute-start(f32[1,384,128]{2,1,0:T(8,128)S(1)} %get-tuple-element.6), channel_id=1, source_target_pairs={{0,16},{2,18},{4,20},{6,22},{8,24},{10,26},{12,28},{14,30},{16,0},... | collective-permute-start | bytes 589832 | tf_op jit(solution)/shard_map/ppermute | solution.py:33
  25.6 12.1 %collective-permute-start.6 = (f32[2,384,128]{2,1,0:T(8,128)S(1)}, f32[2,384,128]{2,1,0:T(8,128)S(1)}, u32[]{:S(2)}, u32[]{:S(2)}) collective-permute-start(f32[2,384,128]{2,1,0:T(8,128)S(1)} %maximum_select_fusion.8), channel_id=1, source_target_pairs={{0,8},{2,10},{4,12},{6,14},{8,0},{10,2},{12,4},{14,6},{16,24},{18,... | collective-permute-start | bytes 1179656 | tf_op jit(solution)/shard_map/ppermute | solution.py:33
  29.1 16.7 %collective-permute-start.11 = (f32[2,384,128]{2,1,0:T(8,128)S(1)}, f32[2,384,128]{2,1,0:T(8,128)S(1)}, u32[]{:S(2)}, u32[]{:S(2)}) collective-permute-start(f32[2,384,128]{2,1,0:T(8,128)S(1)} %maximum_select_fusion.10), channel_id=1, source_target_pairs={{0,8},{2,10},{4,12},{6,14},{8,0},{10,2},{12,4},{14,6},{16,24},{18,... | collective-permute-start | bytes 1179656 | tf_op jit(solution)/shard_map/ppermute | solution.py:33
  37.8 20.5 %collective-permute-start.7 = (f32[4,384,128]{2,1,0:T(8,128)S(1)}, f32[4,384,128]{2,1,0:T(8,128)S(1)}, u32[]{:S(2)}, u32[]{:S(2)}) collective-permute-start(f32[4,384,128]{2,1,0:T(8,128)S(1)} %bitcast.110), channel_id=1, source_target_pairs={{0,4},{2,6},{4,0},{6,2},{8,12},{10,14},{12,8},{14,10},{16,20},{18,... | collective-permute-start | bytes 2359304 | tf_op jit(solution)/shard_map/ppermute | solution.py:33
  45.9 27.9 %copy-start.3 = (f32[2,2,384,128]{3,2,1,0:T(8,128)}, f32[2,2,384,128]{3,2,1,0:T(8,128)S(1)}, u32[]{:S(2)}) copy-start(f32[2,2,384,128]{3,2,1,0:T(8,128)S(1)} %maximum_select_fusion.7) | copy-start | bytes 2359300
  45.9 27.9 %collective-permute-start.12 = (f32[4,384,128]{2,1,0:T(8,128)S(1)}, f32[4,384,128]{2,1,0:T(8,128)}, u32[]{:S(2)}, u32[]{:S(2)}) collective-permute-start(f32[4,384,128]{2,1,0:T(8,128)S(1)} %bitcast.112), channel_id=1, source_target_pairs={{0,4},{2,6},{4,0},{6,2},{8,12},{10,14},{12,8},{14,10},{16,20},{18,... | collective-permute-start | bytes 2359304 | tf_op jit(solution)/shard_map/ppermute | solution.py:33
  60.8 37.5 %collective-permute-start.8 = (f32[8,384,128]{2,1,0:T(8,128)S(1)}, f32[8,384,128]{2,1,0:T(8,128)}, u32[]{:S(2)}, u32[]{:S(2)}) collective-permute-start(f32[8,384,128]{2,1,0:T(8,128)S(1)} %bitcast.104), channel_id=1, source_target_pairs={{0,2},{2,0},{4,6},{6,4},{8,10},{10,8},{12,14},{14,12},{16,18},{18,... | collective-permute-start | bytes 4718600 | tf_op jit(solution)/shard_map/ppermute | solution.py:33
  75.8 52.3 %collective-permute-start.13 = (f32[8,384,128]{2,1,0:T(8,128)S(1)}, f32[8,384,128]{2,1,0:T(8,128)}, u32[]{:S(2)}, u32[]{:S(2)}) collective-permute-start(f32[8,384,128]{2,1,0:T(8,128)S(1)} %bitcast.106), channel_id=1, source_target_pairs={{0,2},{2,0},{4,6},{6,4},{8,10},{10,8},{12,14},{14,12},{16,18},{18,... | collective-permute-start | bytes 4718600 | tf_op jit(solution)/shard_map/ppermute | solution.py:33
  102.1 46.6 %collective-permute-start.9 = (f32[16,384,128]{2,1,0:T(8,128)}, f32[16,384,128]{2,1,0:T(8,128)}, u32[]{:S(2)}, u32[]{:S(2)}) collective-permute-start(f32[16,384,128]{2,1,0:T(8,128)} %bitcast.30), channel_id=1, source_target_pairs={{0,1},{1,0},{2,3},{3,2},{4,5},{5,4},{6,7},{7,6},{8,9},{9,8},{10,11... | collective-permute-start | bytes 9437192 | tf_op jit(solution)/shard_map/ppermute | solution.py:33
  128.2 3.8 %copy-start.7 = (s32[256]{0:T(256)S(1)}, s32[256]{0:T(256)}, u32[]{:S(2)}) copy-start(s32[256]{0:T(256)} %param.16) | copy-start | bytes 3076
  128.2 20.1 %copy-start.8 = (f32[128]{0:T(128)S(1)}, f32[128]{0:T(128)}, u32[]{:S(2)}) copy-start(f32[128]{0:T(128)} %param.19) | copy-start | bytes 1540
  132.0 26.1 %collective-permute-start.14 = (f32[16,384,128]{2,1,0:T(8,128)}, f32[16,384,128]{2,1,0:T(8,128)}, u32[]{:S(2)}, u32[]{:S(2)}) collective-permute-start(f32[16,384,128]{2,1,0:T(8,128)} %bitcast.48), channel_id=1, source_target_pairs={{0,1},{1,0},{2,3},{3,2},{4,5},{5,4},{6,7},{7,6},{8,9},{9,8},{10,11... | collective-permute-start | bytes 9437192 | tf_op jit(solution)/shard_map/ppermute | solution.py:33
  132.0 4.5 %collective-permute-start = (f32[1,128]{1,0:T(1,128)S(1)}, f32[1,128]{1,0:T(1,128)S(1)}, u32[]{:S(2)}, u32[]{:S(2)}) collective-permute-start(f32[1,128]{1,0:T(1,128)S(1)} %fusion.8), channel_id=1, source_target_pairs={{0,16},{2,18},{4,20},{6,22},{8,24},{10,26},{12,28},{14,30},{16,0},... | collective-permute-start | bytes 1544 | tf_op jit(solution)/shard_map/ppermute | solution.py:33
  136.5 3.6 %collective-permute-start.1 = (f32[2,128]{1,0:T(2,128)S(1)}, f32[2,128]{1,0:T(2,128)S(1)}, u32[]{:S(2)}, u32[]{:S(2)}) collective-permute-start(f32[2,128]{1,0:T(2,128)S(1)} %maximum_select_fusion.19), channel_id=1, source_target_pairs={{0,8},{2,10},{4,12},{6,14},{8,0},{10,2},{12,4},{14,6},{16,24},{18,... | collective-permute-start | bytes 3080 | tf_op jit(solution)/shard_map/ppermute | solution.py:33
  140.1 3.6 %collective-permute-start.2 = (f32[4,128]{1,0:T(4,128)S(1)}, f32[4,128]{1,0:T(4,128)S(1)}, u32[]{:S(2)}, u32[]{:S(2)}) collective-permute-start(f32[4,128]{1,0:T(4,128)S(1)} %bitcast.138), channel_id=1, source_target_pairs={{0,4},{2,6},{4,0},{6,2},{8,12},{10,14},{12,8},{14,10},{16,20},{18,... | collective-permute-start | bytes 6152 | tf_op jit(solution)/shard_map/ppermute | solution.py:33
  143.8 3.7 %collective-permute-start.3 = (f32[8,128]{1,0:T(8,128)S(1)}, f32[8,128]{1,0:T(8,128)S(1)}, u32[]{:S(2)}, u32[]{:S(2)}) collective-permute-start(f32[8,128]{1,0:T(8,128)S(1)} %bitcast.134), channel_id=1, source_target_pairs={{0,2},{2,0},{4,6},{6,4},{8,10},{10,8},{12,14},{14,12},{16,18},{18,... | collective-permute-start | bytes 12296 | tf_op jit(solution)/shard_map/ppermute | solution.py:33
  147.5 1.2 collective-permute-start.4
  154.6 2.6 %copy-start.2 = (f32[16,2,384,128]{3,2,1,0:T(8,128)}, f32[16,2,384,128]{3,2,1,0:T(8,128)S(1)}, u32[]{:S(2)}) copy-start(f32[16,2,384,128]{3,2,1,0:T(8,128)S(1)} %maximum_select_fusion) | copy-start | bytes 18874372
  158.0 7.9 %copy-start = (bf16[256,512]{1,0:T(8,128)(2,1)S(1)}, bf16[256,512]{1,0:T(8,128)(2,1)}, u32[]{:S(2)}) copy-start(bf16[256,512]{1,0:T(8,128)(2,1)} %constant.130.clone.block_ref) | copy-start | bytes 786436
  158.0 7.9 %copy-start.1 = (bf16[256,128]{1,0:T(8,128)(2,1)S(1)}, bf16[256,128]{1,0:T(8,128)(2,1)}, u32[]{:S(2)}) copy-start(bf16[256,128]{1,0:T(8,128)(2,1)} %constant.129.clone.lane_ref) | copy-start | bytes 196612
  222.4 2.9 %collective-permute-start.19 = (f32[16,1,128,128]{3,2,0,1:T(8,128)S(1)}, f32[16,1,128,128]{3,2,0,1:T(8,128)}, u32[]{:S(2)}, u32[]{:S(2)}) collective-permute-start(f32[16,1,128,128]{3,2,0,1:T(8,128)S(1)} %dynamic-slice_bitcast_fusion), channel_id=1, source_target_pairs={{0,1},{1,0},{2,3},{3,2},{4,5},{5,4},{6,7},{7,6},{8,9},{9,8},{10,11... | collective-permute-start | bytes 3145736 | tf_op jit(solution)/shard_map/ppermute | solution.py:33
  226.7 14.1 %collective-permute-start.20 = (f32[8,128,128]{2,1,0:T(8,128)S(1)}, f32[8,128,128]{2,1,0:T(8,128)S(1)}, u32[]{:S(2)}, u32[]{:S(2)}) collective-permute-start(f32[8,128,128]{2,1,0:T(8,128)S(1)} %dynamic-slice_bitcast_fusion.1), channel_id=1, source_target_pairs={{0,2},{2,0},{4,6},{6,4},{8,10},{10,8},{12,14},{14,12},{16,18},{18,... | collective-permute-start | bytes 1572872 | tf_op jit(solution)/shard_map/ppermute | solution.py:33
  240.8 8.1 %collective-permute-start.21 = (f32[4,128,128]{2,1,0:T(8,128)S(1)}, f32[4,128,128]{2,1,0:T(8,128)S(1)}, u32[]{:S(2)}, u32[]{:S(2)}) collective-permute-start(f32[4,128,128]{2,1,0:T(8,128)S(1)} %dynamic-slice_bitcast_fusion.2), channel_id=1, source_target_pairs={{0,4},{2,6},{4,0},{6,2},{8,12},{10,14},{12,8},{14,10},{16,20},{18,... | collective-permute-start | bytes 786440 | tf_op jit(solution)/shard_map/ppermute | solution.py:33
  242.3 4.5 %collective-permute-start.15 = (f32[1,8]{1,0:T(1,128)S(1)}, f32[1,8]{1,0:T(1,128)S(1)}, u32[]{:S(2)}, u32[]{:S(2)}) collective-permute-start(f32[1,8]{1,0:T(1,128)S(1)} %bitcast.141), channel_id=1, source_target_pairs={{0,16},{2,18},{4,20},{6,22},{8,24},{10,26},{12,28},{14,30},{16,0},... | collective-permute-start | bytes 104 | tf_op jit(solution)/shard_map/ppermute | solution.py:33
  246.8 3.6 %collective-permute-start.16 = (f32[2,8]{1,0:T(2,128)S(1)}, f32[2,8]{1,0:T(2,128)S(1)}, u32[]{:S(2)}, u32[]{:S(2)}) collective-permute-start(f32[2,8]{1,0:T(2,128)S(1)} %maximum_select_fusion.20), channel_id=1, source_target_pairs={{0,8},{2,10},{4,12},{6,14},{8,0},{10,2},{12,4},{14,6},{16,24},{18,... | collective-permute-start | bytes 200 | tf_op jit(solution)/shard_map/ppermute | solution.py:33
  249.0 6.7 %collective-permute-start.22 = (f32[2,128,128]{2,1,0:T(8,128)S(1)}, f32[2,128,128]{2,1,0:T(8,128)S(1)}, u32[]{:S(2)}, u32[]{:S(2)}) collective-permute-start(f32[2,128,128]{2,1,0:T(8,128)S(1)} %dynamic-slice_bitcast_fusion.3), channel_id=1, source_target_pairs={{0,8},{2,10},{4,12},{6,14},{8,0},{10,2},{12,4},{14,6},{16,24},{18,... | collective-permute-start | bytes 393224 | tf_op jit(solution)/shard_map/ppermute | solution.py:33
  250.5 3.6 %collective-permute-start.17 = (f32[4,8]{1,0:T(4,128)S(1)}, f32[4,8]{1,0:T(4,128)S(1)}, u32[]{:S(2)}, u32[]{:S(2)}) collective-permute-start(f32[4,8]{1,0:T(4,128)S(1)} %bitcast.136), channel_id=1, source_target_pairs={{0,4},{2,6},{4,0},{6,2},{8,12},{10,14},{12,8},{14,10},{16,20},{18,... | collective-permute-start | bytes 392 | tf_op jit(solution)/shard_map/ppermute | solution.py:33
  254.1 4.6 %collective-permute-start.18 = (f32[8,8]{1,0:T(8,128)S(1)}, f32[8,8]{1,0:T(8,128)S(1)}, u32[]{:S(2)}, u32[]{:S(2)}) collective-permute-start(f32[8,8]{1,0:T(8,128)S(1)} %bitcast.132), channel_id=1, source_target_pairs={{0,2},{2,0},{4,6},{6,4},{8,10},{10,8},{12,14},{14,12},{16,18},{18,... | collective-permute-start | bytes 776 | tf_op jit(solution)/shard_map/ppermute | solution.py:33
  255.7 5.2 %collective-permute-start.23 = (f32[1,128,128]{2,1,0:T(8,128)S(1)}, f32[1,128,128]{2,1,0:T(8,128)S(1)}, u32[]{:S(2)}, u32[]{:S(2)}) collective-permute-start(f32[1,128,128]{2,1,0:T(8,128)S(1)} %constant_dynamic-slice_fusion), channel_id=1, source_target_pairs={{0,16},{2,18},{4,20},{6,22},{8,24},{10,26},{12,28},{14,30},{16,0},... | collective-permute-start | bytes 196616 | tf_op jit(solution)/shard_map/ppermute | solution.py:33
  (1 other events, 0.9 us)

commit v2 on v1

v2 whole, which is shorter than its diff:
```python
import functools
import math

import jax
import jax.numpy as jnp
import numpy as np
from jax import lax
from jax.experimental import pallas as pl
from jax.experimental.pallas import tpu as pltpu
from jax.sharding import PartitionSpec as P

LANES = 128
CHUNK = 256
BOTH = ("feat", "rows")
MIB = 1024 * 1024


def hadamard(length):
    matrix = np.ones((1, 1), np.float32)
    while matrix.shape[0] < length:
        matrix = np.block([[matrix, matrix], [matrix, -matrix]])
    return matrix


def halves(values):
    high = values.astype(jnp.bfloat16)
    low = (values - high.astype(jnp.float32)).astype(jnp.bfloat16)
    return high, low


def swap(values, axis_name, bit):
    size = lax.axis_size(axis_name)
    return lax.ppermute(values, axis_name, [(i, i ^ bit) for i in range(size)])


def bits_of(axis_name):
    return [1 << i for i in reversed(range(lax.axis_size(axis_name).bit_length() - 1))]


def gather_ordered(piece):
    shape = piece.shape
    held = piece[None]
    for axis_name in BOTH:
        index = lax.axis_index(axis_name)
        for bit in bits_of(axis_name):
            other = swap(held, axis_name, bit)
            upper = (index & bit) != 0
            held = jnp.where(
                upper, jnp.stack([other, held], 1), jnp.stack([held, other], 1)
            ).reshape((-1,) + shape)
    return held


def gather_relative(piece, bits):
    held = piece[None]
    for bit in bits:
        held = jnp.concatenate([held, swap(held, "feat", bit)], axis=0)
    return held


def place_of(distance, bits):
    place = 0
    for i, bit in enumerate(bits):
        place = place + (((distance >> (bit.bit_length() - 1)) & 1) << i)
    return place


def take_part(values, axis, index):
    return lax.dynamic_index_in_dim(values, index, axis, False)


def scatter_sum(terms, extra):
    place = lax.axis_index("feat")
    core = lax.axis_index("rows")
    for bit in bits_of("rows"):
        pair = terms.reshape((terms.shape[0], 2, bit) + terms.shape[2:])
        mine = (core & bit) // bit
        terms = take_part(pair, 1, mine) + swap(take_part(pair, 1, 1 - mine), "rows", bit)
    lanes = terms.shape[-1]
    bits = bits_of("feat")
    count = terms.shape[2]
    terms = terms.reshape((2,) * len(bits) + (count, lanes))
    cut = count // 2
    parts = [terms[..., :cut, :], terms[..., cut:, :]]
    names = [list(bits), list(bits)]
    orders = [[1, 2], [2, 1]]

    def exchange(part, left, bit, extra):
        axis = left.index(bit)
        left.remove(bit)
        mine = (place & bit) // bit
        keep = take_part(part, axis, mine)
        send = take_part(part, axis, 1 - mine).reshape(-1, lanes)
        if extra is None:
            return keep + swap(send, "feat", bit).reshape(keep.shape), None
        got = swap(jnp.concatenate([send, extra], axis=0), "feat", bit)
        return keep + got[: send.shape[0]].reshape(keep.shape), extra + got[send.shape[0] :]

    for turn in range(2):
        parts[0], extra = exchange(parts[0], names[0], orders[0][turn], extra)
        parts[1], _ = exchange(parts[1], names[1], orders[1][turn], None)
    rest = jnp.concatenate(parts, axis=-2)
    for bit in list(reversed(names[0])):
        rest, extra = exchange(rest, names[0], bit, extra)
    return rest, extra


def mix_kernel(rows, bits_a, bits_b, me_ref, a_own, a_other, b_own, b_other, emb_ref, lane_ref, block_ref, out_ref, sign_ref, wide_ref, spread_ref):
    f32 = jnp.float32
    bf16 = jnp.bfloat16
    chunks = a_own.shape[0]
    width = emb_ref.shape[0]
    quarters = width // LANES
    here = LANES // quarters
    chunk = pl.program_id(0)

    def flip(bits):
        return (1 - 2 * (bits & 1)).astype(f32)

    @pl.when(chunk == 0)
    def _():
        for c, ref in enumerate((a_own, a_other)):
            for p in range(chunks):
                top = (c * chunks + p) * here
                for q in range(quarters):
                    sign_ref[top : top + here, q * LANES : (q + 1) * LANES] = ref[
                        p, q * here : (q + 1) * here, :
                    ].astype(bf16)
        sums = jnp.dot(jnp.ones((16, sign_ref.shape[0]), bf16), sign_ref[...], preferred_element_type=f32)
        odd = 0.5 * sums - 2.0 * jnp.floor(0.25 * sums)
        row = lax.broadcasted_iota(jnp.int32, odd.shape, 0)
        column = lax.broadcasted_iota(jnp.int32, odd.shape, 1)
        odd = jnp.where((row < 2 * quarters) & ((row & (quarters - 1)) == column // LANES), 0.5 * odd, 0.0)
        rest = jnp.dot(odd.astype(bf16), emb_ref[...], preferred_element_type=f32)
        high = rest.astype(bf16).astype(f32)
        row = lax.broadcasted_iota(jnp.int32, rest.shape, 0)
        wide_ref[0:width, :] = emb_ref[...]
        wide_ref[width:, :] = jnp.zeros((LANES, wide_ref.shape[1]), bf16)
        wide_ref[width : width + 16, :] = jnp.where(row < quarters, high, rest - high).astype(bf16)

    pa = place_of(chunk, bits_a)
    pb = place_of(chunk, bits_b)
    major_me = me_ref[0] * here
    columns = []
    for ref in (a_own, a_other):
        source = ref[pa, 3 * LANES // 2 : 3 * LANES // 2 + 1, :].astype(jnp.int32)
        major = source >> 2
        low = here.bit_length() - 1
        code = major & (here - 1)
        for i, bit in enumerate(bits_a):
            code = code | (((major >> (low + bit.bit_length())) & 1) << (low + i))
        code = code | (((major >> low) & 1) << (low + len(bits_a)))
        code = code | ((source & 3) << 10) | ((lax.population_count(major & major_me) & 1) << 12)
        columns.append(jnp.broadcast_to(code.astype(f32), (LANES, LANES)).T)
    code = jnp.concatenate(columns, axis=0).astype(jnp.int32)
    lane = lax.broadcasted_iota(jnp.int32, (CHUNK, LANES), 1)
    tiles = [flip(lax.population_count(code & lane))]
    for shift in range(7, 10):
        turn = flip(code >> shift)
        tiles = tiles + [tile * turn for tile in tiles]
    signs = jnp.concatenate([tile.astype(bf16) for tile in tiles], axis=1)
    sums = jnp.dot(signs, sign_ref[...], preferred_element_type=f32)
    flip_me, flip_1, flip_2 = flip(code >> 12), flip(code >> 10), flip(code >> 11)
    turns = [flip_me, flip_me * flip_1, flip_me * flip_2, flip_me * flip_1 * flip_2]
    left = [
        (jnp.floor(0.25 * sums[:, q * LANES : (q + 1) * LANES]) * turns[q]).astype(bf16) for q in range(4)
    ]
    tail = flip_me * jnp.where((lane & 1) != 0, flip_1, 1.0) * jnp.where((lane & 2) != 0, flip_2, 1.0)
    left.append(jnp.where(lane < 8, tail, 0.0).astype(bf16))
    first = jnp.dot(jnp.concatenate(left, axis=1), wide_ref[...], preferred_element_type=f32)

    half = LANES // 2
    order = jnp.concatenate(
        [
            ref[p, LANES : LANES + half, :]
            for ref, p in ((a_own, pa), (b_own, pb), (a_other, pa), (b_other, pb))
        ],
        axis=0,
    ).astype(jnp.int32)
    gain = jnp.concatenate([b_own[pb, 0:LANES, :], b_other[pb, 0:LANES, :]], axis=0)
    for r in range(rows):
        columns = slice(r * LANES, (r + 1) * LANES)
        mixed = jnp.take_along_axis(first[:, columns], order, axis=1) * gain
        across = jnp.dot(
            jnp.concatenate(halves(mixed), axis=1), lane_ref[...], preferred_element_type=f32
        )
        high, low = halves(across)
        spread_ref[0:CHUNK, columns] = high
        spread_ref[CHUNK:, columns] = low
    result = jnp.dot(block_ref[...], spread_ref[...], preferred_element_type=f32)
    for r in range(rows):
        out_ref[0, r] = result[:, r * LANES : (r + 1) * LANES]


def turn_cosine_coefficients(degree):
    points = np.cos(np.pi * (np.arange(400) + 0.5) / 400)
    u = 0.5 * points
    fit = np.polynomial.chebyshev.Chebyshev.fit(u * u, np.cos(2 * np.pi * u), degree, domain=[0, 0.25])
    return [float(c) for c in fit.convert(kind=np.polynomial.Polynomial).coef]


def head_kernel(rows, chunks, tile, coefs, grad_scale, me_ref, target_ref, y_ref, scale_ref, phase_ref, weight_ref, pred_ref, grad_ref, feat_ref, acc_ref, turn_ref):
    f32 = jnp.float32
    step = pl.program_id(0)
    steps = pl.num_programs(0)

    @pl.when(step == 0)
    def _():
        acc_ref[...] = jnp.zeros_like(acc_ref)

    second_half = (step * tile) // LANES
    for k in range(chunks):
        shared = (2 * k + second_half) & me_ref[0]
        shared = shared ^ (shared >> 4)
        shared = shared ^ (shared >> 2)
        shared = shared ^ (shared >> 1)
        turn_ref[k] = scale_ref[k, 0] * (1 - 2 * (shared & 1)).astype(f32)

    for part in range(tile // 8):
        here = slice(part * 8, part * 8 + 8)
        for r in range(rows):
            values = [y_ref[k, r, here, :] for k in range(chunks)]
            width = 1
            while width < chunks:
                for k in range(chunks):
                    if not k & width:
                        a, b = values[k], values[k | width]
                        values[k], values[k | width] = a + b, a - b
                width *= 2
            acc = acc_ref[r]
            for k in range(chunks):
                turns = values[k] * turn_ref[k, here, :] + phase_ref[k, 0, here, :]
                u = turns - jnp.round(turns)
                square = u * u
                cosine = jnp.full_like(square, coefs[-1])
                for c in coefs[-2::-1]:
                    cosine = cosine * square + c
                feat_ref[k, r, pl.ds(pl.multiple_of(step * tile + part * 8, 8), 8), :] = cosine
                acc = acc + cosine * weight_ref[k, 0, here, :]
            acc_ref[r] = acc

    @pl.when(step == steps - 1)
    def _():
        residuals = []
        lane = lax.broadcasted_iota(jnp.int32, (1, LANES), 1)
        found = jnp.zeros((1, LANES), f32)
        for r in range(rows):
            total = jnp.sum(jnp.sum(acc_ref[r], axis=0, keepdims=True), axis=1, keepdims=True)
            found = found + jnp.where(lane == me_ref[1] + r, total, 0.0)
            residuals.append(jnp.broadcast_to((total - target_ref[r]) * grad_scale, (8, LANES)))
        pred_ref[...] = jnp.broadcast_to(found, (8, LANES))

        for k in range(chunks):

            @pl.loop(0, CHUNK // 32)
            def _(i):
                for j in range(4):
                    rows_here = pl.ds(pl.multiple_of(i * 32 + j * 8, 8), 8)
                    total = feat_ref[k, 0, rows_here, :] * residuals[0]
                    for r in range(1, rows):
                        total = total + feat_ref[k, r, rows_here, :] * residuals[r]
                    grad_ref[k, rows_here, :] = total


def local(
    embeddings,
    sign_flips,
    gaussian,
    scales,
    phases,
    source_blocks,
    block_permutations,
    weights,
    targets,
):
    f32 = jnp.float32
    feat_size = lax.axis_size("feat")
    rows_size = lax.axis_size("rows")
    place = lax.axis_index("feat")
    core = lax.axis_index("rows")
    devices = feat_size * rows_size
    width = embeddings.shape[1]
    rows = embeddings.shape[0] // feat_size
    total_rows = embeddings.shape[0] * rows_size
    features = sign_flips.shape[0] * feat_size
    blocks = features // LANES
    mine = blocks // devices
    quarters = width // LANES
    chunks = blocks // CHUNK
    per_chunk = CHUNK // mine

    def half(values):
        parts = values.reshape((rows_size, values.shape[0] // rows_size) + values.shape[1:])
        return lax.dynamic_index_in_dim(parts, core, 0, False)

    def rows_of(*vectors):
        return jnp.concatenate([half(v) for v in vectors]).reshape(len(vectors), mine, LANES)

    positions = jnp.einsum(
        "bij,j->bi", half(block_permutations), jnp.arange(LANES).astype(jnp.bfloat16), preferred_element_type=f32
    )
    signs, gains = rows_of(sign_flips, gaussian)
    numbers = half(source_blocks).astype(f32)
    late = rows_of(
        scales * f32(4.0 / (2.0 * math.pi * features)),
        phases * f32(1.0 / (2.0 * math.pi)),
        weights * f32(1.0 / math.sqrt(features)),
    )
    late = lax.all_gather(late.reshape(3 * mine, LANES), BOTH)
    bits = bits_of("feat")
    if mine == LANES and feat_size == chunks and rows_size == 2:
        me = place * rows_size + core
        bits_a = bits[:-2] + [2, 1]
        bits_b = bits[:-2] + [1, 2]
    else:
        me = 0
        bits_a = bits_b = [1 << i for i in range(chunks.bit_length() - 1)]
        whole = gather_ordered(
            jnp.concatenate([signs, positions, gains, jnp.pad(numbers.reshape(1, mine), ((0, 7), (0, LANES - mine)))])
        )
        signs, positions, gains = (
            whole[:, i * mine : (i + 1) * mine].reshape(chunks, 2, LANES, LANES) for i in range(3)
        )
        numbers = whole[:, 3 * mine, :mine].reshape(chunks, 2, LANES)

    per_half = LANES // quarters
    shape = signs.shape
    signs = jnp.swapaxes(signs.reshape(shape[:-2] + (per_half, quarters, LANES)), -3, -2).reshape(shape)
    numbers = jnp.broadcast_to(numbers[..., None, :], shape[:-2] + (8, LANES))
    cut = LANES // 2
    part_a = jnp.concatenate([signs, positions[..., :cut, :], numbers], axis=-2)
    part_b = jnp.concatenate([gains, positions[..., cut:, :]], axis=-2)
    if part_a.ndim == 2:
        part_a = gather_relative(part_a, bits_a)
        part_b = gather_relative(part_b, bits_b)
        a_pair = (part_a, swap(part_a, "rows", 1))
        b_pair = (part_b, swap(part_b, "rows", 1))
    else:
        a_pair = (part_a[:, 0], part_a[:, 1])
        b_pair = (part_b[:, 0], part_b[:, 1])

    emb = lax.dynamic_slice_in_dim(embeddings, place * rows, rows, 0)
    lane_signs = hadamard(LANES)
    emb = (emb.T.reshape(quarters, LANES, rows, 1) * jnp.asarray(lane_signs, jnp.bfloat16)[None, :, None, :]).reshape(
        width, rows * LANES
    )
    lane_matrix = jnp.asarray(np.concatenate([lane_signs] * 2, 0), jnp.bfloat16)
    block_matrix = jnp.asarray(np.concatenate([hadamard(CHUNK)] * 2, 1), jnp.bfloat16)
    about_me = jnp.stack([jnp.asarray(me, jnp.int32), (place * rows).astype(jnp.int32)])

    def resident(array):
        return pl.BlockSpec(array.shape, lambda k: (0,) * array.ndim)

    scalars = pl.BlockSpec(memory_space=pltpu.SMEM)
    resident_args = (*a_pair, *b_pair, emb, lane_matrix, block_matrix)
    spread = pl.pallas_call(
        functools.partial(mix_kernel, rows, bits_a, bits_b),
        grid=(chunks,),
        in_specs=[scalars] + [resident(x) for x in resident_args],
        out_specs=pl.BlockSpec((1, rows, CHUNK, LANES), lambda k: (k, 0, 0, 0)),
        out_shape=jax.ShapeDtypeStruct((chunks, rows, CHUNK, LANES), f32),
        scratch_shapes=[
            pltpu.VMEM((blocks // quarters, width), jnp.bfloat16),
            pltpu.VMEM((width + LANES, rows * LANES), jnp.bfloat16),
            pltpu.VMEM((2 * CHUNK, rows * LANES), jnp.bfloat16),
        ],
        compiler_params=pltpu.CompilerParams(vmem_limit_bytes=48 * MIB),
        name="mix",
    )(about_me, *resident_args)

    tile = min(32, mine)
    tiles_here = mine // tile
    late = late.reshape(chunks, per_chunk, 3 * mine, LANES)

    def late_part(which):
        return pl.BlockSpec(
            (chunks, 1, tile, LANES), lambda i: (0, i // tiles_here, which * tiles_here + i % tiles_here, 0)
        )

    my_targets = lax.dynamic_slice_in_dim(targets, place * rows, rows, 0)
    found, grads = pl.pallas_call(
        functools.partial(
            head_kernel, rows, chunks, tile, turn_cosine_coefficients(5), 1.0 / math.sqrt(total_rows)
        ),
        grid=(CHUNK // tile,),
        in_specs=[
            scalars,
            scalars,
            pl.BlockSpec((chunks, rows, tile, LANES), lambda i: (0, 0, i, 0)),
            late_part(0),
            late_part(1),
            late_part(2),
        ],
        out_specs=[
            pl.BlockSpec((8, LANES), lambda i: (0, 0)),
            pl.BlockSpec((chunks, CHUNK, LANES), lambda i: (0, 0, 0)),
        ],
        out_shape=[
            jax.ShapeDtypeStruct((8, LANES), f32),
            jax.ShapeDtypeStruct((chunks, CHUNK, LANES), f32),
        ],
        scratch_shapes=[
            pltpu.VMEM((chunks, rows, CHUNK, LANES), f32),
            pltpu.VMEM((rows, 8, LANES), f32),
            pltpu.VMEM((chunks, tile, LANES), f32),
        ],
        compiler_params=pltpu.CompilerParams(vmem_limit_bytes=48 * MIB),
        name="head",
    )(about_me, my_targets, spread, late, late, late)

    feature_grad, found = scatter_sum(grads.reshape(feat_size, rows_size, mine, LANES), found)
    return found[0], feature_grad.reshape(-1)


def solution(mesh):
    in_specs = (
        P("rows", None),
        P("feat"),
        P("feat"),
        P("feat"),
        P("feat"),
        P("feat"),
        P("feat", None, None),
        P("feat"),
        P("rows"),
    )
    out_specs = (P("rows"), P(("feat", "rows")))
    return jax.shard_map(local, mesh=mesh, in_specs=in_specs, out_specs=out_specs, check_vma=False)
```

time: 262 us -> 183 us (0.70)
  waiting for transfers between devices: 130 us -> 74.9 us
  other arithmetic: 28.4 us -> 7.35 us
  between operations: 0.99 us -> 14.5 us
  starting transfers between devices: 34 us -> 25.8 us
  Pallas kernels: 56.4 us -> 50.4 us
    ppermute x24 -> x17, waiting for transfers between devices: 130 us -> 74.9 us  [swap(): return lax.ppermute(values, axis_name, [(i, i ^ bit) for i in range(size)])]
    select_n x23 -> x0, other arithmetic: 25.2 us -> none  [gather_all(): jnp.where(upper, jnp.stack([other, held], 1), jnp.stack([held, other], 1))]
    ppermute x24 -> x17, starting transfers between devices: 34 us -> 25.8 us  [swap(): return lax.ppermute(values, axis_name, [(i, i ^ bit) for i in range(size)])]
    pallas_call x1, Pallas kernels: 24.2 us -> 16.7 us  [local(): pl.pallas_call(functools.partial(head_kernel, rows, chunks, tile, turn_co...]
    mul x2 -> x4, other arithmetic: 0.34 us -> 3.5 us  [the longest x1 0.95 us: local(): scales * f32(4.0 / (2.0 * math.pi * features))]
  transfers between devices with their start and end apart: 24 -> 18, of which waited for: 19 -> 15; matrix products, arithmetic and copies ran while one was open for 8% -> 5% of each run, Pallas kernels for 0% -> 18%
where the time goes in v2:
time: 183 us
  waiting for transfers between devices  74.9 us (41%)
  Pallas kernels  50.4 us (28%)
  starting transfers between devices  25.8 us (14%)
  between operations  14.5 us (8%)
  other arithmetic  7.35 us (4%)
  local copies, waits for them, and re-layouts  6.23 us (3%)
  matrix products  3.37 us (2%)
    ppermute x17, waiting for transfers between devices, swap(): return lax.ppermute(values, axis_name, [(i, i ^ bit) for i in range(size)])  74.9 us
    pallas_call x1, Pallas kernels, local(): pl.pallas_call(functools.partial(mix_kernel, rows, bits_a, bits_b), grid=...  33.7 us
    ppermute x17, starting transfers between devices, swap(): return lax.ppermute(values, axis_name, [(i, i ^ bit) for i in range(size)])  25.8 us
    pallas_call x1, Pallas kernels, local(): pl.pallas_call(functools.partial(head_kernel, rows, chunks, tile, turn_co...  16.7 us
  transfers between devices with their start and end apart: 18, of which 15 were waited for; matrix products, arithmetic and copies ran while one was open for 5% of the time, Pallas kernels for 18%

profile of v2, /device:TPU:0, one launch (start us, length us, event | category | flops | bytes accessed | tf_op | source)
XLA Modules:
  0.0 182.6 jit_solution(7833973189993437170)
XLA Ops:
  7.2 1.0 broadcast_multiply_fusion.3
  8.3 1.0 reshape.98
  12.5 3.4 %fusion = f32[1,128,128]{2,0,1:T(1,128)S(1)} fusion(bf16[2,128,128,128]{3,2,1,0:T(8,128)(2,1)} %bitcast.86, s32[]{:T(128)S(6)} %select_n.72), kind=kOutput, calls=%fused_computation | convolution fusion | flops 4194432 | bytes 4259844 | tf_op jit(solution)/shard_map/bij,j->bi/dot_general | solution.py:299
  15.9 4.1 %collective-permute-start = (f32[1,200,128]{2,1,0:T(8,128)S(1)}, f32[1,200,128]{2,1,0:T(8,128)S(1)}, u32[]{:S(2)}, u32[]{:S(2)}) collective-permute-start(f32[1,200,128]{2,1,0:T(8,128)S(1)} %maximum_bitcast_fusion.1), channel_id=1, source_target_pairs={{0,16},{2,18},{4,20},{6,22},{8,24},{10,26},{12,28},{14,30},{16,0},... | collective-permute-start | bytes 307208 | tf_op jit(solution)/shard_map/ppermute | solution.py:33
  20.1 8.8 %collective-permute-done = f32[1,200,128]{2,1,0:T(8,128)S(1)} collective-permute-done((f32[1,200,128]{2,1,0:T(8,128)S(1)}, f32[1,200,128]{2,1,0:T(8,128)S(1)}, u32[]{:S(2)}, u32[]{:S(2)}) %collective-permute-start) | collective-permute-done | bytes 102432 | tf_op jit(solution)/shard_map/ppermute | solution.py:33
  29.5 1.4 collective-permute-done.5
  30.9 2.0 %collective-permute-start.6 = (f32[2,192,128]{2,1,0:T(8,128)S(1)}, f32[2,192,128]{2,1,0:T(8,128)S(1)}, u32[]{:S(2)}, u32[]{:S(2)}) collective-permute-start(f32[2,192,128]{2,1,0:T(8,128)S(1)} %pad_maximum_fusion.6), channel_id=1, source_target_pairs={{0,8},{2,10},{4,12},{6,14},{8,0},{10,2},{12,4},{14,6},{16,24},{18,... | collective-permute-start | bytes 589832 | tf_op jit(solution)/shard_map/ppermute | solution.py:33
  32.9 5.3 %collective-permute-done.1 = f32[2,200,128]{2,1,0:T(8,128)S(1)} collective-permute-done((f32[2,200,128]{2,1,0:T(8,128)S(1)}, f32[2,200,128]{2,1,0:T(8,128)S(1)}, u32[]{:S(2)}, u32[]{:S(2)}) %collective-permute-start.1) | collective-permute-done | bytes 204832 | tf_op jit(solution)/shard_map/ppermute | solution.py:33
  38.3 2.4 %collective-permute-start.2 = (f32[4,200,128]{2,1,0:T(8,128)S(1)}, f32[4,200,128]{2,1,0:T(8,128)S(1)}, u32[]{:S(2)}, u32[]{:S(2)}) collective-permute-start(f32[4,200,128]{2,1,0:T(8,128)S(1)} %pad_maximum_fusion.2), channel_id=1, source_target_pairs={{0,4},{2,6},{4,0},{6,2},{8,12},{10,14},{12,8},{14,10},{16,20},{18,... | collective-permute-start | bytes 1228808 | tf_op jit(solution)/shard_map/ppermute | solution.py:33
  40.7 1.5 collective-permute-done.6
  42.2 1.6 collective-permute-start.7
  44.4 7.2 %collective-permute-done.2 = f32[4,200,128]{2,1,0:T(8,128)S(1)} collective-permute-done((f32[4,200,128]{2,1,0:T(8,128)S(1)}, f32[4,200,128]{2,1,0:T(8,128)S(1)}, u32[]{:S(2)}, u32[]{:S(2)}) %collective-permute-start.2) | collective-permute-done | bytes 409632 | tf_op jit(solution)/shard_map/ppermute | solution.py:33
  51.7 1.3 collective-permute-start.3
  53.0 6.1 %collective-permute-done.7 = f32[4,192,128]{2,1,0:T(8,128)S(1)} collective-permute-done((f32[4,192,128]{2,1,0:T(8,128)S(1)}, f32[4,192,128]{2,1,0:T(8,128)S(1)}, u32[]{:S(2)}, u32[]{:S(2)}) %collective-permute-start.7) | collective-permute-done | bytes 393248 | tf_op jit(solution)/shard_map/ppermute | solution.py:33
  59.2 1.6 collective-permute-start.8
  63.0 20.6 %collective-permute-done.3 = f32[8,200,128]{2,1,0:T(8,128)S(1)} collective-permute-done((f32[8,200,128]{2,1,0:T(8,128)S(1)}, f32[8,200,128]{2,1,0:T(8,128)S(1)}, u32[]{:S(2)}, u32[]{:S(2)}) %collective-permute-start.3) | collective-permute-done | bytes 819232 | tf_op jit(solution)/shard_map/ppermute | solution.py:33
  83.7 4.5 %collective-permute-done.8 = f32[8,192,128]{2,1,0:T(8,128)S(1)} collective-permute-done((f32[8,192,128]{2,1,0:T(8,128)S(1)}, f32[8,192,128]{2,1,0:T(8,128)S(1)}, u32[]{:S(2)}, u32[]{:S(2)}) %collective-permute-start.8) | collective-permute-done | bytes 786464 | tf_op jit(solution)/shard_map/ppermute | solution.py:33
  90.5 2.7 %collective-permute-done.9.b_other = f32[16,192,128]{2,1,0:T(8,128)} collective-permute-done((f32[16,192,128]{2,1,0:T(8,128)}, f32[16,192,128]{2,1,0:T(8,128)}, u32[]{:S(2)}, u32[]{:S(2)}) %collective-permute-start.9) | collective-permute-done | bytes 1572896 | tf_op jit(solution)/shard_map/ppermute | solution.py:33
  93.2 33.7 %mix.1.y_ref = f32[16,8,256,128]{3,2,1,0:T(8,128)} custom-call(s32[2]{0:T(128)S(1)} %pad_add_fusion.me_ref, f32[16,200,128]{2,1,0:T(8,128)S(1)} %constant_dynamic-update-slice_fusion.a_own, f32[16,200,128]{2,1,0:T(8,128)} %collective-permute-done.4.a_other, f32[16,192,128]{2,1,0:T(8,128)} %constant_dynamic-update-slice_fusion.5.b_own, ...), custom_call_target="tpu_custom_call" | custom-call | tf_op jit(solution)/shard_map/mix/pallas_call | solution.py:356
  126.9 16.7 %head.1 = (f32[8,128]{1,0:T(8,128)S(1)}, f32[16,256,128]{2,1,0:T(8,128)S(1)}) custom-call(s32[2]{0:T(128)S(1)} %pad_add_fusion.me_ref, f32[8]{0:T(128)S(1)} %dynamic_slice.78.target_ref, f32[16,8,256,128]{3,2,1,0:T(8,128)} %mix.1.y_ref, f32[16,2,384,128]{3,2,1,0:T(8,128)} %bitcast.81, f32[16,2,384,128]{3,2,1,0:T(8,128)} %bitcast.82, f32[16,2,384,128]{3,2,1,0:T(8,128)} %bitcast.83), custom_call_target="tpu_custom_call" | custom-call | tf_op jit(solution)/shard_map/head/pallas_call | solution.py:381
  143.9 2.7 %collective-permute-done.10 = f32[16,1,128,128]{3,2,0,1:T(8,128)} collective-permute-done((f32[16,1,128,128]{3,2,0,1:T(8,128)S(1)}, f32[16,1,128,128]{3,2,0,1:T(8,128)}, u32[]{:S(2)}, u32[]{:S(2)}) %collective-permute-start.10) | collective-permute-done | bytes 1048608 | tf_op jit(solution)/shard_map/ppermute | solution.py:33
  146.6 1.4 bitcast_add_fusion
  148.9 2.0 %collective-permute-start.11 = (f32[520,128]{1,0:T(8,128)S(1)}, f32[520,128]{1,0:T(8,128)S(1)}, u32[]{:S(2)}, u32[]{:S(2)}) collective-permute-start(f32[520,128]{1,0:T(8,128)S(1)} %pad_maximum_fusion.4), channel_id=1, source_target_pairs={{0,2},{2,0},{4,6},{6,4},{8,10},{10,8},{12,14},{14,12},{16,18},{18,... | collective-permute-start | bytes 798728 | tf_op jit(solution)/shard_map/ppermute | solution.py:33
  150.9 5.6 %collective-permute-done.13 = f32[512,128]{1,0:T(8,128)S(1)} collective-permute-done((f32[512,128]{1,0:T(8,128)S(1)}, f32[512,128]{1,0:T(8,128)S(1)}, u32[]{:S(2)}, u32[]{:S(2)}) %collective-permute-start.13) | collective-permute-done | bytes 262176 | tf_op jit(solution)/shard_map/ppermute | solution.py:33
  156.6 1.2 collective-permute-start.14
  157.8 1.8 collective-permute-start.12
  159.6 1.9 %collective-permute-done.14 = f32[256,128]{1,0:T(8,128)S(1)} collective-permute-done((f32[256,128]{1,0:T(8,128)S(1)}, f32[256,128]{1,0:T(8,128)S(1)}, u32[]{:S(2)}, u32[]{:S(2)}) %collective-permute-start.14) | collective-permute-done | bytes 131104 | tf_op jit(solution)/shard_map/ppermute | solution.py:33
  161.6 1.3 collective-permute-done.12
  163.0 2.0 %collective-permute-start.15 = (f32[264,128]{1,0:T(8,128)S(1)}, f32[264,128]{1,0:T(8,128)S(1)}, u32[]{:S(2)}, u32[]{:S(2)}) collective-permute-start(f32[264,128]{1,0:T(8,128)S(1)} %pad_maximum_fusion.8), channel_id=1, source_target_pairs={{0,8},{2,10},{4,12},{6,14},{8,0},{10,2},{12,4},{14,6},{16,24},{18,... | collective-permute-start | bytes 405512 | tf_op jit(solution)/shard_map/ppermute | solution.py:33
  165.0 3.1 %collective-permute-done.15 = f32[264,128]{1,0:T(8,128)S(1)} collective-permute-done((f32[264,128]{1,0:T(8,128)S(1)}, f32[264,128]{1,0:T(8,128)S(1)}, u32[]{:S(2)}, u32[]{:S(2)}) %collective-permute-start.15) | collective-permute-done | bytes 135200 | tf_op jit(solution)/shard_map/ppermute | solution.py:33
  168.2 4.1 %collective-permute-start.16 = (f32[136,128]{1,0:T(8,128)S(1)}, f32[136,128]{1,0:T(8,128)S(1)}, u32[]{:S(2)}, u32[]{:S(2)}) collective-permute-start(f32[136,128]{1,0:T(8,128)S(1)} %pad_maximum_fusion.9), channel_id=1, source_target_pairs={{0,16},{2,18},{4,20},{6,22},{8,24},{10,26},{12,28},{14,30},{16,0},... | collective-permute-start | bytes 208904 | tf_op jit(solution)/shard_map/ppermute | solution.py:33
  172.3 2.3 %collective-permute-done.16 = f32[136,128]{1,0:T(8,128)S(1)} collective-permute-done((f32[136,128]{1,0:T(8,128)S(1)}, f32[136,128]{1,0:T(8,128)S(1)}, u32[]{:S(2)}, u32[]{:S(2)}) %collective-permute-start.16) | collective-permute-done | bytes 69664 | tf_op jit(solution)/shard_map/ppermute | solution.py:33
  (89 shorter events, 12.0 us)
Async XLA Ops:
  7.2 81.9 %copy-start = (bf16[128,512]{1,0:T(8,128)(2,1)S(1)}, bf16[128,512]{1,0:T(8,128)(2,1)}, u32[]{:S(2)}) copy-start(bf16[128,512]{1,0:T(8,128)(2,1)} %param.12) | copy-start | bytes 393220
  7.2 5.1 %copy-start.3 = (f32[32768]{0:T(1024)S(1)}, f32[32768]{0:T(1024)}, u32[]{:S(2)}) copy-start(f32[32768]{0:T(1024)} %param.13) | copy-start | bytes 393220
  7.2 119.7 %all-gather.2.cloned.1.call-start = ((), (), s32[]{:S(2)}) async-start(), calls=%async_computation | async-start | bytes 6488064 | tf_op jit(solution)/shard_map/all_gather | solution.py:309
  8.2 4.3 %copy-start.5 = (s32[256]{0:T(256)S(1)}, s32[256]{0:T(256)}, u32[]{:S(2)}) copy-start(s32[256]{0:T(256)} %param.17) | copy-start | bytes 3076
  15.9 13.0 %collective-permute-start = (f32[1,200,128]{2,1,0:T(8,128)S(1)}, f32[1,200,128]{2,1,0:T(8,128)S(1)}, u32[]{:S(2)}, u32[]{:S(2)}) collective-permute-start(f32[1,200,128]{2,1,0:T(8,128)S(1)} %maximum_bitcast_fusion.1), channel_id=1, source_target_pairs={{0,16},{2,18},{4,20},{6,22},{8,24},{10,26},{12,28},{14,30},{16,0},... | collective-permute-start | bytes 307208 | tf_op jit(solution)/shard_map/ppermute | solution.py:33
  20.0 10.9 %collective-permute-start.5 = (f32[1,192,128]{2,1,0:T(8,128)S(1)}, f32[1,192,128]{2,1,0:T(8,128)S(1)}, u32[]{:S(2)}, u32[]{:S(2)}) collective-permute-start(f32[1,192,128]{2,1,0:T(8,128)S(1)} %maximum_bitcast_fusion.2), channel_id=1, source_target_pairs={{0,16},{2,18},{4,20},{6,22},{8,24},{10,26},{12,28},{14,30},{16,0},... | collective-permute-start | bytes 294920 | tf_op jit(solution)/shard_map/ppermute | solution.py:33
  28.9 9.3 %collective-permute-start.1 = (f32[2,200,128]{2,1,0:T(8,128)S(1)}, f32[2,200,128]{2,1,0:T(8,128)S(1)}, u32[]{:S(2)}, u32[]{:S(2)}) collective-permute-start(f32[2,200,128]{2,1,0:T(8,128)S(1)} %pad_maximum_fusion.5), channel_id=1, source_target_pairs={{0,8},{2,10},{4,12},{6,14},{8,0},{10,2},{12,4},{14,6},{16,24},{18,... | collective-permute-start | bytes 614408 | tf_op jit(solution)/shard_map/ppermute | solution.py:33
  30.9 11.2 %collective-permute-start.6 = (f32[2,192,128]{2,1,0:T(8,128)S(1)}, f32[2,192,128]{2,1,0:T(8,128)S(1)}, u32[]{:S(2)}, u32[]{:S(2)}) collective-permute-start(f32[2,192,128]{2,1,0:T(8,128)S(1)} %pad_maximum_fusion.6), channel_id=1, source_target_pairs={{0,8},{2,10},{4,12},{6,14},{8,0},{10,2},{12,4},{14,6},{16,24},{18,... | collective-permute-start | bytes 589832 | tf_op jit(solution)/shard_map/ppermute | solution.py:33
  38.3 13.3 %collective-permute-start.2 = (f32[4,200,128]{2,1,0:T(8,128)S(1)}, f32[4,200,128]{2,1,0:T(8,128)S(1)}, u32[]{:S(2)}, u32[]{:S(2)}) collective-permute-start(f32[4,200,128]{2,1,0:T(8,128)S(1)} %pad_maximum_fusion.2), channel_id=1, source_target_pairs={{0,4},{2,6},{4,0},{6,2},{8,12},{10,14},{12,8},{14,10},{16,20},{18,... | collective-permute-start | bytes 1228808 | tf_op jit(solution)/shard_map/ppermute | solution.py:33
  42.2 17.0 %collective-permute-start.7 = (f32[4,192,128]{2,1,0:T(8,128)S(1)}, f32[4,192,128]{2,1,0:T(8,128)S(1)}, u32[]{:S(2)}, u32[]{:S(2)}) collective-permute-start(f32[4,192,128]{2,1,0:T(8,128)S(1)} %pad_maximum_fusion.3), channel_id=1, source_target_pairs={{0,2},{2,0},{4,6},{6,4},{8,10},{10,8},{12,14},{14,12},{16,18},{18,... | collective-permute-start | bytes 1179656 | tf_op jit(solution)/shard_map/ppermute | solution.py:33
  51.7 31.9 %collective-permute-start.3 = (f32[8,200,128]{2,1,0:T(8,128)S(1)}, f32[8,200,128]{2,1,0:T(8,128)S(1)}, u32[]{:S(2)}, u32[]{:S(2)}) collective-permute-start(f32[8,200,128]{2,1,0:T(8,128)S(1)} %pad_maximum_fusion), channel_id=1, source_target_pairs={{0,2},{2,0},{4,6},{6,4},{8,10},{10,8},{12,14},{14,12},{16,18},{18,... | collective-permute-start | bytes 2457608 | tf_op jit(solution)/shard_map/ppermute | solution.py:33
  59.2 29.0 %collective-permute-start.8 = (f32[8,192,128]{2,1,0:T(8,128)S(1)}, f32[8,192,128]{2,1,0:T(8,128)S(1)}, u32[]{:S(2)}, u32[]{:S(2)}) collective-permute-start(f32[8,192,128]{2,1,0:T(8,128)S(1)} %pad_maximum_fusion.1), channel_id=1, source_target_pairs={{0,4},{2,6},{4,0},{6,2},{8,12},{10,14},{12,8},{14,10},{16,20},{18,... | collective-permute-start | bytes 2359304 | tf_op jit(solution)/shard_map/ppermute | solution.py:33
  63.0 26.3 %copy-start.4 = (bf16[128,128]{1,0:T(8,128)(2,1)S(1)}, bf16[128,128]{1,0:T(8,128)(2,1)}, u32[]{:S(2)}) copy-start(bf16[128,128]{1,0:T(8,128)(2,1)} %constant.145.clone) | copy-start | bytes 98308
  83.6 9.5 %collective-permute-start.4 = (f32[16,200,128]{2,1,0:T(8,128)S(1)}, f32[16,200,128]{2,1,0:T(8,128)}, u32[]{:S(2)}, u32[]{:S(2)}) collective-permute-start(f32[16,200,128]{2,1,0:T(8,128)S(1)} %constant_dynamic-update-slice_fusion.a_own), channel_id=1, source_target_pairs={{0,1},{1,0},{2,3},{3,2},{4,5},{5,4},{6,7},{7,6},{8,9},{9,8},{10,11... | collective-permute-start | bytes 4915208 | tf_op jit(solution)/shard_map/ppermute | solution.py:33
  89.1 4.0 %collective-permute-start.9 = (f32[16,192,128]{2,1,0:T(8,128)}, f32[16,192,128]{2,1,0:T(8,128)}, u32[]{:S(2)}, u32[]{:S(2)}) collective-permute-start(f32[16,192,128]{2,1,0:T(8,128)} %constant_dynamic-update-slice_fusion.5.b_own), channel_id=1, source_target_pairs={{0,1},{1,0},{2,3},{3,2},{4,5},{5,4},{6,7},{7,6},{8,9},{9,8},{10,11... | collective-permute-start | bytes 4718600 | tf_op jit(solution)/shard_map/ppermute | solution.py:33
  89.3 1.0 copy-start.6
  89.3 3.8 %copy-start.1 = (bf16[256,512]{1,0:T(8,128)(2,1)S(1)}, bf16[256,512]{1,0:T(8,128)(2,1)}, u32[]{:S(2)}) copy-start(bf16[256,512]{1,0:T(8,128)(2,1)} %constant.147.clone.block_ref) | copy-start | bytes 786436
  89.3 3.8 %copy-start.2 = (bf16[256,128]{1,0:T(8,128)(2,1)S(1)}, bf16[256,128]{1,0:T(8,128)(2,1)}, u32[]{:S(2)}) copy-start(bf16[256,128]{1,0:T(8,128)(2,1)} %constant.146.clone.lane_ref) | copy-start | bytes 196612
  143.7 2.9 %collective-permute-start.10 = (f32[16,1,128,128]{3,2,0,1:T(8,128)S(1)}, f32[16,1,128,128]{3,2,0,1:T(8,128)}, u32[]{:S(2)}, u32[]{:S(2)}) collective-permute-start(f32[16,1,128,128]{3,2,0,1:T(8,128)S(1)} %dynamic-slice_bitcast_fusion), channel_id=1, source_target_pairs={{0,1},{1,0},{2,3},{3,2},{4,5},{5,4},{6,7},{7,6},{8,9},{9,8},{10,11... | collective-permute-start | bytes 3145736 | tf_op jit(solution)/shard_map/ppermute | solution.py:33
  148.1 8.4 %collective-permute-start.13 = (f32[512,128]{1,0:T(8,128)S(1)}, f32[512,128]{1,0:T(8,128)S(1)}, u32[]{:S(2)}, u32[]{:S(2)}) collective-permute-start(f32[512,128]{1,0:T(8,128)S(1)} %bitcast.98), channel_id=1, source_target_pairs={{0,4},{2,6},{4,0},{6,2},{8,12},{10,14},{12,8},{14,10},{16,20},{18,... | collective-permute-start | bytes 786440 | tf_op jit(solution)/shard_map/ppermute | solution.py:33
  148.9 8.8 %collective-permute-start.11 = (f32[520,128]{1,0:T(8,128)S(1)}, f32[520,128]{1,0:T(8,128)S(1)}, u32[]{:S(2)}, u32[]{:S(2)}) collective-permute-start(f32[520,128]{1,0:T(8,128)S(1)} %pad_maximum_fusion.4), channel_id=1, source_target_pairs={{0,2},{2,0},{4,6},{6,4},{8,10},{10,8},{12,14},{14,12},{16,18},{18,... | collective-permute-start | bytes 798728 | tf_op jit(solution)/shard_map/ppermute | solution.py:33
  156.6 5.0 %collective-permute-start.14 = (f32[256,128]{1,0:T(8,128)S(1)}, f32[256,128]{1,0:T(8,128)S(1)}, u32[]{:S(2)}, u32[]{:S(2)}) collective-permute-start(f32[256,128]{1,0:T(8,128)S(1)} %bitcast.105), channel_id=1, source_target_pairs={{0,2},{2,0},{4,6},{6,4},{8,10},{10,8},{12,14},{14,12},{16,18},{18,... | collective-permute-start | bytes 393224 | tf_op jit(solution)/shard_map/ppermute | solution.py:33
  157.8 5.1 %collective-permute-start.12 = (f32[264,128]{1,0:T(8,128)S(1)}, f32[264,128]{1,0:T(8,128)S(1)}, u32[]{:S(2)}, u32[]{:S(2)}) collective-permute-start(f32[264,128]{1,0:T(8,128)S(1)} %pad_maximum_fusion.7), channel_id=1, source_target_pairs={{0,4},{2,6},{4,0},{6,2},{8,12},{10,14},{12,8},{14,10},{16,20},{18,... | collective-permute-start | bytes 405512 | tf_op jit(solution)/shard_map/ppermute | solution.py:33
  163.0 5.1 %collective-permute-start.15 = (f32[264,128]{1,0:T(8,128)S(1)}, f32[264,128]{1,0:T(8,128)S(1)}, u32[]{:S(2)}, u32[]{:S(2)}) collective-permute-start(f32[264,128]{1,0:T(8,128)S(1)} %pad_maximum_fusion.8), channel_id=1, source_target_pairs={{0,8},{2,10},{4,12},{6,14},{8,0},{10,2},{12,4},{14,6},{16,24},{18,... | collective-permute-start | bytes 405512 | tf_op jit(solution)/shard_map/ppermute | solution.py:33
  168.2 6.4 %collective-permute-start.16 = (f32[136,128]{1,0:T(8,128)S(1)}, f32[136,128]{1,0:T(8,128)S(1)}, u32[]{:S(2)}, u32[]{:S(2)}) collective-permute-start(f32[136,128]{1,0:T(8,128)S(1)} %pad_maximum_fusion.9), channel_id=1, source_target_pairs={{0,16},{2,18},{4,20},{6,22},{8,24},{10,26},{12,28},{14,30},{16,0},... | collective-permute-start | bytes 208904 | tf_op jit(solution)/shard_map/ppermute | solution.py:33
Sparse Core Ops, SparseCore 0:
  12.4 86.3 all-gather.1

commit v3 on v2

--- a/solution.py
+++ b/solution.py
@@ -65,59 +65,53 @@
     return place
 
 
-def take_part(values, axis, index):
-    return lax.dynamic_index_in_dim(values, index, axis, False)
-
-
-def scatter_sum(terms, extra):
-    place = lax.axis_index("feat")
-    core = lax.axis_index("rows")
-    for bit in bits_of("rows"):
-        pair = terms.reshape((terms.shape[0], 2, bit) + terms.shape[2:])
-        mine = (core & bit) // bit
-        terms = take_part(pair, 1, mine) + swap(take_part(pair, 1, 1 - mine), "rows", bit)
-    lanes = terms.shape[-1]
+def scatter_sum(keep, send, extra):
+    terms = keep + swap(send, "rows", 1)
     bits = bits_of("feat")
-    count = terms.shape[2]
+    count, lanes = terms.shape[1:]
     terms = terms.reshape((2,) * len(bits) + (count, lanes))
     cut = count // 2
     parts = [terms[..., :cut, :], terms[..., cut:, :]]
     names = [list(bits), list(bits)]
-    orders = [[1, 2], [2, 1]]
 
     def exchange(part, left, bit, extra):
         axis = left.index(bit)
         left.remove(bit)
-        mine = (place & bit) // bit
-        keep = take_part(part, axis, mine)
-        send = take_part(part, axis, 1 - mine).reshape(-1, lanes)
+        keep = lax.index_in_dim(part, 0, axis, False)
+        send = lax.index_in_dim(part, 1, axis, False).reshape(-1, lanes)
         if extra is None:
             return keep + swap(send, "feat", bit).reshape(keep.shape), None
         got = swap(jnp.concatenate([send, extra], axis=0), "feat", bit)
         return keep + got[: send.shape[0]].reshape(keep.shape), extra + got[send.shape[0] :]
 
-    for turn in range(2):
-        parts[0], extra = exchange(parts[0], names[0], orders[0][turn], extra)
-        parts[1], _ = exchange(parts[1], names[1], orders[1][turn], None)
+    for bit_a, bit_b in ((1, 2), (2, 1)):
+        parts[0], extra = exchange(parts[0], names[0], bit_a, extra)
+        parts[1], _ = exchange(parts[1], names[1], bit_b, None)
     rest = jnp.concatenate(parts, axis=-2)
     for bit in list(reversed(names[0])):
         rest, extra = exchange(rest, names[0], bit, extra)
     return rest, extra
 
 
-def mix_kernel(rows, bits_a, bits_b, me_ref, a_own, a_other, b_own, b_other, emb_ref, lane_ref, block_ref, out_ref, sign_ref, wide_ref, spread_ref):
+def odd_bits(value):
+    value = value ^ (value >> 4)
+    value = value ^ (value >> 2)
+    return (value ^ (value >> 1)) & 1
+
+
+def mix_kernel(rows, begin, bits_a, bits_b, me_ref, a_own, a_other, b_own, b_other, emb_ref, lane_ref, block_ref, out_ref, sign_ref, wide_ref, spread_ref):
     f32 = jnp.float32
     bf16 = jnp.bfloat16
     chunks = a_own.shape[0]
     width = emb_ref.shape[0]
     quarters = width // LANES
     here = LANES // quarters
-    chunk = pl.program_id(0)
+    chunk = pl.program_id(0) + begin
 
     def flip(bits):
         return (1 - 2 * (bits & 1)).astype(f32)
 
-    @pl.when(chunk == 0)
+    @pl.when(chunk == begin)
     def _():
         for c, ref in enumerate((a_own, a_other)):
             for p in range(chunks):
@@ -177,7 +171,13 @@
         ],
         axis=0,
     ).astype(jnp.int32)
-    gain = jnp.concatenate([b_own[pb, 0:LANES, :], b_other[pb, 0:LANES, :]], axis=0)
+    gain = jnp.concatenate(
+        [
+            ref[pb, 0:LANES, :] * (1 - 2 * odd_bits((2 * chunk + c) & me_ref[0])).astype(f32)
+            for c, ref in enumerate((b_own, b_other))
+        ],
+        axis=0,
+    )
     for r in range(rows):
         columns = slice(r * LANES, (r + 1) * LANES)
         mixed = jnp.take_along_axis(first[:, columns], order, axis=1) * gain
@@ -199,27 +199,39 @@
     return [float(c) for c in fit.convert(kind=np.polynomial.Polynomial).coef]
 
 
-def head_kernel(rows, chunks, tile, coefs, grad_scale, me_ref, target_ref, y_ref, scale_ref, phase_ref, weight_ref, pred_ref, grad_ref, feat_ref, acc_ref, turn_ref):
+def head_kernel(
+    rows, tile, coefs, grad_scale, bits_a, bits_b, me_ref, target_ref, y_low, y_high, *refs
+):
+    late_refs, (pred_ref, keep_ref, send_ref, feat_ref, acc_ref, stage_ref) = refs[:12], refs[12:]
     f32 = jnp.float32
     step = pl.program_id(0)
     steps = pl.num_programs(0)
+    chunks = feat_ref.shape[0]
+    y_chunks = y_low.shape[0]
+    per_part = steps // 4
 
     @pl.when(step == 0)
     def _():
         acc_ref[...] = jnp.zeros_like(acc_ref)
 
-    second_half = (step * tile) // LANES
-    for k in range(chunks):
-        shared = (2 * k + second_half) & me_ref[0]
-        shared = shared ^ (shared >> 4)
-        shared = shared ^ (shared >> 2)
-        shared = shared ^ (shared >> 1)
-        turn_ref[k] = scale_ref[k, 0] * (1 - 2 * (shared & 1)).astype(f32)
+    for part in range(4):
+        core, bits = part // 2, (bits_a, bits_b)[part % 2]
+
+        @pl.when(step // per_part == part)
+        def _():
+            scale_ref, phase_ref, weight_ref = late_refs[3 * part : 3 * part + 3]
+            for k in range(chunks):
+                place = place_of(k, bits)
+                shared = odd_bits((2 * k + core) & me_ref[0]) ^ odd_bits(me_ref[0])
+                stage_ref[0, k] = scale_ref[place] * (1 - 2 * shared).astype(f32)
+                stage_ref[1, k] = phase_ref[place]
+                stage_ref[2, k] = weight_ref[place]
 
     for part in range(tile // 8):
         here = slice(part * 8, part * 8 + 8)
         for r in range(rows):
-            values = [y_ref[k, r, here, :] for k in range(chunks)]
+            values = [y_low[k, r, here, :] for k in range(y_chunks)]
+            values += [y_high[k, r, here, :] for k in range(chunks - y_chunks)]
             width = 1
             while width < chunks:
                 for k in range(chunks):
@@ -229,14 +241,14 @@
                 width *= 2
             acc = acc_ref[r]
             for k in range(chunks):
-                turns = values[k] * turn_ref[k, here, :] + phase_ref[k, 0, here, :]
+                turns = values[k] * stage_ref[0, k, here, :] + stage_ref[1, k, here, :]
                 u = turns - jnp.round(turns)
                 square = u * u
                 cosine = jnp.full_like(square, coefs[-1])
                 for c in coefs[-2::-1]:
                     cosine = cosine * square + c
                 feat_ref[k, r, pl.ds(pl.multiple_of(step * tile + part * 8, 8), 8), :] = cosine
-                acc = acc + cosine * weight_ref[k, 0, here, :]
+                acc = acc + cosine * stage_ref[2, k, here, :]
             acc_ref[r] = acc
 
     @pl.when(step == steps - 1)
@@ -250,16 +262,18 @@
             residuals.append(jnp.broadcast_to((total - target_ref[r]) * grad_scale, (8, LANES)))
         pred_ref[...] = jnp.broadcast_to(found, (8, LANES))
 
-        for k in range(chunks):
-
-            @pl.loop(0, CHUNK // 32)
-            def _(i):
-                for j in range(4):
-                    rows_here = pl.ds(pl.multiple_of(i * 32 + j * 8, 8), 8)
-                    total = feat_ref[k, 0, rows_here, :] * residuals[0]
-                    for r in range(1, rows):
-                        total = total + feat_ref[k, r, rows_here, :] * residuals[r]
-                    grad_ref[k, rows_here, :] = total
+        for half, out_ref in enumerate((keep_ref, send_ref)):
+            for k in range(chunks):
+
+                @pl.loop(0, LANES // 32)
+                def _(i):
+                    for j in range(4):
+                        row = pl.multiple_of(i * 32 + j * 8, 8)
+                        rows_here = pl.ds(row + half * LANES, 8)
+                        total = feat_ref[k, 0, rows_here, :] * residuals[0]
+                        for r in range(1, rows):
+                            total = total + feat_ref[k, r, rows_here, :] * residuals[r]
+                        out_ref[k, pl.ds(row, 8), :] = total
 
 
 def local(
@@ -306,38 +320,39 @@
         phases * f32(1.0 / (2.0 * math.pi)),
         weights * f32(1.0 / math.sqrt(features)),
     )
-    late = lax.all_gather(late.reshape(3 * mine, LANES), BOTH)
     bits = bits_of("feat")
-    if mine == LANES and feat_size == chunks and rows_size == 2:
+    numbers = jnp.broadcast_to(jnp.pad(numbers, (0, LANES - mine))[None, :], (8, LANES))
+    everything = [signs, positions, gains, *late, numbers]
+    direct = mine == LANES and feat_size == chunks and rows_size == 2
+    if direct:
         me = place * rows_size + core
         bits_a = bits[:-2] + [2, 1]
         bits_b = bits[:-2] + [1, 2]
     else:
         me = 0
         bits_a = bits_b = [1 << i for i in range(chunks.bit_length() - 1)]
-        whole = gather_ordered(
-            jnp.concatenate([signs, positions, gains, jnp.pad(numbers.reshape(1, mine), ((0, 7), (0, LANES - mine)))])
-        )
-        signs, positions, gains = (
-            whole[:, i * mine : (i + 1) * mine].reshape(chunks, 2, LANES, LANES) for i in range(3)
-        )
-        numbers = whole[:, 3 * mine, :mine].reshape(chunks, 2, LANES)
+        whole = gather_ordered(jnp.concatenate(everything))
+        numbers = whole[:, 6 * mine, :mine].reshape(chunks, 2, 1, LANES)
+        numbers = jnp.broadcast_to(numbers, (chunks, 2, 8, LANES))
+        everything = [whole[:, i * mine : (i + 1) * mine].reshape(chunks, 2, LANES, LANES) for i in range(6)]
+        everything.append(numbers)
+    signs, positions, gains, *late, numbers = everything
 
     per_half = LANES // quarters
     shape = signs.shape
     signs = jnp.swapaxes(signs.reshape(shape[:-2] + (per_half, quarters, LANES)), -3, -2).reshape(shape)
-    numbers = jnp.broadcast_to(numbers[..., None, :], shape[:-2] + (8, LANES))
     cut = LANES // 2
-    part_a = jnp.concatenate([signs, positions[..., :cut, :], numbers], axis=-2)
-    part_b = jnp.concatenate([gains, positions[..., cut:, :]], axis=-2)
-    if part_a.ndim == 2:
-        part_a = gather_relative(part_a, bits_a)
-        part_b = gather_relative(part_b, bits_b)
-        a_pair = (part_a, swap(part_a, "rows", 1))
-        b_pair = (part_b, swap(part_b, "rows", 1))
+    pieces = [
+        jnp.concatenate([signs, positions[..., :cut, :], numbers], axis=-2),
+        jnp.concatenate([gains, positions[..., cut:, :]], axis=-2),
+        jnp.concatenate([x[..., :cut, :] for x in late], axis=-2),
+        jnp.concatenate([x[..., cut:, :] for x in late], axis=-2),
+    ]
+    if direct:
+        pieces = [gather_relative(x, b) for x, b in zip(pieces, (bits_a, bits_b) * 2)]
+        a_pair, b_pair, c_pair, d_pair = ((x, swap(x, "rows", 1)) for x in pieces)
     else:
-        a_pair = (part_a[:, 0], part_a[:, 1])
-        b_pair = (part_b[:, 0], part_b[:, 1])
+        a_pair, b_pair, c_pair, d_pair = ((x[:, 0], x[:, 1]) for x in pieces)
 
     emb = lax.dynamic_slice_in_dim(embeddings, place * rows, rows, 0)
     lane_signs = hadamard(LANES)
@@ -353,62 +368,73 @@
 
     scalars = pl.BlockSpec(memory_space=pltpu.SMEM)
     resident_args = (*a_pair, *b_pair, emb, lane_matrix, block_matrix)
-    spread = pl.pallas_call(
-        functools.partial(mix_kernel, rows, bits_a, bits_b),
-        grid=(chunks,),
-        in_specs=[scalars] + [resident(x) for x in resident_args],
-        out_specs=pl.BlockSpec((1, rows, CHUNK, LANES), lambda k: (k, 0, 0, 0)),
-        out_shape=jax.ShapeDtypeStruct((chunks, rows, CHUNK, LANES), f32),
-        scratch_shapes=[
-            pltpu.VMEM((blocks // quarters, width), jnp.bfloat16),
-            pltpu.VMEM((width + LANES, rows * LANES), jnp.bfloat16),
-            pltpu.VMEM((2 * CHUNK, rows * LANES), jnp.bfloat16),
-        ],
-        compiler_params=pltpu.CompilerParams(vmem_limit_bytes=48 * MIB),
-        name="mix",
-    )(about_me, *resident_args)
-
-    tile = min(32, mine)
-    tiles_here = mine // tile
-    late = late.reshape(chunks, per_chunk, 3 * mine, LANES)
-
-    def late_part(which):
-        return pl.BlockSpec(
-            (chunks, 1, tile, LANES), lambda i: (0, i // tiles_here, which * tiles_here + i % tiles_here, 0)
-        )
+
+    def mix(begin, count):
+        return pl.pallas_call(
+            functools.partial(mix_kernel, rows, begin, bits_a, bits_b),
+            grid=(count,),
+            in_specs=[scalars] + [resident(x) for x in resident_args],
+            out_specs=pl.BlockSpec((1, rows, CHUNK, LANES), lambda k: (k, 0, 0, 0)),
+            out_shape=jax.ShapeDtypeStruct((count, rows, CHUNK, LANES), f32),
+            scratch_shapes=[
+                pltpu.VMEM((blocks // quarters, width), jnp.bfloat16),
+                pltpu.VMEM((width + LANES, rows * LANES), jnp.bfloat16),
+                pltpu.VMEM((2 * CHUNK, rows * LANES), jnp.bfloat16),
+            ],
+            compiler_params=pltpu.CompilerParams(vmem_limit_bytes=48 * MIB),
+            cost_estimate=pl.CostEstimate(
+                flops=count * 2 * 256 * 8192 * 256, bytes_accessed=count * rows * CHUNK * LANES * 4, transcendentals=0
+            ),
+            name="mix",
+        )(about_me, *resident_args)
+
+    split = chunks // 2
+    y_low, y_high = mix(0, split), mix(split, chunks - split)
+
+    tile = 32
+    per_part = cut // tile
+
+    def late_part(part, which):
+        def where(i):
+            return (0, which * per_part + jnp.clip(i - part * per_part, 0, per_part - 1), 0)
+
+        return pl.BlockSpec((chunks, tile, LANES), where)
 
     my_targets = lax.dynamic_slice_in_dim(targets, place * rows, rows, 0)
-    found, grads = pl.pallas_call(
+    late_args = [x for x in (c_pair[0], d_pair[0], c_pair[1], d_pair[1]) for _ in range(3)]
+    found, keep, send = pl.pallas_call(
         functools.partial(
-            head_kernel, rows, chunks, tile, turn_cosine_coefficients(5), 1.0 / math.sqrt(total_rows)
+            head_kernel, rows, tile, turn_cosine_coefficients(5), 1.0 / math.sqrt(total_rows), bits_a, bits_b
         ),
         grid=(CHUNK // tile,),
-        in_specs=[
-            scalars,
-            scalars,
-            pl.BlockSpec((chunks, rows, tile, LANES), lambda i: (0, 0, i, 0)),
-            late_part(0),
-            late_part(1),
-            late_part(2),
-        ],
+        in_specs=[scalars, scalars]
+        + [pl.BlockSpec((y.shape[0], rows, tile, LANES), lambda i: (0, 0, i, 0)) for y in (y_low, y_high)]
+        + [late_part(part, which) for part in range(4) for which in range(3)],
         out_specs=[
             pl.BlockSpec((8, LANES), lambda i: (0, 0)),
-            pl.BlockSpec((chunks, CHUNK, LANES), lambda i: (0, 0, 0)),
+            pl.BlockSpec((chunks, LANES, LANES), lambda i: (0, 0, 0)),
+            pl.BlockSpec((chunks, LANES, LANES), lambda i: (0, 0, 0)),
         ],
         out_shape=[
             jax.ShapeDtypeStruct((8, LANES), f32),
-            jax.ShapeDtypeStruct((chunks, CHUNK, LANES), f32),
+            jax.ShapeDtypeStruct((chunks, LANES, LANES), f32),
+            jax.ShapeDtypeStruct((chunks, LANES, LANES), f32),
         ],
         scratch_shapes=[
             pltpu.VMEM((chunks, rows, CHUNK, LANES), f32),
             pltpu.VMEM((rows, 8, LANES), f32),
-            pltpu.VMEM((chunks, tile, LANES), f32),
+            pltpu.VMEM((3, chunks, tile, LANES), f32),
         ],
         compiler_params=pltpu.CompilerParams(vmem_limit_bytes=48 * MIB),
         name="head",
-    )(about_me, my_targets, spread, late, late, late)
-
-    feature_grad, found = scatter_sum(grads.reshape(feat_size, rows_size, mine, LANES), found)
+    )(about_me, my_targets, y_low, y_high, *late_args)
+
+    if not direct:
+        grads = jnp.stack([keep, send], 1).reshape(feat_size, rows_size, mine, LANES)
+        grads = jnp.take(grads, jnp.arange(feat_size) ^ place, axis=0)
+        keep = lax.dynamic_index_in_dim(grads, core, 1, False)
+        send = lax.dynamic_index_in_dim(grads, core ^ 1, 1, False)
+    feature_grad, found = scatter_sum(keep, send, found)
     return found[0], feature_grad.reshape(-1)
 
 

time: 183 us -> 180 us (0.984)
  between operations: 14.5 us -> 1.35 us
  waiting for transfers between devices: 74.9 us -> 84.9 us
  other arithmetic: 7.35 us -> 3.01 us
  Pallas kernels: 50.4 us -> 53.6 us
    ppermute x17 -> x27, waiting for transfers between devices: 74.9 us -> 84.9 us  [swap(): return lax.ppermute(values, axis_name, [(i, i ^ bit) for i in range(size)])]
    pallas_call x2 -> x3, Pallas kernels: 50.4 us -> 53.6 us  [the longest x2 35.5 us: mix(): pl.pallas_call(functools.partial(mix_kernel, rows, begin, bits_a, bits_b)...]
    ppermute x17 -> x27, starting transfers between devices: 25.8 us -> 27.5 us  [swap(): return lax.ppermute(values, axis_name, [(i, i ^ bit) for i in range(size)])]
    unnamed x21 -> x39, local copies, waits for them, and re-layouts: 2.49 us -> 4.08 us
  transfers between devices with their start and end apart: 18 -> 27, of which waited for: 15 -> 19; matrix products, arithmetic and copies ran while one was open for 5% -> 2% of each run, Pallas kernels for 18% -> 20%
where the time goes in v3:
time: 180 us
  waiting for transfers between devices  84.9 us (47%)
  Pallas kernels  53.6 us (30%)
  starting transfers between devices  27.5 us (15%)
  local copies, waits for them, and re-layouts  6.12 us (3%)
  matrix products  3.42 us (2%)
  other arithmetic  3.01 us (2%)
    ppermute x27, waiting for transfers between devices, swap(): return lax.ppermute(values, axis_name, [(i, i ^ bit) for i in range(size)])  84.9 us
    pallas_call x2, Pallas kernels, mix(): pl.pallas_call(functools.partial(mix_kernel, rows, begin, bits_a, bits_b)...  35.5 us
    ppermute x27, starting transfers between devices, swap(): return lax.ppermute(values, axis_name, [(i, i ^ bit) for i in range(size)])  27.5 us
    pallas_call x1, Pallas kernels, local(): pl.pallas_call(functools.partial(head_kernel, rows, tile, turn_cosine_coe...  18 us
    unnamed x39, local copies, waits for them, and re-layouts  4.08 us
  transfers between devices with their start and end apart: 27, of which 19 were waited for; matrix products, arithmetic and copies ran while one was open for 2% of the time, Pallas kernels for 20%

profile of v3, /device:TPU:0, one launch (start us, length us, event | category | flops | bytes accessed | tf_op | source)
XLA Modules:
  0.0 180.0 jit_solution(18360275850036557347)
XLA Ops:
  1.4 3.4 %fusion = f32[1,128,128]{2,0,1:T(1,128)S(1)} fusion(bf16[2,128,128,128]{3,2,1,0:T(8,128)(2,1)} %bitcast.96, s32[]{:T(128)S(6)} %select_n.17), kind=kOutput, calls=%fused_computation | convolution fusion | flops 4194432 | bytes 4259844 | tf_op jit(solution)/shard_map/bij,j->bi/dot_general | solution.py:313
  5.2 4.1 %collective-permute-start = (f32[1,200,128]{2,1,0:T(8,128)S(1)}, f32[1,200,128]{2,1,0:T(8,128)S(1)}, u32[]{:S(2)}, u32[]{:S(2)}) collective-permute-start(f32[1,200,128]{2,1,0:T(8,128)S(1)} %maximum_bitcast_fusion), channel_id=1, source_target_pairs={{0,16},{2,18},{4,20},{6,22},{8,24},{10,26},{12,28},{14,30},{16,0},... | collective-permute-start | bytes 307208 | tf_op jit(solution)/shard_map/ppermute | solution.py:33
  10.1 3.0 %collective-permute-start.10 = (f32[1,192,128]{2,1,0:T(8,128)S(1)}, f32[1,192,128]{2,1,0:T(8,128)S(1)}, u32[]{:S(2)}, u32[]{:S(2)}) collective-permute-start(f32[1,192,128]{2,1,0:T(8,128)S(1)} %maximum_bitcast_fusion.2), channel_id=1, source_target_pairs={{0,16},{2,18},{4,20},{6,22},{8,24},{10,26},{12,28},{14,30},{16,0},... | collective-permute-start | bytes 294920 | tf_op jit(solution)/shard_map/ppermute | solution.py:33
  14.2 7.4 %collective-permute-done = f32[1,200,128]{2,1,0:T(8,128)S(1)} collective-permute-done((f32[1,200,128]{2,1,0:T(8,128)S(1)}, f32[1,200,128]{2,1,0:T(8,128)S(1)}, u32[]{:S(2)}, u32[]{:S(2)}) %collective-permute-start) | collective-permute-done | bytes 102432 | tf_op jit(solution)/shard_map/ppermute | solution.py:33
  21.6 2.1 %collective-permute-done.5 = f32[1,192,128]{2,1,0:T(8,128)S(1)} collective-permute-done((f32[1,192,128]{2,1,0:T(8,128)S(1)}, f32[1,192,128]{2,1,0:T(8,128)S(1)}, u32[]{:S(2)}, u32[]{:S(2)}) %collective-permute-start.5) | collective-permute-done | bytes 98336 | tf_op jit(solution)/shard_map/ppermute | solution.py:33
  23.8 2.0 %collective-permute-done.10 = f32[1,192,128]{2,1,0:T(8,128)S(1)} collective-permute-done((f32[1,192,128]{2,1,0:T(8,128)S(1)}, f32[1,192,128]{2,1,0:T(8,128)S(1)}, u32[]{:S(2)}, u32[]{:S(2)}) %collective-permute-start.10) | collective-permute-done | bytes 98336 | tf_op jit(solution)/shard_map/ppermute | solution.py:33
  26.0 5.6 %collective-permute-done.1 = f32[2,200,128]{2,1,0:T(8,128)S(1)} collective-permute-done((f32[2,200,128]{2,1,0:T(8,128)S(1)}, f32[2,200,128]{2,1,0:T(8,128)S(1)}, u32[]{:S(2)}, u32[]{:S(2)}) %collective-permute-start.1) | collective-permute-done | bytes 204832 | tf_op jit(solution)/shard_map/ppermute | solution.py:33
  31.6 1.6 collective-permute-start.2
  33.2 2.5 %collective-permute-done.6 = f32[2,192,128]{2,1,0:T(8,128)S(1)} collective-permute-done((f32[2,192,128]{2,1,0:T(8,128)S(1)}, f32[2,192,128]{2,1,0:T(8,128)S(1)}, u32[]{:S(2)}, u32[]{:S(2)}) %collective-permute-start.6) | collective-permute-done | bytes 196640 | tf_op jit(solution)/shard_map/ppermute | solution.py:33
  35.8 1.6 collective-permute-start.7
  37.5 5.4 %collective-permute-done.2 = f32[4,200,128]{2,1,0:T(8,128)S(1)} collective-permute-done((f32[4,200,128]{2,1,0:T(8,128)S(1)}, f32[4,200,128]{2,1,0:T(8,128)S(1)}, u32[]{:S(2)}, u32[]{:S(2)}) %collective-permute-start.2) | collective-permute-done | bytes 409632 | tf_op jit(solution)/shard_map/ppermute | solution.py:33
  43.0 1.6 collective-permute-start.3
  44.6 3.2 %collective-permute-done.7 = f32[4,192,128]{2,1,0:T(8,128)S(1)} collective-permute-done((f32[4,192,128]{2,1,0:T(8,128)S(1)}, f32[4,192,128]{2,1,0:T(8,128)S(1)}, u32[]{:S(2)}, u32[]{:S(2)}) %collective-permute-start.7) | collective-permute-done | bytes 393248 | tf_op jit(solution)/shard_map/ppermute | solution.py:33
  47.9 1.6 collective-permute-start.8
  50.1 1.6 collective-permute-start.16
  51.8 13.5 %collective-permute-done.3 = f32[8,200,128]{2,1,0:T(8,128)S(1)} collective-permute-done((f32[8,200,128]{2,1,0:T(8,128)S(1)}, f32[8,200,128]{2,1,0:T(8,128)S(1)}, u32[]{:S(2)}, u32[]{:S(2)}) %collective-permute-start.3) | collective-permute-done | bytes 819232 | tf_op jit(solution)/shard_map/ppermute | solution.py:33
  65.5 2.9 %collective-permute-done.8 = f32[8,192,128]{2,1,0:T(8,128)S(1)} collective-permute-done((f32[8,192,128]{2,1,0:T(8,128)S(1)}, f32[8,192,128]{2,1,0:T(8,128)S(1)}, u32[]{:S(2)}, u32[]{:S(2)}) %collective-permute-start.8) | collective-permute-done | bytes 786464 | tf_op jit(solution)/shard_map/ppermute | solution.py:33
  69.0 4.8 %collective-permute-done.12 = f32[4,192,128]{2,1,0:T(8,128)S(1)} collective-permute-done((f32[4,192,128]{2,1,0:T(8,128)S(1)}, f32[4,192,128]{2,1,0:T(8,128)S(1)}, u32[]{:S(2)}, u32[]{:S(2)}) %collective-permute-start.12) | collective-permute-done | bytes 393248 | tf_op jit(solution)/shard_map/ppermute | solution.py:33
  73.9 1.6 collective-permute-start.13
  75.6 1.6 collective-permute-start.17
  77.3 13.2 %collective-permute-done.13 = f32[8,192,128]{2,1,0:T(8,128)S(1)} collective-permute-done((f32[8,192,128]{2,1,0:T(8,128)S(1)}, f32[8,192,128]{2,1,0:T(8,128)S(1)}, u32[]{:S(2)}, u32[]{:S(2)}) %collective-permute-start.13) | collective-permute-done | bytes 786464 | tf_op jit(solution)/shard_map/ppermute | solution.py:33
  93.2 17.8 %mix.2.y_low = f32[8,8,256,128]{3,2,1,0:T(8,128)} custom-call(s32[2]{0:T(128)S(1)} %pad_add_fusion.me_ref, f32[16,200,128]{2,1,0:T(8,128)S(1)} %constant_dynamic-update-slice_fusion.a_own, f32[16,200,128]{2,1,0:T(8,128)} %copy-done.11, f32[16,192,128]{2,1,0:T(8,128)S(1)} %constant_dynamic-update-slice_fusion.5.b_own, ...), custom_call_target="tpu_custom_call" | custom-call | flops 8589934592 | bytes 8388608 | tf_op jit(solution)/shard_map/mix/pallas_call | solution.py:373
  111.0 17.7 %mix.3.y_high = f32[8,8,256,128]{3,2,1,0:T(8,128)} custom-call(s32[2]{0:T(128)S(1)} %pad_add_fusion.me_ref, f32[16,200,128]{2,1,0:T(8,128)S(1)} %constant_dynamic-update-slice_fusion.a_own, f32[16,200,128]{2,1,0:T(8,128)} %copy-done.11, f32[16,192,128]{2,1,0:T(8,128)S(1)} %constant_dynamic-update-slice_fusion.5.b_own, ...), custom_call_target="tpu_custom_call" | custom-call | flops 8589934592 | bytes 8388608 | tf_op jit(solution)/shard_map/mix/pallas_call | solution.py:373
  131.1 18.0 %head.1 = (f32[8,128]{1,0:T(8,128)S(1)}, f32[16,128,128]{2,1,0:T(8,128)S(1)}, f32[16,128,128]{2,1,0:T(8,128)S(1)}) custom-call(s32[2]{0:T(128)S(1)} %pad_add_fusion.me_ref, f32[8]{0:T(128)S(1)} %dynamic_slice.30.target_ref, f32[8,8,256,128]{3,2,1,0:T(8,128)} %mix.2.y_low, f32[8,8,256,128]{3,2,1,0:T(8,128)} %mix.3.y_high, ...), custom_call_target="tpu_custom_call" | custom-call | tf_op jit(solution)/shard_map/head/pallas_call | solution.py:405
  149.7 2.3 %collective-permute-done.20 = f32[16,128,128]{2,1,0:T(8,128)S(1)} collective-permute-done((f32[16,128,128]{2,1,0:T(8,128)S(1)}, f32[16,128,128]{2,1,0:T(8,128)S(1)}, u32[]{:S(2)}, u32[]{:S(2)}) %collective-permute-start.20) | collective-permute-done | bytes 1048608 | tf_op jit(solution)/shard_map/ppermute | solution.py:33
  152.2 1.6 collective-permute-start.23
  155.0 5.9 %collective-permute-done.23 = f32[512,128]{1,0:T(8,128)S(1)} collective-permute-done((f32[512,128]{1,0:T(8,128)S(1)}, f32[512,128]{1,0:T(8,128)S(1)}, u32[]{:S(2)}, u32[]{:S(2)}) %collective-permute-start.23) | collective-permute-done | bytes 262176 | tf_op jit(solution)/shard_map/ppermute | solution.py:33
  163.8 2.2 %collective-permute-done.24 = f32[256,128]{1,0:T(8,128)S(1)} collective-permute-done((f32[256,128]{1,0:T(8,128)S(1)}, f32[256,128]{1,0:T(8,128)S(1)}, u32[]{:S(2)}, u32[]{:S(2)}) %collective-permute-start.24) | collective-permute-done | bytes 131104 | tf_op jit(solution)/shard_map/ppermute | solution.py:33
  166.0 1.5 collective-permute-done.22
  167.7 5.0 %collective-permute-done.25 = f32[264,128]{1,0:T(8,128)S(1)} collective-permute-done((f32[264,128]{1,0:T(8,128)S(1)}, f32[264,128]{1,0:T(8,128)S(1)}, u32[]{:S(2)}, u32[]{:S(2)}) %collective-permute-start.25) | collective-permute-done | bytes 135200 | tf_op jit(solution)/shard_map/ppermute | solution.py:33
  172.8 2.1 %collective-permute-start.26 = (f32[136,128]{1,0:T(8,128)S(1)}, f32[136,128]{1,0:T(8,128)S(1)}, u32[]{:S(2)}, u32[]{:S(2)}) collective-permute-start(f32[136,128]{1,0:T(8,128)S(1)} %pad_maximum_fusion.16), channel_id=1, source_target_pairs={{0,16},{2,18},{4,20},{6,22},{8,24},{10,26},{12,28},{14,30},{16,0},... | collective-permute-start | bytes 208904 | tf_op jit(solution)/shard_map/ppermute | solution.py:33
  174.9 3.9 %collective-permute-done.26 = f32[136,128]{1,0:T(8,128)S(1)} collective-permute-done((f32[136,128]{1,0:T(8,128)S(1)}, f32[136,128]{1,0:T(8,128)S(1)}, u32[]{:S(2)}, u32[]{:S(2)}) %collective-permute-start.26) | collective-permute-done | bytes 69664 | tf_op jit(solution)/shard_map/ppermute | solution.py:33
  (136 shorter events, 16.1 us)
Async XLA Ops:
  0.6 12.6 %copy-start = (bf16[128,512]{1,0:T(8,128)(2,1)S(1)}, bf16[128,512]{1,0:T(8,128)(2,1)}, u32[]{:S(2)}) copy-start(bf16[128,512]{1,0:T(8,128)(2,1)} %param.12) | copy-start | bytes 393220
  5.2 8.2 %copy-start.10 = (bf16[128,128]{1,0:T(8,128)(2,1)S(1)}, bf16[128,128]{1,0:T(8,128)(2,1)}, u32[]{:S(2)}) copy-start(bf16[128,128]{1,0:T(8,128)(2,1)} %constant.48.clone) | copy-start | bytes 98308
  5.2 16.3 %collective-permute-start = (f32[1,200,128]{2,1,0:T(8,128)S(1)}, f32[1,200,128]{2,1,0:T(8,128)S(1)}, u32[]{:S(2)}, u32[]{:S(2)}) collective-permute-start(f32[1,200,128]{2,1,0:T(8,128)S(1)} %maximum_bitcast_fusion), channel_id=1, source_target_pairs={{0,16},{2,18},{4,20},{6,22},{8,24},{10,26},{12,28},{14,30},{16,0},... | collective-permute-start | bytes 307208 | tf_op jit(solution)/shard_map/ppermute | solution.py:33
  9.3 14.4 %collective-permute-start.5 = (f32[1,192,128]{2,1,0:T(8,128)S(1)}, f32[1,192,128]{2,1,0:T(8,128)S(1)}, u32[]{:S(2)}, u32[]{:S(2)}) collective-permute-start(f32[1,192,128]{2,1,0:T(8,128)S(1)} %maximum_bitcast_fusion.1), channel_id=1, source_target_pairs={{0,16},{2,18},{4,20},{6,22},{8,24},{10,26},{12,28},{14,30},{16,0},... | collective-permute-start | bytes 294920 | tf_op jit(solution)/shard_map/ppermute | solution.py:33
  10.1 15.7 %collective-permute-start.10 = (f32[1,192,128]{2,1,0:T(8,128)S(1)}, f32[1,192,128]{2,1,0:T(8,128)S(1)}, u32[]{:S(2)}, u32[]{:S(2)}) collective-permute-start(f32[1,192,128]{2,1,0:T(8,128)S(1)} %maximum_bitcast_fusion.2), channel_id=1, source_target_pairs={{0,16},{2,18},{4,20},{6,22},{8,24},{10,26},{12,28},{14,30},{16,0},... | collective-permute-start | bytes 294920 | tf_op jit(solution)/shard_map/ppermute | solution.py:33
  13.1 24.3 %collective-permute-start.14 = (f32[1,192,128]{2,1,0:T(8,128)S(1)}, f32[1,192,128]{2,1,0:T(8,128)S(1)}, u32[]{:S(2)}, u32[]{:S(2)}) collective-permute-start(f32[1,192,128]{2,1,0:T(8,128)S(1)} %maximum_bitcast_fusion.3), channel_id=1, source_target_pairs={{0,16},{2,18},{4,20},{6,22},{8,24},{10,26},{12,28},{14,30},{16,0},... | collective-permute-start | bytes 294920 | tf_op jit(solution)/shard_map/ppermute | solution.py:33
  21.6 9.9 %collective-permute-start.1 = (f32[2,200,128]{2,1,0:T(8,128)S(1)}, f32[2,200,128]{2,1,0:T(8,128)S(1)}, u32[]{:S(2)}, u32[]{:S(2)}) collective-permute-start(f32[2,200,128]{2,1,0:T(8,128)S(1)} %pad_maximum_fusion.9), channel_id=1, source_target_pairs={{0,8},{2,10},{4,12},{6,14},{8,0},{10,2},{12,4},{14,6},{16,24},{18,... | collective-permute-start | bytes 614408 | tf_op jit(solution)/shard_map/ppermute | solution.py:33
  23.8 12.0 %collective-permute-start.6 = (f32[2,192,128]{2,1,0:T(8,128)S(1)}, f32[2,192,128]{2,1,0:T(8,128)S(1)}, u32[]{:S(2)}, u32[]{:S(2)}) collective-permute-start(f32[2,192,128]{2,1,0:T(8,128)S(1)} %pad_maximum_fusion.10), channel_id=1, source_target_pairs={{0,8},{2,10},{4,12},{6,14},{8,0},{10,2},{12,4},{14,6},{16,24},{18,... | collective-permute-start | bytes 589832 | tf_op jit(solution)/shard_map/ppermute | solution.py:33
  25.9 23.6 %collective-permute-start.11 = (f32[2,192,128]{2,1,0:T(8,128)S(1)}, f32[2,192,128]{2,1,0:T(8,128)S(1)}, u32[]{:S(2)}, u32[]{:S(2)}) collective-permute-start(f32[2,192,128]{2,1,0:T(8,128)S(1)} %pad_maximum_fusion.11), channel_id=1, source_target_pairs={{0,8},{2,10},{4,12},{6,14},{8,0},{10,2},{12,4},{14,6},{16,24},{18,... | collective-permute-start | bytes 589832 | tf_op jit(solution)/shard_map/ppermute | solution.py:33
  31.6 11.4 %collective-permute-start.2 = (f32[4,200,128]{2,1,0:T(8,128)S(1)}, f32[4,200,128]{2,1,0:T(8,128)S(1)}, u32[]{:S(2)}, u32[]{:S(2)}) collective-permute-start(f32[4,200,128]{2,1,0:T(8,128)S(1)} %pad_maximum_fusion.4), channel_id=1, source_target_pairs={{0,4},{2,6},{4,0},{6,2},{8,12},{10,14},{12,8},{14,10},{16,20},{18,... | collective-permute-start | bytes 1228808 | tf_op jit(solution)/shard_map/ppermute | solution.py:33
  35.8 12.1 %collective-permute-start.7 = (f32[4,192,128]{2,1,0:T(8,128)S(1)}, f32[4,192,128]{2,1,0:T(8,128)S(1)}, u32[]{:S(2)}, u32[]{:S(2)}) collective-permute-start(f32[4,192,128]{2,1,0:T(8,128)S(1)} %pad_maximum_fusion.5), channel_id=1, source_target_pairs={{0,2},{2,0},{4,6},{6,4},{8,10},{10,8},{12,14},{14,12},{16,18},{18,... | collective-permute-start | bytes 1179656 | tf_op jit(solution)/shard_map/ppermute | solution.py:33
  37.4 12.7 %collective-permute-start.15 = (f32[2,192,128]{2,1,0:T(8,128)S(1)}, f32[2,192,128]{2,1,0:T(8,128)S(1)}, u32[]{:S(2)}, u32[]{:S(2)}) collective-permute-start(f32[2,192,128]{2,1,0:T(8,128)S(1)} %pad_maximum_fusion.12), channel_id=1, source_target_pairs={{0,8},{2,10},{4,12},{6,14},{8,0},{10,2},{12,4},{14,6},{16,24},{18,... | collective-permute-start | bytes 589832 | tf_op jit(solution)/shard_map/ppermute | solution.py:33
  43.0 22.4 %collective-permute-start.3 = (f32[8,200,128]{2,1,0:T(8,128)S(1)}, f32[8,200,128]{2,1,0:T(8,128)S(1)}, u32[]{:S(2)}, u32[]{:S(2)}) collective-permute-start(f32[8,200,128]{2,1,0:T(8,128)S(1)} %pad_maximum_fusion), channel_id=1, source_target_pairs={{0,2},{2,0},{4,6},{6,4},{8,10},{10,8},{12,14},{14,12},{16,18},{18,... | collective-permute-start | bytes 2457608 | tf_op jit(solution)/shard_map/ppermute | solution.py:33
  47.9 20.5 %collective-permute-start.8 = (f32[8,192,128]{2,1,0:T(8,128)S(1)}, f32[8,192,128]{2,1,0:T(8,128)S(1)}, u32[]{:S(2)}, u32[]{:S(2)}) collective-permute-start(f32[8,192,128]{2,1,0:T(8,128)S(1)} %pad_maximum_fusion.1), channel_id=1, source_target_pairs={{0,4},{2,6},{4,0},{6,2},{8,12},{10,14},{12,8},{14,10},{16,20},{18,... | collective-permute-start | bytes 2359304 | tf_op jit(solution)/shard_map/ppermute | solution.py:33
  49.5 24.3 %collective-permute-start.12 = (f32[4,192,128]{2,1,0:T(8,128)S(1)}, f32[4,192,128]{2,1,0:T(8,128)S(1)}, u32[]{:S(2)}, u32[]{:S(2)}) collective-permute-start(f32[4,192,128]{2,1,0:T(8,128)S(1)} %pad_maximum_fusion.6), channel_id=1, source_target_pairs={{0,4},{2,6},{4,0},{6,2},{8,12},{10,14},{12,8},{14,10},{16,20},{18,... | collective-permute-start | bytes 1179656 | tf_op jit(solution)/shard_map/ppermute | solution.py:33
  50.1 25.4 %collective-permute-start.16 = (f32[4,192,128]{2,1,0:T(8,128)S(1)}, f32[4,192,128]{2,1,0:T(8,128)S(1)}, u32[]{:S(2)}, u32[]{:S(2)}) collective-permute-start(f32[4,192,128]{2,1,0:T(8,128)S(1)} %pad_maximum_fusion.7), channel_id=1, source_target_pairs={{0,2},{2,0},{4,6},{6,4},{8,10},{10,8},{12,14},{14,12},{16,18},{18,... | collective-permute-start | bytes 1179656 | tf_op jit(solution)/shard_map/ppermute | solution.py:33
  51.8 16.8 %copy-start.12 = (f32[128]{0:T(128)S(1)}, f32[128]{0:T(128)}, u32[]{:S(2)}) copy-start(f32[128]{0:T(128)} %param.20) | copy-start | bytes 1540
  65.4 26.6 %collective-permute-start.4 = (f32[16,200,128]{2,1,0:T(8,128)S(1)}, f32[16,200,128]{2,1,0:T(8,128)S(1)}, u32[]{:S(2)}, u32[]{:S(2)}) collective-permute-start(f32[16,200,128]{2,1,0:T(8,128)S(1)} %constant_dynamic-update-slice_fusion.a_own), channel_id=1, source_target_pairs={{0,1},{1,0},{2,3},{3,2},{4,5},{5,4},{6,7},{7,6},{8,9},{9,8},{10,11... | collective-permute-start | bytes 4915208 | tf_op jit(solution)/shard_map/ppermute | solution.py:33
  68.5 23.5 %collective-permute-start.9 = (f32[16,192,128]{2,1,0:T(8,128)S(1)}, f32[16,192,128]{2,1,0:T(8,128)S(1)}, u32[]{:S(2)}, u32[]{:S(2)}) collective-permute-start(f32[16,192,128]{2,1,0:T(8,128)S(1)} %constant_dynamic-update-slice_fusion.5.b_own), channel_id=1, source_target_pairs={{0,1},{1,0},{2,3},{3,2},{4,5},{5,4},{6,7},{7,6},{8,9},{9,8},{10,11... | collective-permute-start | bytes 4718600 | tf_op jit(solution)/shard_map/ppermute | solution.py:33
  73.9 16.6 %collective-permute-start.13 = (f32[8,192,128]{2,1,0:T(8,128)S(1)}, f32[8,192,128]{2,1,0:T(8,128)S(1)}, u32[]{:S(2)}, u32[]{:S(2)}) collective-permute-start(f32[8,192,128]{2,1,0:T(8,128)S(1)} %pad_maximum_fusion.2), channel_id=1, source_target_pairs={{0,2},{2,0},{4,6},{6,4},{8,10},{10,8},{12,14},{14,12},{16,18},{18,... | collective-permute-start | bytes 2359304 | tf_op jit(solution)/shard_map/ppermute | solution.py:33
  75.6 16.3 %collective-permute-start.17 = (f32[8,192,128]{2,1,0:T(8,128)S(1)}, f32[8,192,128]{2,1,0:T(8,128)S(1)}, u32[]{:S(2)}, u32[]{:S(2)}) collective-permute-start(f32[8,192,128]{2,1,0:T(8,128)S(1)} %pad_maximum_fusion.3), channel_id=1, source_target_pairs={{0,4},{2,6},{4,0},{6,2},{8,12},{10,14},{12,8},{14,10},{16,20},{18,... | collective-permute-start | bytes 2359304 | tf_op jit(solution)/shard_map/ppermute | solution.py:33
  77.3 16.0 %copy-start.1 = (bf16[256,512]{1,0:T(8,128)(2,1)S(1)}, bf16[256,512]{1,0:T(8,128)(2,1)}, u32[]{:S(2)}) copy-start(bf16[256,512]{1,0:T(8,128)(2,1)} %constant.50.clone.block_ref) | copy-start | bytes 786436
  77.3 15.9 %copy-start.2 = (bf16[256,128]{1,0:T(8,128)(2,1)S(1)}, bf16[256,128]{1,0:T(8,128)(2,1)}, u32[]{:S(2)}) copy-start(bf16[256,128]{1,0:T(8,128)(2,1)} %constant.49.clone.lane_ref) | copy-start | bytes 196612
  90.6 38.2 %collective-permute-start.18 = (f32[16,192,128]{2,1,0:T(8,128)S(1)}, f32[16,192,128]{2,1,0:T(8,128)S(1)}, u32[]{:S(2)}, u32[]{:S(2)}) collective-permute-start(f32[16,192,128]{2,1,0:T(8,128)S(1)} %constant_dynamic-update-slice_fusion.10.refs_0_.refs_1_.refs_2_), channel_id=1, source_target_pairs={{0,1},{1,0},{2,3},{3,2},{4,5},{5,4},{6,7},{7,6},{8,9},{9,8},{10,11... | collective-permute-start | bytes 4718600 | tf_op jit(solution)/shard_map/ppermute | solution.py:33
  91.9 36.8 %collective-permute-start.19 = (f32[16,192,128]{2,1,0:T(8,128)S(1)}, f32[16,192,128]{2,1,0:T(8,128)S(1)}, u32[]{:S(2)}, u32[]{:S(2)}) collective-permute-start(f32[16,192,128]{2,1,0:T(8,128)S(1)} %constant_dynamic-update-slice_fusion.15.refs_3_.refs_4_.refs_5_), channel_id=1, source_target_pairs={{0,1},{1,0},{2,3},{3,2},{4,5},{5,4},{6,7},{7,6},{8,9},{9,8},{10,11... | collective-permute-start | bytes 4718600 | tf_op jit(solution)/shard_map/ppermute | solution.py:33
  149.2 2.8 %collective-permute-start.20 = (f32[16,128,128]{2,1,0:T(8,128)S(1)}, f32[16,128,128]{2,1,0:T(8,128)S(1)}, u32[]{:S(2)}, u32[]{:S(2)}) collective-permute-start(f32[16,128,128]{2,1,0:T(8,128)S(1)} %get-tuple-element.7), channel_id=1, source_target_pairs={{0,1},{1,0},{2,3},{3,2},{4,5},{5,4},{6,7},{7,6},{8,9},{9,8},{10,11... | collective-permute-start | bytes 3145736 | tf_op jit(solution)/shard_map/ppermute | solution.py:33
  152.2 8.7 %collective-permute-start.23 = (f32[512,128]{1,0:T(8,128)S(1)}, f32[512,128]{1,0:T(8,128)S(1)}, u32[]{:S(2)}, u32[]{:S(2)}) collective-permute-start(f32[512,128]{1,0:T(8,128)S(1)} %bitcast.122), channel_id=1, source_target_pairs={{0,4},{2,6},{4,0},{6,2},{8,12},{10,14},{12,8},{14,10},{16,20},{18,... | collective-permute-start | bytes 786440 | tf_op jit(solution)/shard_map/ppermute | solution.py:33
  153.9 8.4 %collective-permute-start.21 = (f32[520,128]{1,0:T(8,128)S(1)}, f32[520,128]{1,0:T(8,128)S(1)}, u32[]{:S(2)}, u32[]{:S(2)}) collective-permute-start(f32[520,128]{1,0:T(8,128)S(1)} %pad_maximum_fusion.8), channel_id=1, source_target_pairs={{0,2},{2,0},{4,6},{6,4},{8,10},{10,8},{12,14},{14,12},{16,18},{18,... | collective-permute-start | bytes 798728 | tf_op jit(solution)/shard_map/ppermute | solution.py:33
  160.9 5.0 %collective-permute-start.24 = (f32[256,128]{1,0:T(8,128)S(1)}, f32[256,128]{1,0:T(8,128)S(1)}, u32[]{:S(2)}, u32[]{:S(2)}) collective-permute-start(f32[256,128]{1,0:T(8,128)S(1)} %bitcast.124), channel_id=1, source_target_pairs={{0,2},{2,0},{4,6},{6,4},{8,10},{10,8},{12,14},{14,12},{16,18},{18,... | collective-permute-start | bytes 393224 | tf_op jit(solution)/shard_map/ppermute | solution.py:33
  162.5 5.1 %collective-permute-start.22 = (f32[264,128]{1,0:T(8,128)S(1)}, f32[264,128]{1,0:T(8,128)S(1)}, u32[]{:S(2)}, u32[]{:S(2)}) collective-permute-start(f32[264,128]{1,0:T(8,128)S(1)} %pad_maximum_fusion.13), channel_id=1, source_target_pairs={{0,4},{2,6},{4,0},{6,2},{8,12},{10,14},{12,8},{14,10},{16,20},{18,... | collective-permute-start | bytes 405512 | tf_op jit(solution)/shard_map/ppermute | solution.py:33
  167.6 5.1 %collective-permute-start.25 = (f32[264,128]{1,0:T(8,128)S(1)}, f32[264,128]{1,0:T(8,128)S(1)}, u32[]{:S(2)}, u32[]{:S(2)}) collective-permute-start(f32[264,128]{1,0:T(8,128)S(1)} %pad_maximum_fusion.14), channel_id=1, source_target_pairs={{0,8},{2,10},{4,12},{6,14},{8,0},{10,2},{12,4},{14,6},{16,24},{18,... | collective-permute-start | bytes 405512 | tf_op jit(solution)/shard_map/ppermute | solution.py:33
  172.8 6.0 %collective-permute-start.26 = (f32[136,128]{1,0:T(8,128)S(1)}, f32[136,128]{1,0:T(8,128)S(1)}, u32[]{:S(2)}, u32[]{:S(2)}) collective-permute-start(f32[136,128]{1,0:T(8,128)S(1)} %pad_maximum_fusion.16), channel_id=1, source_target_pairs={{0,16},{2,18},{4,20},{6,22},{8,24},{10,26},{12,28},{14,30},{16,0},... | collective-permute-start | bytes 208904 | tf_op jit(solution)/shard_map/ppermute | solution.py:33
  (8 other events, 28.2 us)

commit v4 on v3

--- a/solution.py
+++ b/solution.py
@@ -51,11 +51,12 @@
     return held
 
 
-def gather_relative(piece, bits):
-    held = piece[None]
-    for bit in bits:
-        held = jnp.concatenate([held, swap(held, "feat", bit)], axis=0)
-    return held
+def after(value, *others):
+    return lax.optimization_barrier((value, *others))[0]
+
+
+def doubled(held, bit):
+    return jnp.concatenate([held, swap(held, "feat", bit)], axis=0)
 
 
 def place_of(distance, bits):
@@ -200,14 +201,14 @@
 
 
 def head_kernel(
-    rows, tile, coefs, grad_scale, bits_a, bits_b, me_ref, target_ref, y_low, y_high, *refs
+    rows, tile, coefs, grad_scale, bits_a, bits_b, parts, me_ref, target_ref, *refs
 ):
-    late_refs, (pred_ref, keep_ref, send_ref, feat_ref, acc_ref, stage_ref) = refs[:12], refs[12:]
+    y_refs, late_refs, refs = refs[:parts], refs[parts : parts + 12], refs[parts + 12 :]
+    pred_ref, keep_ref, send_ref, feat_ref, acc_ref, stage_ref = refs
     f32 = jnp.float32
     step = pl.program_id(0)
     steps = pl.num_programs(0)
     chunks = feat_ref.shape[0]
-    y_chunks = y_low.shape[0]
     per_part = steps // 4
 
     @pl.when(step == 0)
@@ -230,8 +231,7 @@
     for part in range(tile // 8):
         here = slice(part * 8, part * 8 + 8)
         for r in range(rows):
-            values = [y_low[k, r, here, :] for k in range(y_chunks)]
-            values += [y_high[k, r, here, :] for k in range(chunks - y_chunks)]
+            values = [y_ref[k, r, here, :] for y_ref in y_refs for k in range(y_ref.shape[0])]
             width = 1
             while width < chunks:
                 for k in range(chunks):
@@ -349,8 +349,21 @@
         jnp.concatenate([x[..., cut:, :] for x in late], axis=-2),
     ]
     if direct:
-        pieces = [gather_relative(x, b) for x, b in zip(pieces, (bits_a, bits_b) * 2)]
-        a_pair, b_pair, c_pair, d_pair = ((x, swap(x, "rows", 1)) for x in pieces)
+        early = [x[None] for x in pieces[:2]]
+        late = [x[None] for x in pieces[2:]]
+        for i in range(len(bits)):
+            if i == len(bits) - 2:
+                late = [after(x, *early) for x in late]
+            if i >= len(bits) - 2:
+                late = [doubled(x, bits[i + 2 - len(bits)]) for x in late]
+            early = [doubled(x, b[i]) for x, b in zip(early, (bits_a, bits_b))]
+            if i >= len(bits) - 2:
+                early = [after(x, *late) for x in early]
+        for i in range(2, len(bits) - 2):
+            late = [doubled(x, bits[i]) for x in late]
+        late = [after(x, *early) for x in late]
+        late_got = [swap(x, "feat", b[-2]) for x, b in zip(late, (bits_a, bits_b))]
+        a_pair, b_pair = ((x, swap(x, "rows", 1)) for x in early)
     else:
         a_pair, b_pair, c_pair, d_pair = ((x[:, 0], x[:, 1]) for x in pieces)
 
@@ -388,8 +401,16 @@
             name="mix",
         )(about_me, *resident_args)
 
-    split = chunks // 2
-    y_low, y_high = mix(0, split), mix(split, chunks - split)
+    cuts = (0, chunks // 4, chunks * 3 // 4, chunks)
+    spread = [mix(cuts[0], cuts[1] - cuts[0])]
+    if direct:
+        late = [jnp.concatenate([x, after(y, spread[0])], axis=0) for x, y in zip(late, late_got)]
+        late_got = [swap(x, "feat", b[-1]) for x, b in zip(late, (bits_a, bits_b))]
+    spread.append(mix(cuts[1], cuts[2] - cuts[1]))
+    if direct:
+        late = [jnp.concatenate([x, after(y, spread[1])], axis=0) for x, y in zip(late, late_got)]
+        c_pair, d_pair = ((x, swap(x, "rows", 1)) for x in late)
+    spread.append(mix(cuts[2], cuts[3] - cuts[2]))
 
     tile = 32
     per_part = cut // tile
@@ -404,11 +425,11 @@
     late_args = [x for x in (c_pair[0], d_pair[0], c_pair[1], d_pair[1]) for _ in range(3)]
     found, keep, send = pl.pallas_call(
         functools.partial(
-            head_kernel, rows, tile, turn_cosine_coefficients(5), 1.0 / math.sqrt(total_rows), bits_a, bits_b
+            head_kernel, rows, tile, turn_cosine_coefficients(5), 1.0 / math.sqrt(total_rows), bits_a, bits_b, len(spread)
         ),
         grid=(CHUNK // tile,),
         in_specs=[scalars, scalars]
-        + [pl.BlockSpec((y.shape[0], rows, tile, LANES), lambda i: (0, 0, i, 0)) for y in (y_low, y_high)]
+        + [pl.BlockSpec((y.shape[0], rows, tile, LANES), lambda i: (0, 0, i, 0)) for y in spread]
         + [late_part(part, which) for part in range(4) for which in range(3)],
         out_specs=[
             pl.BlockSpec((8, LANES), lambda i: (0, 0)),
@@ -427,7 +448,7 @@
         ],
         compiler_params=pltpu.CompilerParams(vmem_limit_bytes=48 * MIB),
         name="head",
-    )(about_me, my_targets, y_low, y_high, *late_args)
+    )(about_me, my_targets, *spread, *late_args)
 
     if not direct:
         grads = jnp.stack([keep, send], 1).reshape(feat_size, rows_size, mine, LANES)

time: 180 us -> 162 us (0.900)
  waiting for transfers between devices: 84.9 us -> 60.4 us
  Pallas kernels: 53.6 us -> 58.3 us
  starting transfers between devices: 27.5 us -> 29.4 us
    ppermute x27, waiting for transfers between devices: 84.9 us -> 60.4 us  [swap(): return lax.ppermute(values, axis_name, [(i, i ^ bit) for i in range(size)])]
    pallas_call x2 -> x3, Pallas kernels: 35.5 us -> 40.1 us  [mix(): pl.pallas_call(functools.partial(mix_kernel, rows, begin, bits_a, bits_b)...]
    ppermute x27, starting transfers between devices: 27.5 us -> 29.4 us  [swap(): return lax.ppermute(values, axis_name, [(i, i ^ bit) for i in range(size)])]
    unnamed x39 -> x41, local copies, waits for them, and re-layouts: 4.08 us -> 3.55 us
  transfers between devices with their start and end apart: 27 -> 27, of which waited for: 19 -> 18; matrix products, arithmetic and copies ran while one was open for 2% -> 2% of each run, Pallas kernels for 20% -> 25%
where the time goes in v4:
time: 162 us
  waiting for transfers between devices  60.4 us (37%)
  Pallas kernels  58.3 us (36%)
  starting transfers between devices  29.4 us (18%)
  local copies, waits for them, and re-layouts  5.51 us (3%)
  matrix products  3.42 us (2%)
  other arithmetic  3.33 us (2%)
    ppermute x27, waiting for transfers between devices, swap(): return lax.ppermute(values, axis_name, [(i, i ^ bit) for i in range(size)])  60.4 us
    pallas_call x3, Pallas kernels, mix(): pl.pallas_call(functools.partial(mix_kernel, rows, begin, bits_a, bits_b)...  40.1 us
    ppermute x27, starting transfers between devices, swap(): return lax.ppermute(values, axis_name, [(i, i ^ bit) for i in range(size)])  29.4 us
    pallas_call x1, Pallas kernels, local(): pl.pallas_call(functools.partial(head_kernel, rows, tile, turn_cosine_coe...  18.1 us
    unnamed x41, local copies, waits for them, and re-layouts  3.55 us
    dot_general x1, matrix products, local(): jnp.einsum('bij,j->bi', half(block_permutations), jnp.arange(LANES).astyp...  3.42 us
  transfers between devices with their start and end apart: 27, of which 18 were waited for; matrix products, arithmetic and copies ran while one was open for 2% of the time, Pallas kernels for 25%

profile of v4, /device:TPU:0, one launch (start us, length us, event | category | flops | bytes accessed | tf_op | source)
XLA Modules:
  0.0 161.6 jit_solution(16693718417809674421)
XLA Ops:
  1.4 3.4 %fusion = f32[1,128,128]{2,0,1:T(1,128)S(1)} fusion(bf16[2,128,128,128]{3,2,1,0:T(8,128)(2,1)} %bitcast.89, s32[]{:T(128)S(6)} %select_n.17), kind=kOutput, calls=%fused_computation | convolution fusion | flops 4194432 | bytes 4259844 | tf_op jit(solution)/shard_map/bij,j->bi/dot_general | solution.py:313
  5.2 4.1 %collective-permute-start = (f32[1,200,128]{2,1,0:T(8,128)S(1)}, f32[1,200,128]{2,1,0:T(8,128)S(1)}, u32[]{:S(2)}, u32[]{:S(2)}) collective-permute-start(f32[1,200,128]{2,1,0:T(8,128)S(1)} %maximum_bitcast_fusion), channel_id=1, source_target_pairs={{0,16},{2,18},{4,20},{6,22},{8,24},{10,26},{12,28},{14,30},{16,0},... | collective-permute-start | bytes 307208 | tf_op jit(solution)/shard_map/ppermute | solution.py:33
  10.1 8.5 %collective-permute-done.3 = f32[1,192,128]{2,1,0:T(8,128)S(1)} collective-permute-done((f32[1,192,128]{2,1,0:T(8,128)S(1)}, f32[1,192,128]{2,1,0:T(8,128)S(1)}, u32[]{:S(2)}, u32[]{:S(2)}) %collective-permute-start.3) | collective-permute-done | bytes 98336 | tf_op jit(solution)/shard_map/ppermute | solution.py:33
  19.4 1.4 collective-permute-start.1
  20.8 5.7 %collective-permute-done.4 = f32[2,192,128]{2,1,0:T(8,128)S(1)} collective-permute-done((f32[2,192,128]{2,1,0:T(8,128)S(1)}, f32[2,192,128]{2,1,0:T(8,128)S(1)}, u32[]{:S(2)}, u32[]{:S(2)}) %collective-permute-start.4) | collective-permute-done | bytes 196640 | tf_op jit(solution)/shard_map/ppermute | solution.py:33
  26.6 1.6 collective-permute-start.11
  29.2 1.4 collective-permute-start.2
  30.6 3.4 %collective-permute-start.5 = (f32[1,192,128]{2,1,0:T(8,128)S(1)}, f32[1,192,128]{2,1,0:T(8,128)S(1)}, u32[]{:S(2)}, u32[]{:S(2)}) collective-permute-start(f32[1,192,128]{2,1,0:T(8,128)S(1)} %maximum_bitcast_fusion.1), channel_id=1, source_target_pairs={{0,16},{2,18},{4,20},{6,22},{8,24},{10,26},{12,28},{14,30},{16,0},... | collective-permute-start | bytes 294920 | tf_op jit(solution)/shard_map/ppermute | solution.py:33
  34.1 7.1 %collective-permute-done.5 = f32[1,192,128]{2,1,0:T(8,128)S(1)} collective-permute-done((f32[1,192,128]{2,1,0:T(8,128)S(1)}, f32[1,192,128]{2,1,0:T(8,128)S(1)}, u32[]{:S(2)}, u32[]{:S(2)}) %collective-permute-start.5) | collective-permute-done | bytes 98336 | tf_op jit(solution)/shard_map/ppermute | solution.py:33
  41.2 1.3 collective-permute-done.6
  42.6 1.6 collective-permute-start.7
  45.4 1.3 collective-permute-start.9
  46.8 5.6 %collective-permute-done.8 = f32[2,192,128]{2,1,0:T(8,128)S(1)} collective-permute-done((f32[2,192,128]{2,1,0:T(8,128)S(1)}, f32[2,192,128]{2,1,0:T(8,128)S(1)}, u32[]{:S(2)}, u32[]{:S(2)}) %collective-permute-start.8) | collective-permute-done | bytes 196640 | tf_op jit(solution)/shard_map/ppermute | solution.py:33
  52.5 2.1 %collective-permute-done.9 = f32[2,192,128]{2,1,0:T(8,128)S(1)} collective-permute-done((f32[2,192,128]{2,1,0:T(8,128)S(1)}, f32[2,192,128]{2,1,0:T(8,128)S(1)}, u32[]{:S(2)}, u32[]{:S(2)}) %collective-permute-start.9) | collective-permute-done | bytes 196640 | tf_op jit(solution)/shard_map/ppermute | solution.py:33
  55.3 6.8 %collective-permute-done.7 = f32[8,200,128]{2,1,0:T(8,128)S(1)} collective-permute-done((f32[8,200,128]{2,1,0:T(8,128)S(1)}, f32[8,200,128]{2,1,0:T(8,128)S(1)}, u32[]{:S(2)}, u32[]{:S(2)}) %collective-permute-start.7) | collective-permute-done | bytes 819232 | tf_op jit(solution)/shard_map/ppermute | solution.py:33
  65.0 1.5 collective-permute-start.16
  66.6 1.6 collective-permute-done.13.b_other
  68.2 10.9 %mix.3.refs_0_ = f32[4,8,256,128]{3,2,1,0:T(8,128)} custom-call(s32[2]{0:T(128)S(1)} %pad_add_fusion.me_ref, f32[16,200,128]{2,1,0:T(8,128)S(1)} %pad_maximum_fusion.a_own, f32[16,200,128]{2,1,0:T(8,128)} %collective-permute-done.10.a_other, f32[16,192,128]{2,1,0:T(8,128)S(1)} %pad_maximum_fusion.1.b_own, f32[16,192,128]{2,1,0:T(8,128)} %collective-permute-done.13.b_other, ...), custom_call_target="tpu_custom_call" | custom-call | flops 4294967296 | bytes 4194304 | tf_op jit(solution)/shard_map/mix/pallas_call | solution.py:386
  79.2 1.6 collective-permute-start.15
  81.4 18.3 %mix.4.refs_1_ = f32[8,8,256,128]{3,2,1,0:T(8,128)} custom-call(s32[2]{0:T(128)S(1)} %pad_add_fusion.me_ref, f32[16,200,128]{2,1,0:T(8,128)S(1)} %pad_maximum_fusion.a_own, f32[16,200,128]{2,1,0:T(8,128)} %collective-permute-done.10.a_other, f32[16,192,128]{2,1,0:T(8,128)S(1)} %pad_maximum_fusion.1.b_own, f32[16,192,128]{2,1,0:T(8,128)} %collective-permute-done.13.b_other, ...), custom_call_target="tpu_custom_call" | custom-call | flops 8589934592 | bytes 8388608 | tf_op jit(solution)/shard_map/mix/pallas_call | solution.py:386
  101.1 10.9 %mix.5.refs_2_ = f32[4,8,256,128]{3,2,1,0:T(8,128)} custom-call(s32[2]{0:T(128)S(1)} %pad_add_fusion.me_ref, f32[16,200,128]{2,1,0:T(8,128)S(1)} %pad_maximum_fusion.a_own, f32[16,200,128]{2,1,0:T(8,128)} %collective-permute-done.10.a_other, f32[16,192,128]{2,1,0:T(8,128)S(1)} %pad_maximum_fusion.1.b_own, f32[16,192,128]{2,1,0:T(8,128)} %collective-permute-done.13.b_other, ...), custom_call_target="tpu_custom_call" | custom-call | flops 4294967296 | bytes 4194304 | tf_op jit(solution)/shard_map/mix/pallas_call | solution.py:386
  112.0 1.2 copy-done.3
  113.1 1.1 copy-done.4
  114.3 18.1 %head.1 = (f32[8,128]{1,0:T(8,128)S(1)}, f32[16,128,128]{2,1,0:T(8,128)S(1)}, f32[16,128,128]{2,1,0:T(8,128)S(1)}) custom-call(s32[2]{0:T(128)S(1)} %pad_add_fusion.me_ref, f32[8]{0:T(128)S(1)} %dynamic_slice.30.target_ref, f32[4,8,256,128]{3,2,1,0:T(8,128)} %mix.3.refs_0_, f32[8,8,256,128]{3,2,1,0:T(8,128)} %mix.4.refs_1_, f32[4,8,256,128]{3,2,1,0:T(8,128)} %mix.5.refs_2_, ...), custom_call_target="tpu_custom_call" | custom-call | tf_op jit(solution)/shard_map/head/pallas_call | solution.py:426
  132.5 2.6 %collective-permute-done.20 = f32[16,128,128]{2,1,0:T(8,128)S(1)} collective-permute-done((f32[16,128,128]{2,1,0:T(8,128)S(1)}, f32[16,128,128]{2,1,0:T(8,128)S(1)}, u32[]{:S(2)}, u32[]{:S(2)}) %collective-permute-start.20) | collective-permute-done | bytes 1048608 | tf_op jit(solution)/shard_map/ppermute | solution.py:33
  135.3 1.1 collective-permute-start.23
  137.1 6.6 %collective-permute-done.23 = f32[512,128]{1,0:T(8,128)S(1)} collective-permute-done((f32[512,128]{1,0:T(8,128)S(1)}, f32[512,128]{1,0:T(8,128)S(1)}, u32[]{:S(2)}, u32[]{:S(2)}) %collective-permute-start.23) | collective-permute-done | bytes 262176 | tf_op jit(solution)/shard_map/ppermute | solution.py:33
  145.9 2.9 %collective-permute-done.24 = f32[256,128]{1,0:T(8,128)S(1)} collective-permute-done((f32[256,128]{1,0:T(8,128)S(1)}, f32[256,128]{1,0:T(8,128)S(1)}, u32[]{:S(2)}, u32[]{:S(2)}) %collective-permute-start.24) | collective-permute-done | bytes 131104 | tf_op jit(solution)/shard_map/ppermute | solution.py:33
  150.0 1.4 collective-permute-start.25
  151.4 3.7 %collective-permute-done.25 = f32[264,128]{1,0:T(8,128)S(1)} collective-permute-done((f32[264,128]{1,0:T(8,128)S(1)}, f32[264,128]{1,0:T(8,128)S(1)}, u32[]{:S(2)}, u32[]{:S(2)}) %collective-permute-start.25) | collective-permute-done | bytes 135200 | tf_op jit(solution)/shard_map/ppermute | solution.py:33
  155.2 2.7 %collective-permute-start.26 = (f32[136,128]{1,0:T(8,128)S(1)}, f32[136,128]{1,0:T(8,128)S(1)}, u32[]{:S(2)}, u32[]{:S(2)}) collective-permute-start(f32[136,128]{1,0:T(8,128)S(1)} %pad_maximum_fusion.14), channel_id=1, source_target_pairs={{0,16},{2,18},{4,20},{6,22},{8,24},{10,26},{12,28},{14,30},{16,0},... | collective-permute-start | bytes 208904 | tf_op jit(solution)/shard_map/ppermute | solution.py:33
  157.9 2.5 %collective-permute-done.26 = f32[136,128]{1,0:T(8,128)S(1)} collective-permute-done((f32[136,128]{1,0:T(8,128)S(1)}, f32[136,128]{1,0:T(8,128)S(1)}, u32[]{:S(2)}, u32[]{:S(2)}) %collective-permute-start.26) | collective-permute-done | bytes 69664 | tf_op jit(solution)/shard_map/ppermute | solution.py:33
  (133 shorter events, 16.3 us)
Async XLA Ops:
  0.6 62.4 %copy-start = (bf16[128,512]{1,0:T(8,128)(2,1)S(1)}, bf16[128,512]{1,0:T(8,128)(2,1)}, u32[]{:S(2)}) copy-start(bf16[128,512]{1,0:T(8,128)(2,1)} %param.12) | copy-start | bytes 393220
  1.4 8.0 %copy-start.11 = (f32[32768]{0:T(1024)S(1)}, f32[32768]{0:T(1024)}, u32[]{:S(2)}) copy-start(f32[32768]{0:T(1024)} %param.19) | copy-start | bytes 393220
  4.8 4.7 %copy-start.12 = (f32[32768]{0:T(1024)S(1)}, f32[32768]{0:T(1024)}, u32[]{:S(2)}) copy-start(f32[32768]{0:T(1024)} %param.15) | copy-start | bytes 393220
  4.8 4.8 %copy-start.13 = (f32[32768]{0:T(1024)S(1)}, f32[32768]{0:T(1024)}, u32[]{:S(2)}) copy-start(f32[32768]{0:T(1024)} %param.16) | copy-start | bytes 393220
  5.2 14.2 %collective-permute-start = (f32[1,200,128]{2,1,0:T(8,128)S(1)}, f32[1,200,128]{2,1,0:T(8,128)S(1)}, u32[]{:S(2)}, u32[]{:S(2)}) collective-permute-start(f32[1,200,128]{2,1,0:T(8,128)S(1)} %maximum_bitcast_fusion), channel_id=1, source_target_pairs={{0,16},{2,18},{4,20},{6,22},{8,24},{10,26},{12,28},{14,30},{16,0},... | collective-permute-start | bytes 307208 | tf_op jit(solution)/shard_map/ppermute | solution.py:33
  9.3 9.3 %collective-permute-start.3 = (f32[1,192,128]{2,1,0:T(8,128)S(1)}, f32[1,192,128]{2,1,0:T(8,128)S(1)}, u32[]{:S(2)}, u32[]{:S(2)}) collective-permute-start(f32[1,192,128]{2,1,0:T(8,128)S(1)} %maximum_bitcast_fusion.2), channel_id=1, source_target_pairs={{0,16},{2,18},{4,20},{6,22},{8,24},{10,26},{12,28},{14,30},{16,0},... | collective-permute-start | bytes 294920 | tf_op jit(solution)/shard_map/ppermute | solution.py:33
  18.6 7.9 %collective-permute-start.4 = (f32[2,192,128]{2,1,0:T(8,128)S(1)}, f32[2,192,128]{2,1,0:T(8,128)S(1)}, u32[]{:S(2)}, u32[]{:S(2)}) collective-permute-start(f32[2,192,128]{2,1,0:T(8,128)S(1)} %pad_maximum_fusion.10), channel_id=1, source_target_pairs={{0,8},{2,10},{4,12},{6,14},{8,0},{10,2},{12,4},{14,6},{16,24},{18,... | collective-permute-start | bytes 589832 | tf_op jit(solution)/shard_map/ppermute | solution.py:33
  19.4 9.7 %collective-permute-start.1 = (f32[2,200,128]{2,1,0:T(8,128)S(1)}, f32[2,200,128]{2,1,0:T(8,128)S(1)}, u32[]{:S(2)}, u32[]{:S(2)}) collective-permute-start(f32[2,200,128]{2,1,0:T(8,128)S(1)} %pad_maximum_fusion.9), channel_id=1, source_target_pairs={{0,8},{2,10},{4,12},{6,14},{8,0},{10,2},{12,4},{14,6},{16,24},{18,... | collective-permute-start | bytes 614408 | tf_op jit(solution)/shard_map/ppermute | solution.py:33
  26.6 17.6 %collective-permute-start.11 = (f32[4,192,128]{2,1,0:T(8,128)S(1)}, f32[4,192,128]{2,1,0:T(8,128)S(1)}, u32[]{:S(2)}, u32[]{:S(2)}) collective-permute-start(f32[4,192,128]{2,1,0:T(8,128)S(1)} %pad_maximum_fusion.7), channel_id=1, source_target_pairs={{0,2},{2,0},{4,6},{6,4},{8,10},{10,8},{12,14},{14,12},{16,18},{18,... | collective-permute-start | bytes 1179656 | tf_op jit(solution)/shard_map/ppermute | solution.py:33
  29.2 13.3 %collective-permute-start.2 = (f32[4,200,128]{2,1,0:T(8,128)S(1)}, f32[4,200,128]{2,1,0:T(8,128)S(1)}, u32[]{:S(2)}, u32[]{:S(2)}) collective-permute-start(f32[4,200,128]{2,1,0:T(8,128)S(1)} %pad_maximum_fusion.6), channel_id=1, source_target_pairs={{0,4},{2,6},{4,0},{6,2},{8,12},{10,14},{12,8},{14,10},{16,20},{18,... | collective-permute-start | bytes 1228808 | tf_op jit(solution)/shard_map/ppermute | solution.py:33
  30.6 10.5 %collective-permute-start.5 = (f32[1,192,128]{2,1,0:T(8,128)S(1)}, f32[1,192,128]{2,1,0:T(8,128)S(1)}, u32[]{:S(2)}, u32[]{:S(2)}) collective-permute-start(f32[1,192,128]{2,1,0:T(8,128)S(1)} %maximum_bitcast_fusion.1), channel_id=1, source_target_pairs={{0,16},{2,18},{4,20},{6,22},{8,24},{10,26},{12,28},{14,30},{16,0},... | collective-permute-start | bytes 294920 | tf_op jit(solution)/shard_map/ppermute | solution.py:33
  34.0 8.5 %collective-permute-start.6 = (f32[1,192,128]{2,1,0:T(8,128)S(1)}, f32[1,192,128]{2,1,0:T(8,128)S(1)}, u32[]{:S(2)}, u32[]{:S(2)}) collective-permute-start(f32[1,192,128]{2,1,0:T(8,128)S(1)} %maximum_bitcast_fusion.3), channel_id=1, source_target_pairs={{0,16},{2,18},{4,20},{6,22},{8,24},{10,26},{12,28},{14,30},{16,0},... | collective-permute-start | bytes 294920 | tf_op jit(solution)/shard_map/ppermute | solution.py:33
  42.6 19.5 %collective-permute-start.7 = (f32[8,200,128]{2,1,0:T(8,128)S(1)}, f32[8,200,128]{2,1,0:T(8,128)S(1)}, u32[]{:S(2)}, u32[]{:S(2)}) collective-permute-start(f32[8,200,128]{2,1,0:T(8,128)S(1)} %pad_maximum_fusion.2), channel_id=1, source_target_pairs={{0,2},{2,0},{4,6},{6,4},{8,10},{10,8},{12,14},{14,12},{16,18},{18,... | collective-permute-start | bytes 2457608 | tf_op jit(solution)/shard_map/ppermute | solution.py:33
  44.2 18.5 %collective-permute-start.12 = (f32[8,192,128]{2,1,0:T(8,128)S(1)}, f32[8,192,128]{2,1,0:T(8,128)S(1)}, u32[]{:S(2)}, u32[]{:S(2)}) collective-permute-start(f32[8,192,128]{2,1,0:T(8,128)S(1)} %pad_maximum_fusion.3), channel_id=1, source_target_pairs={{0,4},{2,6},{4,0},{6,2},{8,12},{10,14},{12,8},{14,10},{16,20},{18,... | collective-permute-start | bytes 2359304 | tf_op jit(solution)/shard_map/ppermute | solution.py:33
  44.8 7.7 %collective-permute-start.8 = (f32[2,192,128]{2,1,0:T(8,128)S(1)}, f32[2,192,128]{2,1,0:T(8,128)S(1)}, u32[]{:S(2)}, u32[]{:S(2)}) collective-permute-start(f32[2,192,128]{2,1,0:T(8,128)S(1)} %get-tuple-element.47), channel_id=1, source_target_pairs={{0,8},{2,10},{4,12},{6,14},{8,0},{10,2},{12,4},{14,6},{16,24},{18,... | collective-permute-start | bytes 589832 | tf_op jit(solution)/shard_map/ppermute | solution.py:33
  45.4 9.1 %collective-permute-start.9 = (f32[2,192,128]{2,1,0:T(8,128)S(1)}, f32[2,192,128]{2,1,0:T(8,128)S(1)}, u32[]{:S(2)}, u32[]{:S(2)}) collective-permute-start(f32[2,192,128]{2,1,0:T(8,128)S(1)} %get-tuple-element.43), channel_id=1, source_target_pairs={{0,8},{2,10},{4,12},{6,14},{8,0},{10,2},{12,4},{14,6},{16,24},{18,... | collective-permute-start | bytes 589832 | tf_op jit(solution)/shard_map/ppermute | solution.py:33
  62.2 6.0 %collective-permute-start.10 = (f32[16,200,128]{2,1,0:T(8,128)S(1)}, f32[16,200,128]{2,1,0:T(8,128)}, u32[]{:S(2)}, u32[]{:S(2)}) collective-permute-start(f32[16,200,128]{2,1,0:T(8,128)S(1)} %pad_maximum_fusion.a_own), channel_id=1, source_target_pairs={{0,1},{1,0},{2,3},{3,2},{4,5},{5,4},{6,7},{7,6},{8,9},{9,8},{10,11... | collective-permute-start | bytes 4915208 | tf_op jit(solution)/shard_map/ppermute | solution.py:33
  62.9 5.3 %collective-permute-start.13 = (f32[16,192,128]{2,1,0:T(8,128)S(1)}, f32[16,192,128]{2,1,0:T(8,128)}, u32[]{:S(2)}, u32[]{:S(2)}) collective-permute-start(f32[16,192,128]{2,1,0:T(8,128)S(1)} %pad_maximum_fusion.1.b_own), channel_id=1, source_target_pairs={{0,1},{1,0},{2,3},{3,2},{4,5},{5,4},{6,7},{7,6},{8,9},{9,8},{10,11... | collective-permute-start | bytes 4718600 | tf_op jit(solution)/shard_map/ppermute | solution.py:33
  64.1 4.1 %copy-start.1 = (bf16[256,512]{1,0:T(8,128)(2,1)S(1)}, bf16[256,512]{1,0:T(8,128)(2,1)}, u32[]{:S(2)}) copy-start(bf16[256,512]{1,0:T(8,128)(2,1)} %constant.50.clone.block_ref) | copy-start | bytes 786436
  64.5 14.6 %collective-permute-start.14 = (f32[4,192,128]{2,1,0:T(8,128)S(1)}, f32[4,192,128]{2,1,0:T(8,128)S(1)}, u32[]{:S(2)}, u32[]{:S(2)}) collective-permute-start(f32[4,192,128]{2,1,0:T(8,128)S(1)} %copy-done.8), channel_id=1, source_target_pairs={{0,4},{2,6},{4,0},{6,2},{8,12},{10,14},{12,8},{14,10},{16,20},{18,... | collective-permute-start | bytes 1179656 | tf_op jit(solution)/shard_map/ppermute | solution.py:33
  65.0 15.7 %collective-permute-start.16 = (f32[4,192,128]{2,1,0:T(8,128)S(1)}, f32[4,192,128]{2,1,0:T(8,128)S(1)}, u32[]{:S(2)}, u32[]{:S(2)}) collective-permute-start(f32[4,192,128]{2,1,0:T(8,128)S(1)} %copy-done.6), channel_id=1, source_target_pairs={{0,2},{2,0},{4,6},{6,4},{8,10},{10,8},{12,14},{14,12},{16,18},{18,... | collective-permute-start | bytes 1179656 | tf_op jit(solution)/shard_map/ppermute | solution.py:33
  79.2 20.6 %collective-permute-start.15 = (f32[8,192,128]{2,1,0:T(8,128)S(1)}, f32[8,192,128]{2,1,0:T(8,128)S(1)}, u32[]{:S(2)}, u32[]{:S(2)}) collective-permute-start(f32[8,192,128]{2,1,0:T(8,128)S(1)} %pad_maximum_fusion.4), channel_id=1, source_target_pairs={{0,2},{2,0},{4,6},{6,4},{8,10},{10,8},{12,14},{14,12},{16,18},{18,... | collective-permute-start | bytes 2359304 | tf_op jit(solution)/shard_map/ppermute | solution.py:33
  80.9 19.4 %collective-permute-start.17 = (f32[8,192,128]{2,1,0:T(8,128)S(1)}, f32[8,192,128]{2,1,0:T(8,128)S(1)}, u32[]{:S(2)}, u32[]{:S(2)}) collective-permute-start(f32[8,192,128]{2,1,0:T(8,128)S(1)} %pad_maximum_fusion.5), channel_id=1, source_target_pairs={{0,4},{2,6},{4,0},{6,2},{8,12},{10,14},{12,8},{14,10},{16,20},{18,... | collective-permute-start | bytes 2359304 | tf_op jit(solution)/shard_map/ppermute | solution.py:33
  100.3 11.7 %collective-permute-start.18 = (f32[16,192,128]{2,1,0:T(8,128)S(1)}, f32[16,192,128]{2,1,0:T(8,128)S(1)}, u32[]{:S(2)}, u32[]{:S(2)}) collective-permute-start(f32[16,192,128]{2,1,0:T(8,128)S(1)} %constant_dynamic-update-slice_fusion.10.refs_3_.refs_4_.refs_5_), channel_id=1, source_target_pairs={{0,1},{1,0},{2,3},{3,2},{4,5},{5,4},{6,7},{7,6},{8,9},{9,8},{10,11... | collective-permute-start | bytes 4718600 | tf_op jit(solution)/shard_map/ppermute | solution.py:33
  100.4 11.5 %collective-permute-start.19 = (f32[16,192,128]{2,1,0:T(8,128)S(1)}, f32[16,192,128]{2,1,0:T(8,128)S(1)}, u32[]{:S(2)}, u32[]{:S(2)}) collective-permute-start(f32[16,192,128]{2,1,0:T(8,128)S(1)} %constant_dynamic-update-slice_fusion.13.refs_6_.refs_7_.refs_8_), channel_id=1, source_target_pairs={{0,1},{1,0},{2,3},{3,2},{4,5},{5,4},{6,7},{7,6},{8,9},{9,8},{10,11... | collective-permute-start | bytes 4718600 | tf_op jit(solution)/shard_map/ppermute | solution.py:33
  132.4 2.7 %collective-permute-start.20 = (f32[16,128,128]{2,1,0:T(8,128)S(1)}, f32[16,128,128]{2,1,0:T(8,128)S(1)}, u32[]{:S(2)}, u32[]{:S(2)}) collective-permute-start(f32[16,128,128]{2,1,0:T(8,128)S(1)} %get-tuple-element.31), channel_id=1, source_target_pairs={{0,1},{1,0},{2,3},{3,2},{4,5},{5,4},{6,7},{7,6},{8,9},{9,8},{10,11... | collective-permute-start | bytes 3145736 | tf_op jit(solution)/shard_map/ppermute | solution.py:33
  135.3 8.4 %collective-permute-start.23 = (f32[512,128]{1,0:T(8,128)S(1)}, f32[512,128]{1,0:T(8,128)S(1)}, u32[]{:S(2)}, u32[]{:S(2)}) collective-permute-start(f32[512,128]{1,0:T(8,128)S(1)} %bitcast.101), channel_id=1, source_target_pairs={{0,4},{2,6},{4,0},{6,2},{8,12},{10,14},{12,8},{14,10},{16,20},{18,... | collective-permute-start | bytes 786440 | tf_op jit(solution)/shard_map/ppermute | solution.py:33
  136.5 8.2 %collective-permute-start.21 = (f32[520,128]{1,0:T(8,128)S(1)}, f32[520,128]{1,0:T(8,128)S(1)}, u32[]{:S(2)}, u32[]{:S(2)}) collective-permute-start(f32[520,128]{1,0:T(8,128)S(1)} %pad_maximum_fusion.8), channel_id=1, source_target_pairs={{0,2},{2,0},{4,6},{6,4},{8,10},{10,8},{12,14},{14,12},{16,18},{18,... | collective-permute-start | bytes 798728 | tf_op jit(solution)/shard_map/ppermute | solution.py:33
  143.8 5.0 %collective-permute-start.24 = (f32[256,128]{1,0:T(8,128)S(1)}, f32[256,128]{1,0:T(8,128)S(1)}, u32[]{:S(2)}, u32[]{:S(2)}) collective-permute-start(f32[256,128]{1,0:T(8,128)S(1)} %bitcast.103), channel_id=1, source_target_pairs={{0,2},{2,0},{4,6},{6,4},{8,10},{10,8},{12,14},{14,12},{16,18},{18,... | collective-permute-start | bytes 393224 | tf_op jit(solution)/shard_map/ppermute | solution.py:33
  144.8 5.1 %collective-permute-start.22 = (f32[264,128]{1,0:T(8,128)S(1)}, f32[264,128]{1,0:T(8,128)S(1)}, u32[]{:S(2)}, u32[]{:S(2)}) collective-permute-start(f32[264,128]{1,0:T(8,128)S(1)} %pad_maximum_fusion.11), channel_id=1, source_target_pairs={{0,4},{2,6},{4,0},{6,2},{8,12},{10,14},{12,8},{14,10},{16,20},{18,... | collective-permute-start | bytes 405512 | tf_op jit(solution)/shard_map/ppermute | solution.py:33
  150.0 5.1 %collective-permute-start.25 = (f32[264,128]{1,0:T(8,128)S(1)}, f32[264,128]{1,0:T(8,128)S(1)}, u32[]{:S(2)}, u32[]{:S(2)}) collective-permute-start(f32[264,128]{1,0:T(8,128)S(1)} %pad_maximum_fusion.12), channel_id=1, source_target_pairs={{0,8},{2,10},{4,12},{6,14},{8,0},{10,2},{12,4},{14,6},{16,24},{18,... | collective-permute-start | bytes 405512 | tf_op jit(solution)/shard_map/ppermute | solution.py:33
  155.2 5.3 %collective-permute-start.26 = (f32[136,128]{1,0:T(8,128)S(1)}, f32[136,128]{1,0:T(8,128)S(1)}, u32[]{:S(2)}, u32[]{:S(2)}) collective-permute-start(f32[136,128]{1,0:T(8,128)S(1)} %pad_maximum_fusion.14), channel_id=1, source_target_pairs={{0,16},{2,18},{4,20},{6,22},{8,24},{10,26},{12,28},{14,30},{16,0},... | collective-permute-start | bytes 208904 | tf_op jit(solution)/shard_map/ppermute | solution.py:33
  (11 other events, 21.6 us)

commit v5 on v4

v5 whole, which is shorter than its diff:
```python
import functools
import math

import jax
import jax.numpy as jnp
import numpy as np
from jax import lax
from jax.experimental import pallas as pl
from jax.experimental.pallas import tpu as pltpu
from jax.sharding import PartitionSpec as P

LANES = 128
CHUNK = 256
BOTH = ("feat", "rows")
MIB = 1024 * 1024
VMEM_MIX = 16 * MIB
VMEM_HEAD = 20 * MIB


def hadamard(length):
    matrix = np.ones((1, 1), np.float32)
    while matrix.shape[0] < length:
        matrix = np.block([[matrix, matrix], [matrix, -matrix]])
    return matrix


def halves(values):
    high = values.astype(jnp.bfloat16)
    low = (values - high.astype(jnp.float32)).astype(jnp.bfloat16)
    return high, low


def swap(values, axis_name, bit):
    size = lax.axis_size(axis_name)
    return lax.ppermute(values, axis_name, [(i, i ^ bit) for i in range(size)])


def bits_of(axis_name):
    return [1 << i for i in reversed(range(lax.axis_size(axis_name).bit_length() - 1))]


def gather_ordered(piece):
    shape = piece.shape
    held = piece[None]
    for axis_name in BOTH:
        index = lax.axis_index(axis_name)
        for bit in bits_of(axis_name):
            other = swap(held, axis_name, bit)
            upper = (index & bit) != 0
            held = jnp.where(
                upper, jnp.stack([other, held], 1), jnp.stack([held, other], 1)
            ).reshape((-1,) + shape)
    return held


def after(value, *others):
    return lax.optimization_barrier((value, *others))[0]


def doubled(held, bit):
    return jnp.concatenate([held, swap(held, "feat", bit)], axis=0)


def place_of(distance, bits):
    place = 0
    for i, bit in enumerate(bits):
        place = place + (((distance >> (bit.bit_length() - 1)) & 1) << i)
    return place


def scatter_sum(keep, send, extra):
    terms = keep + swap(send, "rows", 1)
    bits = bits_of("feat")
    count, lanes = terms.shape[1:]
    terms = terms.reshape((2,) * len(bits) + (count, lanes))
    cut = count // 2
    parts = [terms[..., :cut, :], terms[..., cut:, :]]
    names = [list(bits), list(bits)]

    def exchange(part, left, bit, extra):
        axis = left.index(bit)
        left.remove(bit)
        keep = lax.index_in_dim(part, 0, axis, False)
        send = lax.index_in_dim(part, 1, axis, False).reshape(-1, lanes)
        if extra is None:
            return keep + swap(send, "feat", bit).reshape(keep.shape), None
        got = swap(jnp.concatenate([send, extra], axis=0), "feat", bit)
        return keep + got[: send.shape[0]].reshape(keep.shape), extra + got[send.shape[0] :]

    for bit_a, bit_b in ((1, 2), (2, 1)):
        parts[0], extra = exchange(parts[0], names[0], bit_a, extra)
        parts[1], _ = exchange(parts[1], names[1], bit_b, None)
    rest = jnp.concatenate(parts, axis=-2)
    for bit in list(reversed(names[0])):
        rest, extra = exchange(rest, names[0], bit, extra)
    return rest, extra


def odd_bits(value):
    value = value ^ (value >> 4)
    value = value ^ (value >> 2)
    return (value ^ (value >> 1)) & 1


def mix_kernel(rows, begin, group, bits_a, bits_b, me_ref, a_own, a_other, b_own, b_other, emb_ref, lane_ref, block_ref, out_ref, sign_ref, wide_ref, spread_ref):
    f32 = jnp.float32
    bf16 = jnp.bfloat16
    chunks = a_own.shape[0]
    width = emb_ref.shape[0]
    quarters = width // LANES
    here = LANES // quarters
    def flip(bits):
        return (1 - 2 * (bits & 1)).astype(f32)

    for c, ref in enumerate((a_own, a_other)):
        for p in range(chunks):
            top = (c * chunks + p) * here
            for q in range(quarters):
                sign_ref[top : top + here, q * LANES : (q + 1) * LANES] = ref[
                    p, q * here : (q + 1) * here, :
                ].astype(bf16)
    sums = jnp.dot(jnp.ones((16, sign_ref.shape[0]), bf16), sign_ref[...], preferred_element_type=f32)
    odd = 0.5 * sums - 2.0 * jnp.floor(0.25 * sums)
    row = lax.broadcasted_iota(jnp.int32, odd.shape, 0)
    column = lax.broadcasted_iota(jnp.int32, odd.shape, 1)
    odd = jnp.where((row < 2 * quarters) & ((row & (quarters - 1)) == column // LANES), 0.5 * odd, 0.0)
    rest = jnp.dot(odd.astype(bf16), emb_ref[...], preferred_element_type=f32)
    high = rest.astype(bf16).astype(f32)
    row = lax.broadcasted_iota(jnp.int32, rest.shape, 0)
    wide_ref[0:width, :] = emb_ref[...]
    wide_ref[width:, :] = jnp.zeros((LANES, wide_ref.shape[1]), bf16)
    wide_ref[width : width + 16, :] = jnp.where(row < quarters, high, rest - high).astype(bf16)

    major_me = me_ref[0] * here
    low = here.bit_length() - 1
    half = LANES // 2
    lane = lax.broadcasted_iota(jnp.int32, (CHUNK, LANES), 1)
    @pl.loop(0, out_ref.shape[0] // group)
    def _(step):
        left = []
        orders = []
        gains = []
        for g in range(group):
            chunk = begin + step * group + g
            pa = place_of(chunk, bits_a)
            pb = place_of(chunk, bits_b)
            columns = []
            for ref in (a_own, a_other):
                source = ref[pa, 3 * half : 3 * half + 1, :].astype(jnp.int32)
                major = source >> 2
                code = major & (here - 1)
                for i, bit in enumerate(bits_a):
                    code = code | (((major >> (low + bit.bit_length())) & 1) << (low + i))
                code = code | (((major >> low) & 1) << (low + len(bits_a)))
                code = code | ((source & 3) << 10) | ((lax.population_count(major & major_me) & 1) << 12)
                columns.append(jnp.broadcast_to(code.astype(f32), (LANES, LANES)).T)
            code = jnp.concatenate(columns, axis=0).astype(jnp.int32)
            tiles = [flip(lax.population_count(code & lane))]
            for shift in range(7, 10):
                turn = flip(code >> shift)
                tiles = tiles + [tile * turn for tile in tiles]
            signs = jnp.concatenate([tile.astype(bf16) for tile in tiles], axis=1)
            sums = jnp.dot(signs, sign_ref[...], preferred_element_type=f32)
            flip_me, flip_1, flip_2 = flip(code >> 12), flip(code >> 10), flip(code >> 11)
            turns = [flip_me, flip_me * flip_1, flip_me * flip_2, flip_me * flip_1 * flip_2]
            parts = [
                (jnp.floor(0.25 * sums[:, q * LANES : (q + 1) * LANES]) * turns[q]).astype(bf16) for q in range(4)
            ]
            tail = flip_me * jnp.where((lane & 1) != 0, flip_1, 1.0) * jnp.where((lane & 2) != 0, flip_2, 1.0)
            parts.append(jnp.where(lane < 8, tail, 0.0).astype(bf16))
            left.append(jnp.concatenate(parts, axis=1))
            orders.append(
                jnp.concatenate(
                    [
                        ref[p, LANES : LANES + half, :]
                        for ref, p in ((a_own, pa), (b_own, pb), (a_other, pa), (b_other, pb))
                    ],
                    axis=0,
                ).astype(jnp.int32)
            )
            gains.append(
                jnp.concatenate(
                    [
                        ref[pb, 0:LANES, :] * (1 - 2 * odd_bits((2 * chunk + c) & me_ref[0])).astype(f32)
                        for c, ref in enumerate((b_own, b_other))
                    ],
                    axis=0,
                )
            )
        order = jnp.concatenate(orders, axis=0)
        gain = jnp.concatenate(gains, axis=0)
        first = jnp.dot(jnp.concatenate(left, axis=0), wide_ref[...], preferred_element_type=f32)
        for r in range(rows):
            columns = slice(r * LANES, (r + 1) * LANES)
            mixed = jnp.take_along_axis(first[:, columns], order, axis=1) * gain
            across = jnp.dot(
                jnp.concatenate(halves(mixed), axis=1), lane_ref[...], preferred_element_type=f32
            )
            high, low_part = halves(across)
            for g in range(group):
                here_rows = slice(g * CHUNK, (g + 1) * CHUNK)
                spread_ref[g, 0:CHUNK, columns] = high[here_rows]
                spread_ref[g, CHUNK:, columns] = low_part[here_rows]
        for g in range(group):
            result = jnp.dot(block_ref[...], spread_ref[g], preferred_element_type=f32)
            for r in range(rows):
                out_ref[step * group + g, r] = result[:, r * LANES : (r + 1) * LANES]


def turn_cosine_coefficients(degree):
    points = np.cos(np.pi * (np.arange(400) + 0.5) / 400)
    u = 0.5 * points
    fit = np.polynomial.chebyshev.Chebyshev.fit(u * u, np.cos(2 * np.pi * u), degree, domain=[0, 0.25])
    return [float(c) for c in fit.convert(kind=np.polynomial.Polynomial).coef]


def head_kernel(rows, coefs, grad_scale, bits_a, bits_b, parts, me_ref, target_ref, *refs):
    y_refs, late_refs, refs = refs[:parts], refs[parts : parts + 4], refs[parts + 4 :]
    pred_ref, keep_ref, send_ref, feat_ref, acc_ref, scale_ref = refs
    f32 = jnp.float32
    chunks = feat_ref.shape[0]
    cut = LANES // 2
    acc_ref[...] = jnp.zeros_like(acc_ref)

    for part, late_ref in enumerate(late_refs):
        core, bits = part // 2, (bits_a, bits_b)[part % 2]
        turns_me = [
            (1 - 2 * (odd_bits((2 * k + core) & me_ref[0]) ^ odd_bits(me_ref[0]))).astype(f32)
            for k in range(chunks)
        ]

        @pl.loop(0, cut // 8)
        def _(i):
            row = pl.multiple_of(i * 8, 8)
            here = pl.ds(row + part * cut, 8)
            for k in range(chunks):
                scale_ref[k] = late_ref[place_of(k, bits), pl.ds(row, 8), :] * turns_me[k]
            for r in range(rows):
                values = [y_ref[k, r, here, :] for y_ref in y_refs for k in range(y_ref.shape[0])]
                width = 1
                while width < chunks:
                    for k in range(chunks):
                        if not k & width:
                            a, b = values[k], values[k | width]
                            values[k], values[k | width] = a + b, a - b
                    width *= 2
                acc = acc_ref[r]
                for k in range(chunks):
                    place = place_of(k, bits)
                    turns = values[k] * scale_ref[k] + late_ref[place, pl.ds(row + cut, 8), :]
                    u = turns - jnp.round(turns)
                    square = u * u
                    cosine = jnp.full_like(square, coefs[-1])
                    for c in coefs[-2::-1]:
                        cosine = cosine * square + c
                    feat_ref[k, r, here, :] = cosine
                    acc = acc + cosine * late_ref[place, pl.ds(row + 2 * cut, 8), :]
                acc_ref[r] = acc

    residuals = []
    lane = lax.broadcasted_iota(jnp.int32, (1, LANES), 1)
    found = jnp.zeros((1, LANES), f32)
    for r in range(rows):
        total = jnp.sum(jnp.sum(acc_ref[r], axis=0, keepdims=True), axis=1, keepdims=True)
        found = found + jnp.where(lane == me_ref[1] + r, total, 0.0)
        residuals.append(jnp.broadcast_to((total - target_ref[r]) * grad_scale, (8, LANES)))
    pred_ref[...] = jnp.broadcast_to(found, (8, LANES))

    for half, out_ref in enumerate((keep_ref, send_ref)):

        @pl.loop(0, LANES // 8)
        def _(i):
            row = pl.multiple_of(i * 8, 8)
            rows_here = pl.ds(row + half * LANES, 8)
            for k in range(chunks):
                total = feat_ref[k, 0, rows_here, :] * residuals[0]
                for r in range(1, rows):
                    total = total + feat_ref[k, r, rows_here, :] * residuals[r]
                out_ref[k, pl.ds(row, 8), :] = total


def local(
    embeddings,
    sign_flips,
    gaussian,
    scales,
    phases,
    source_blocks,
    block_permutations,
    weights,
    targets,
):
    f32 = jnp.float32
    feat_size = lax.axis_size("feat")
    rows_size = lax.axis_size("rows")
    place = lax.axis_index("feat")
    core = lax.axis_index("rows")
    devices = feat_size * rows_size
    width = embeddings.shape[1]
    rows = embeddings.shape[0] // feat_size
    total_rows = embeddings.shape[0] * rows_size
    features = sign_flips.shape[0] * feat_size
    blocks = features // LANES
    mine = blocks // devices
    quarters = width // LANES
    chunks = blocks // CHUNK
    per_chunk = CHUNK // mine

    def half(values):
        parts = values.reshape((rows_size, values.shape[0] // rows_size) + values.shape[1:])
        return lax.dynamic_index_in_dim(parts, core, 0, False)

    def rows_of(*vectors):
        return jnp.concatenate([half(v) for v in vectors]).reshape(len(vectors), mine, LANES)

    positions = jnp.einsum(
        "bij,j->bi", half(block_permutations), jnp.arange(LANES).astype(jnp.bfloat16), preferred_element_type=f32
    )
    signs, gains = rows_of(sign_flips, gaussian)
    numbers = half(source_blocks).astype(f32)
    late = rows_of(
        scales * f32(4.0 / (2.0 * math.pi * features)),
        phases * f32(1.0 / (2.0 * math.pi)),
        weights * f32(1.0 / math.sqrt(features)),
    )
    bits = bits_of("feat")
    numbers = jnp.broadcast_to(jnp.pad(numbers, (0, LANES - mine))[None, :], (8, LANES))
    everything = [signs, positions, gains, *late, numbers]
    direct = mine == LANES and feat_size == chunks and rows_size == 2
    if direct:
        me = place * rows_size + core
        bits_a = bits[:-2] + [2, 1]
        bits_b = bits[:-2] + [1, 2]
    else:
        me = 0
        bits_a = bits_b = [1 << i for i in range(chunks.bit_length() - 1)]
        whole = gather_ordered(jnp.concatenate(everything))
        numbers = whole[:, 6 * mine, :mine].reshape(chunks, 2, 1, LANES)
        numbers = jnp.broadcast_to(numbers, (chunks, 2, 8, LANES))
        everything = [whole[:, i * mine : (i + 1) * mine].reshape(chunks, 2, LANES, LANES) for i in range(6)]
        everything.append(numbers)
    signs, positions, gains, *late, numbers = everything

    per_half = LANES // quarters
    shape = signs.shape
    signs = jnp.swapaxes(signs.reshape(shape[:-2] + (per_half, quarters, LANES)), -3, -2).reshape(shape)
    cut = LANES // 2
    pieces = [
        jnp.concatenate([signs, positions[..., :cut, :], numbers], axis=-2),
        jnp.concatenate([gains, positions[..., cut:, :]], axis=-2),
        jnp.concatenate([x[..., :cut, :] for x in late], axis=-2),
        jnp.concatenate([x[..., cut:, :] for x in late], axis=-2),
    ]
    if direct:
        early = [x[None] for x in pieces[:2]]
        late = [x[None] for x in pieces[2:]]
        for i in range(len(bits)):
            if i == len(bits) - 2:
                late = [after(x, *early) for x in late]
            if i >= len(bits) - 2:
                late = [doubled(x, bits[i + 2 - len(bits)]) for x in late]
            early = [doubled(x, b[i]) for x, b in zip(early, (bits_a, bits_b))]
            if i >= len(bits) - 2:
                early = [after(x, *late) for x in early]
        for i in range(2, len(bits) - 2):
            late = [doubled(x, bits[i]) for x in late]
        late = [after(x, *early) for x in late]
        late_got = [swap(x, "feat", b[-2]) for x, b in zip(late, (bits_a, bits_b))]
        a_pair, b_pair = ((x, swap(x, "rows", 1)) for x in early)
    else:
        a_pair, b_pair, c_pair, d_pair = ((x[:, 0], x[:, 1]) for x in pieces)

    emb = lax.dynamic_slice_in_dim(embeddings, place * rows, rows, 0)
    lane_signs = hadamard(LANES)
    emb = (emb.T.reshape(quarters, LANES, rows, 1) * jnp.asarray(lane_signs, jnp.bfloat16)[None, :, None, :]).reshape(
        width, rows * LANES
    )
    lane_matrix = jnp.asarray(np.concatenate([lane_signs] * 2, 0), jnp.bfloat16)
    block_matrix = jnp.asarray(np.concatenate([hadamard(CHUNK)] * 2, 1), jnp.bfloat16)
    about_me = jnp.stack([jnp.asarray(me, jnp.int32), (place * rows).astype(jnp.int32)])

    scalars = pl.BlockSpec(memory_space=pltpu.SMEM)
    vmem = pl.BlockSpec(memory_space=pltpu.VMEM)
    resident_args = (*a_pair, *b_pair, emb, lane_matrix, block_matrix)

    def mix(begin, count, group=2):
        return pl.pallas_call(
            functools.partial(mix_kernel, rows, begin, group, bits_a, bits_b),
            in_specs=[scalars] + [vmem] * len(resident_args),
            out_specs=vmem,
            out_shape=jax.ShapeDtypeStruct((count, rows, CHUNK, LANES), f32),
            scratch_shapes=[
                pltpu.VMEM((blocks // quarters, width), jnp.bfloat16),
                pltpu.VMEM((width + LANES, rows * LANES), jnp.bfloat16),
                pltpu.VMEM((group, 2 * CHUNK, rows * LANES), jnp.bfloat16),
            ],
            compiler_params=pltpu.CompilerParams(vmem_limit_bytes=VMEM_MIX),
            cost_estimate=pl.CostEstimate(
                flops=count * 2 * 256 * 8192 * 256, bytes_accessed=count * rows * CHUNK * LANES * 4, transcendentals=0
            ),
            name="mix",
        )(about_me, *resident_args)

    cuts = (0, chunks // 4, chunks * 3 // 4, chunks)
    spread = [mix(cuts[0], cuts[1] - cuts[0])]
    if direct:
        late = [jnp.concatenate([x, after(y, spread[0])], axis=0) for x, y in zip(late, late_got)]
        late_got = [swap(x, "feat", b[-1]) for x, b in zip(late, (bits_a, bits_b))]
    spread.append(mix(cuts[1], cuts[2] - cuts[1]))
    if direct:
        late = [jnp.concatenate([x, after(y, spread[1])], axis=0) for x, y in zip(late, late_got)]
        c_pair, d_pair = ((x, swap(x, "rows", 1)) for x in late)
    spread.append(mix(cuts[2], cuts[3] - cuts[2]))

    my_targets = lax.dynamic_slice_in_dim(targets, place * rows, rows, 0)
    found, keep, send = pl.pallas_call(
        functools.partial(
            head_kernel, rows, turn_cosine_coefficients(5), 1.0 / math.sqrt(total_rows), bits_a, bits_b, len(spread)
        ),
        in_specs=[scalars, scalars] + [vmem] * (len(spread) + 4),
        out_specs=[vmem] * 3,
        out_shape=[
            jax.ShapeDtypeStruct((8, LANES), f32),
            jax.ShapeDtypeStruct((chunks, LANES, LANES), f32),
            jax.ShapeDtypeStruct((chunks, LANES, LANES), f32),
        ],
        scratch_shapes=[
            pltpu.VMEM((chunks, rows, CHUNK, LANES), f32),
            pltpu.VMEM((rows, 8, LANES), f32),
            pltpu.VMEM((chunks, 8, LANES), f32),
        ],
        compiler_params=pltpu.CompilerParams(vmem_limit_bytes=VMEM_HEAD),
        name="head",
    )(about_me, my_targets, *spread, c_pair[0], d_pair[0], c_pair[1], d_pair[1])

    if not direct:
        grads = jnp.stack([keep, send], 1).reshape(feat_size, rows_size, mine, LANES)
        grads = jnp.take(grads, jnp.arange(feat_size) ^ place, axis=0)
        keep = lax.dynamic_index_in_dim(grads, core, 1, False)
        send = lax.dynamic_index_in_dim(grads, core ^ 1, 1, False)
    feature_grad, found = scatter_sum(keep, send, found)
    return found[0], feature_grad.reshape(-1)


def solution(mesh):
    in_specs = (
        P("rows", None),
        P("feat"),
        P("feat"),
        P("feat"),
        P("feat"),
        P("feat"),
        P("feat", None, None),
        P("feat"),
        P("rows"),
    )
    out_specs = (P("rows"), P(("feat", "rows")))
    return jax.shard_map(local, mesh=mesh, in_specs=in_specs, out_specs=out_specs, check_vma=False)
```

time: 162 us -> 152 us (0.938)
  Pallas kernels: 58.3 us -> 47 us
  waiting for transfers between devices: 60.4 us -> 64 us
  local copies, waits for them, and re-layouts: 5.51 us -> 3.21 us
    pallas_call x4, Pallas kernels: 58.3 us -> 47 us  [the longest x3 31.5 us: mix(): pl.pallas_call(functools.partial(mix_kernel, rows, begin, group, bits_a,...]
    ppermute x27, waiting for transfers between devices: 60.4 us -> 64 us  [swap(): return lax.ppermute(values, axis_name, [(i, i ^ bit) for i in range(size)])]
    unnamed x41 -> x37, local copies, waits for them, and re-layouts: 3.55 us -> 1.25 us
  transfers between devices with their start and end apart: 27 -> 27, of which waited for: 18 -> 18; matrix products, arithmetic and copies ran while one was open for 2% -> 2% of each run, Pallas kernels for 25% -> 21%
where the time goes in v5:
time: 152 us
  waiting for transfers between devices  64 us (42%)
  Pallas kernels  47 us (31%)
  starting transfers between devices  29.3 us (19%)
  matrix products  3.42 us (2%)
  other arithmetic  3.35 us (2%)
  local copies, waits for them, and re-layouts  3.21 us (2%)
    ppermute x27, waiting for transfers between devices, swap(): return lax.ppermute(values, axis_name, [(i, i ^ bit) for i in range(size)])  64 us
    pallas_call x3, Pallas kernels, mix(): pl.pallas_call(functools.partial(mix_kernel, rows, begin, group, bits_a,...  31.5 us
    ppermute x27, starting transfers between devices, swap(): return lax.ppermute(values, axis_name, [(i, i ^ bit) for i in range(size)])  29.3 us
    pallas_call x1, Pallas kernels, local(): pl.pallas_call(functools.partial(head_kernel, rows, turn_cosine_coefficie...  15.5 us
    dot_general x1, matrix products, local(): jnp.einsum('bij,j->bi', half(block_permutations), jnp.arange(LANES).astyp...  3.42 us
  transfers between devices with their start and end apart: 27, of which 18 were waited for; matrix products, arithmetic and copies ran while one was open for 2% of the time, Pallas kernels for 21%

profile of v5, /device:TPU:0, one launch (start us, length us, event | category | flops | bytes accessed | tf_op | source)
XLA Modules:
  0.0 151.6 jit_solution(13375038444809150854)
XLA Ops:
  1.4 3.4 %fusion = f32[1,128,128]{2,0,1:T(1,128)S(1)} fusion(bf16[2,128,128,128]{3,2,1,0:T(8,128)(2,1)} %bitcast.89, s32[]{:T(128)S(6)} %select_n.17), kind=kOutput, calls=%fused_computation | convolution fusion | flops 4194432 | bytes 4259844 | tf_op jit(solution)/shard_map/bij,j->bi/dot_general | solution.py:316
  5.2 4.1 %collective-permute-start = (f32[1,200,128]{2,1,0:T(8,128)S(1)}, f32[1,200,128]{2,1,0:T(8,128)S(1)}, u32[]{:S(2)}, u32[]{:S(2)}) collective-permute-start(f32[1,200,128]{2,1,0:T(8,128)S(1)} %maximum_bitcast_fusion), channel_id=1, source_target_pairs={{0,16},{2,18},{4,20},{6,22},{8,24},{10,26},{12,28},{14,30},{16,0},... | collective-permute-start | bytes 307208 | tf_op jit(solution)/shard_map/ppermute | solution.py:35
  10.1 8.5 %collective-permute-done.3 = f32[1,192,128]{2,1,0:T(8,128)S(1)} collective-permute-done((f32[1,192,128]{2,1,0:T(8,128)S(1)}, f32[1,192,128]{2,1,0:T(8,128)S(1)}, u32[]{:S(2)}, u32[]{:S(2)}) %collective-permute-start.3) | collective-permute-done | bytes 98336 | tf_op jit(solution)/shard_map/ppermute | solution.py:35
  19.4 1.4 collective-permute-start.1
  20.8 5.7 %collective-permute-done.4 = f32[2,192,128]{2,1,0:T(8,128)S(1)} collective-permute-done((f32[2,192,128]{2,1,0:T(8,128)S(1)}, f32[2,192,128]{2,1,0:T(8,128)S(1)}, u32[]{:S(2)}, u32[]{:S(2)}) %collective-permute-start.4) | collective-permute-done | bytes 196640 | tf_op jit(solution)/shard_map/ppermute | solution.py:35
  26.6 1.6 %collective-permute-start.11 = (f32[4,192,128]{2,1,0:T(8,128)S(1)}, f32[4,192,128]{2,1,0:T(8,128)S(1)}, u32[]{:S(2)}, u32[]{:S(2)}) collective-permute-start(f32[4,192,128]{2,1,0:T(8,128)S(1)} %pad_maximum_fusion.7), channel_id=1, source_target_pairs={{0,2},{2,0},{4,6},{6,4},{8,10},{10,8},{12,14},{14,12},{16,18},{18,... | collective-permute-start | bytes 1179656 | tf_op jit(solution)/shard_map/ppermute | solution.py:35
  29.2 1.4 collective-permute-start.2
  30.6 3.4 %collective-permute-start.5 = (f32[1,192,128]{2,1,0:T(8,128)S(1)}, f32[1,192,128]{2,1,0:T(8,128)S(1)}, u32[]{:S(2)}, u32[]{:S(2)}) collective-permute-start(f32[1,192,128]{2,1,0:T(8,128)S(1)} %maximum_bitcast_fusion.1), channel_id=1, source_target_pairs={{0,16},{2,18},{4,20},{6,22},{8,24},{10,26},{12,28},{14,30},{16,0},... | collective-permute-start | bytes 294920 | tf_op jit(solution)/shard_map/ppermute | solution.py:35
  34.1 7.1 %collective-permute-done.5 = f32[1,192,128]{2,1,0:T(8,128)S(1)} collective-permute-done((f32[1,192,128]{2,1,0:T(8,128)S(1)}, f32[1,192,128]{2,1,0:T(8,128)S(1)}, u32[]{:S(2)}, u32[]{:S(2)}) %collective-permute-start.5) | collective-permute-done | bytes 98336 | tf_op jit(solution)/shard_map/ppermute | solution.py:35
  41.2 1.3 collective-permute-done.6
  42.6 1.6 %collective-permute-start.7 = (f32[8,200,128]{2,1,0:T(8,128)S(1)}, f32[8,200,128]{2,1,0:T(8,128)S(1)}, u32[]{:S(2)}, u32[]{:S(2)}) collective-permute-start(f32[8,200,128]{2,1,0:T(8,128)S(1)} %pad_maximum_fusion.2), channel_id=1, source_target_pairs={{0,2},{2,0},{4,6},{6,4},{8,10},{10,8},{12,14},{14,12},{16,18},{18,... | collective-permute-start | bytes 2457608 | tf_op jit(solution)/shard_map/ppermute | solution.py:35
  45.4 1.3 collective-permute-start.9
  46.8 5.6 %collective-permute-done.8 = f32[2,192,128]{2,1,0:T(8,128)S(1)} collective-permute-done((f32[2,192,128]{2,1,0:T(8,128)S(1)}, f32[2,192,128]{2,1,0:T(8,128)S(1)}, u32[]{:S(2)}, u32[]{:S(2)}) %collective-permute-start.8) | collective-permute-done | bytes 196640 | tf_op jit(solution)/shard_map/ppermute | solution.py:35
  52.5 2.1 %collective-permute-done.9 = f32[2,192,128]{2,1,0:T(8,128)S(1)} collective-permute-done((f32[2,192,128]{2,1,0:T(8,128)S(1)}, f32[2,192,128]{2,1,0:T(8,128)S(1)}, u32[]{:S(2)}, u32[]{:S(2)}) %collective-permute-start.9) | collective-permute-done | bytes 196640 | tf_op jit(solution)/shard_map/ppermute | solution.py:35
  55.3 6.8 %collective-permute-done.7 = f32[8,200,128]{2,1,0:T(8,128)S(1)} collective-permute-done((f32[8,200,128]{2,1,0:T(8,128)S(1)}, f32[8,200,128]{2,1,0:T(8,128)S(1)}, u32[]{:S(2)}, u32[]{:S(2)}) %collective-permute-start.7) | collective-permute-done | bytes 819232 | tf_op jit(solution)/shard_map/ppermute | solution.py:35
  65.0 1.5 collective-permute-start.16
  66.6 1.6 %collective-permute-done.13.b_other = f32[16,192,128]{2,1,0:T(8,128)} collective-permute-done((f32[16,192,128]{2,1,0:T(8,128)S(1)}, f32[16,192,128]{2,1,0:T(8,128)}, u32[]{:S(2)}, u32[]{:S(2)}) %collective-permute-start.13) | collective-permute-done | bytes 1572896 | tf_op jit(solution)/shard_map/ppermute | solution.py:35
  68.2 8.5 %mix.3.refs_0_ = f32[4,8,256,128]{3,2,1,0:T(8,128)S(1)} custom-call(s32[2]{0:T(128)S(1)} %pad_add_fusion.me_ref, f32[16,200,128]{2,1,0:T(8,128)S(1)} %pad_maximum_fusion.a_own, f32[16,200,128]{2,1,0:T(8,128)} %collective-permute-done.10.a_other, f32[16,192,128]{2,1,0:T(8,128)S(1)} %pad_maximum_fusion.1.b_own, ...), custom_call_target="tpu_custom_call" | custom-call | flops 4294967296 | bytes 4194304 | tf_op jit(solution)/shard_map/mix/pallas_call | solution.py:387
  76.8 1.6 %collective-permute-start.15 = (f32[8,192,128]{2,1,0:T(8,128)S(1)}, f32[8,192,128]{2,1,0:T(8,128)S(1)}, u32[]{:S(2)}, u32[]{:S(2)}) collective-permute-start(f32[8,192,128]{2,1,0:T(8,128)S(1)} %pad_maximum_fusion.4), channel_id=1, source_target_pairs={{0,2},{2,0},{4,6},{6,4},{8,10},{10,8},{12,14},{14,12},{16,18},{18,... | collective-permute-start | bytes 2359304 | tf_op jit(solution)/shard_map/ppermute | solution.py:35
  79.0 14.5 %mix.4.refs_1_ = f32[8,8,256,128]{3,2,1,0:T(8,128)S(1)} custom-call(s32[2]{0:T(128)S(1)} %pad_add_fusion.me_ref, f32[16,200,128]{2,1,0:T(8,128)S(1)} %pad_maximum_fusion.a_own, f32[16,200,128]{2,1,0:T(8,128)} %collective-permute-done.10.a_other, f32[16,192,128]{2,1,0:T(8,128)S(1)} %pad_maximum_fusion.1.b_own, ...), custom_call_target="tpu_custom_call" | custom-call | flops 8589934592 | bytes 8388608 | tf_op jit(solution)/shard_map/mix/pallas_call | solution.py:387
  93.6 2.8 %collective-permute-done.15 = f32[8,192,128]{2,1,0:T(8,128)S(1)} collective-permute-done((f32[8,192,128]{2,1,0:T(8,128)S(1)}, f32[8,192,128]{2,1,0:T(8,128)S(1)}, u32[]{:S(2)}, u32[]{:S(2)}) %collective-permute-start.15) | collective-permute-done | bytes 786464 | tf_op jit(solution)/shard_map/ppermute | solution.py:35
  96.4 1.4 collective-permute-done.17
  98.7 8.5 %mix.5.refs_2_ = f32[4,8,256,128]{3,2,1,0:T(8,128)S(1)} custom-call(s32[2]{0:T(128)S(1)} %pad_add_fusion.me_ref, f32[16,200,128]{2,1,0:T(8,128)S(1)} %pad_maximum_fusion.a_own, f32[16,200,128]{2,1,0:T(8,128)} %collective-permute-done.10.a_other, f32[16,192,128]{2,1,0:T(8,128)S(1)} %pad_maximum_fusion.1.b_own, ...), custom_call_target="tpu_custom_call" | custom-call | flops 4294967296 | bytes 4194304 | tf_op jit(solution)/shard_map/mix/pallas_call | solution.py:387
  107.2 15.5 %head.1 = (f32[8,128]{1,0:T(8,128)S(1)}, f32[16,128,128]{2,1,0:T(8,128)S(1)}, f32[16,128,128]{2,1,0:T(8,128)S(1)}) custom-call(s32[2]{0:T(128)S(1)} %pad_add_fusion.me_ref, f32[8]{0:T(128)S(1)} %dynamic_slice.30.target_ref, f32[4,8,256,128]{3,2,1,0:T(8,128)S(1)} %mix.3.refs_0_, f32[8,8,256,128]{3,2,1,0:T(8,128)S(1)} %mix.4.refs_1_, ...), custom_call_target="tpu_custom_call" | custom-call | tf_op jit(solution)/shard_map/head/pallas_call | solution.py:416
  122.8 2.6 %collective-permute-done.20 = f32[16,128,128]{2,1,0:T(8,128)S(1)} collective-permute-done((f32[16,128,128]{2,1,0:T(8,128)S(1)}, f32[16,128,128]{2,1,0:T(8,128)S(1)}, u32[]{:S(2)}, u32[]{:S(2)}) %collective-permute-start.20) | collective-permute-done | bytes 1048608 | tf_op jit(solution)/shard_map/ppermute | solution.py:35
  126.9 7.2 %collective-permute-done.23 = f32[512,128]{1,0:T(8,128)S(1)} collective-permute-done((f32[512,128]{1,0:T(8,128)S(1)}, f32[512,128]{1,0:T(8,128)S(1)}, u32[]{:S(2)}, u32[]{:S(2)}) %collective-permute-start.23) | collective-permute-done | bytes 262176 | tf_op jit(solution)/shard_map/ppermute | solution.py:35
  134.8 1.4 collective-permute-start.22
  136.2 2.9 %collective-permute-done.24 = f32[256,128]{1,0:T(8,128)S(1)} collective-permute-done((f32[256,128]{1,0:T(8,128)S(1)}, f32[256,128]{1,0:T(8,128)S(1)}, u32[]{:S(2)}, u32[]{:S(2)}) %collective-permute-start.24) | collective-permute-done | bytes 131104 | tf_op jit(solution)/shard_map/ppermute | solution.py:35
  140.0 1.4 collective-permute-start.25
  141.4 3.7 %collective-permute-done.25 = f32[264,128]{1,0:T(8,128)S(1)} collective-permute-done((f32[264,128]{1,0:T(8,128)S(1)}, f32[264,128]{1,0:T(8,128)S(1)}, u32[]{:S(2)}, u32[]{:S(2)}) %collective-permute-start.25) | collective-permute-done | bytes 135200 | tf_op jit(solution)/shard_map/ppermute | solution.py:35
  145.1 2.8 %collective-permute-start.26 = (f32[136,128]{1,0:T(8,128)S(1)}, f32[136,128]{1,0:T(8,128)S(1)}, u32[]{:S(2)}, u32[]{:S(2)}) collective-permute-start(f32[136,128]{1,0:T(8,128)S(1)} %pad_maximum_fusion.14), channel_id=1, source_target_pairs={{0,16},{2,18},{4,20},{6,22},{8,24},{10,26},{12,28},{14,30},{16,0},... | collective-permute-start | bytes 208904 | tf_op jit(solution)/shard_map/ppermute | solution.py:35
  147.9 2.5 %collective-permute-done.26 = f32[136,128]{1,0:T(8,128)S(1)} collective-permute-done((f32[136,128]{1,0:T(8,128)S(1)}, f32[136,128]{1,0:T(8,128)S(1)}, u32[]{:S(2)}, u32[]{:S(2)}) %collective-permute-start.26) | collective-permute-done | bytes 69664 | tf_op jit(solution)/shard_map/ppermute | solution.py:35
  (129 shorter events, 14.8 us)
Async XLA Ops:
  0.6 62.4 %copy-start = (bf16[128,512]{1,0:T(8,128)(2,1)S(1)}, bf16[128,512]{1,0:T(8,128)(2,1)}, u32[]{:S(2)}) copy-start(bf16[128,512]{1,0:T(8,128)(2,1)} %param.12) | copy-start | bytes 393220
  1.4 8.0 %copy-start.9 = (f32[32768]{0:T(1024)S(1)}, f32[32768]{0:T(1024)}, u32[]{:S(2)}) copy-start(f32[32768]{0:T(1024)} %param.19) | copy-start | bytes 393220
  4.8 4.7 %copy-start.10 = (f32[32768]{0:T(1024)S(1)}, f32[32768]{0:T(1024)}, u32[]{:S(2)}) copy-start(f32[32768]{0:T(1024)} %param.15) | copy-start | bytes 393220
  4.8 4.8 %copy-start.11 = (f32[32768]{0:T(1024)S(1)}, f32[32768]{0:T(1024)}, u32[]{:S(2)}) copy-start(f32[32768]{0:T(1024)} %param.16) | copy-start | bytes 393220
  5.2 14.2 %collective-permute-start = (f32[1,200,128]{2,1,0:T(8,128)S(1)}, f32[1,200,128]{2,1,0:T(8,128)S(1)}, u32[]{:S(2)}, u32[]{:S(2)}) collective-permute-start(f32[1,200,128]{2,1,0:T(8,128)S(1)} %maximum_bitcast_fusion), channel_id=1, source_target_pairs={{0,16},{2,18},{4,20},{6,22},{8,24},{10,26},{12,28},{14,30},{16,0},... | collective-permute-start | bytes 307208 | tf_op jit(solution)/shard_map/ppermute | solution.py:35
  9.3 9.3 %collective-permute-start.3 = (f32[1,192,128]{2,1,0:T(8,128)S(1)}, f32[1,192,128]{2,1,0:T(8,128)S(1)}, u32[]{:S(2)}, u32[]{:S(2)}) collective-permute-start(f32[1,192,128]{2,1,0:T(8,128)S(1)} %maximum_bitcast_fusion.2), channel_id=1, source_target_pairs={{0,16},{2,18},{4,20},{6,22},{8,24},{10,26},{12,28},{14,30},{16,0},... | collective-permute-start | bytes 294920 | tf_op jit(solution)/shard_map/ppermute | solution.py:35
  18.6 7.9 %collective-permute-start.4 = (f32[2,192,128]{2,1,0:T(8,128)S(1)}, f32[2,192,128]{2,1,0:T(8,128)S(1)}, u32[]{:S(2)}, u32[]{:S(2)}) collective-permute-start(f32[2,192,128]{2,1,0:T(8,128)S(1)} %pad_maximum_fusion.10), channel_id=1, source_target_pairs={{0,8},{2,10},{4,12},{6,14},{8,0},{10,2},{12,4},{14,6},{16,24},{18,... | collective-permute-start | bytes 589832 | tf_op jit(solution)/shard_map/ppermute | solution.py:35
  19.4 9.7 %collective-permute-start.1 = (f32[2,200,128]{2,1,0:T(8,128)S(1)}, f32[2,200,128]{2,1,0:T(8,128)S(1)}, u32[]{:S(2)}, u32[]{:S(2)}) collective-permute-start(f32[2,200,128]{2,1,0:T(8,128)S(1)} %pad_maximum_fusion.9), channel_id=1, source_target_pairs={{0,8},{2,10},{4,12},{6,14},{8,0},{10,2},{12,4},{14,6},{16,24},{18,... | collective-permute-start | bytes 614408 | tf_op jit(solution)/shard_map/ppermute | solution.py:35
  26.6 17.6 %collective-permute-start.11 = (f32[4,192,128]{2,1,0:T(8,128)S(1)}, f32[4,192,128]{2,1,0:T(8,128)S(1)}, u32[]{:S(2)}, u32[]{:S(2)}) collective-permute-start(f32[4,192,128]{2,1,0:T(8,128)S(1)} %pad_maximum_fusion.7), channel_id=1, source_target_pairs={{0,2},{2,0},{4,6},{6,4},{8,10},{10,8},{12,14},{14,12},{16,18},{18,... | collective-permute-start | bytes 1179656 | tf_op jit(solution)/shard_map/ppermute | solution.py:35
  29.2 13.3 %collective-permute-start.2 = (f32[4,200,128]{2,1,0:T(8,128)S(1)}, f32[4,200,128]{2,1,0:T(8,128)S(1)}, u32[]{:S(2)}, u32[]{:S(2)}) collective-permute-start(f32[4,200,128]{2,1,0:T(8,128)S(1)} %pad_maximum_fusion.6), channel_id=1, source_target_pairs={{0,4},{2,6},{4,0},{6,2},{8,12},{10,14},{12,8},{14,10},{16,20},{18,... | collective-permute-start | bytes 1228808 | tf_op jit(solution)/shard_map/ppermute | solution.py:35
  30.6 10.5 %collective-permute-start.5 = (f32[1,192,128]{2,1,0:T(8,128)S(1)}, f32[1,192,128]{2,1,0:T(8,128)S(1)}, u32[]{:S(2)}, u32[]{:S(2)}) collective-permute-start(f32[1,192,128]{2,1,0:T(8,128)S(1)} %maximum_bitcast_fusion.1), channel_id=1, source_target_pairs={{0,16},{2,18},{4,20},{6,22},{8,24},{10,26},{12,28},{14,30},{16,0},... | collective-permute-start | bytes 294920 | tf_op jit(solution)/shard_map/ppermute | solution.py:35
  34.0 8.5 %collective-permute-start.6 = (f32[1,192,128]{2,1,0:T(8,128)S(1)}, f32[1,192,128]{2,1,0:T(8,128)S(1)}, u32[]{:S(2)}, u32[]{:S(2)}) collective-permute-start(f32[1,192,128]{2,1,0:T(8,128)S(1)} %maximum_bitcast_fusion.3), channel_id=1, source_target_pairs={{0,16},{2,18},{4,20},{6,22},{8,24},{10,26},{12,28},{14,30},{16,0},... | collective-permute-start | bytes 294920 | tf_op jit(solution)/shard_map/ppermute | solution.py:35
  42.6 19.5 %collective-permute-start.7 = (f32[8,200,128]{2,1,0:T(8,128)S(1)}, f32[8,200,128]{2,1,0:T(8,128)S(1)}, u32[]{:S(2)}, u32[]{:S(2)}) collective-permute-start(f32[8,200,128]{2,1,0:T(8,128)S(1)} %pad_maximum_fusion.2), channel_id=1, source_target_pairs={{0,2},{2,0},{4,6},{6,4},{8,10},{10,8},{12,14},{14,12},{16,18},{18,... | collective-permute-start | bytes 2457608 | tf_op jit(solution)/shard_map/ppermute | solution.py:35
  44.2 18.5 %collective-permute-start.12 = (f32[8,192,128]{2,1,0:T(8,128)S(1)}, f32[8,192,128]{2,1,0:T(8,128)S(1)}, u32[]{:S(2)}, u32[]{:S(2)}) collective-permute-start(f32[8,192,128]{2,1,0:T(8,128)S(1)} %pad_maximum_fusion.3), channel_id=1, source_target_pairs={{0,4},{2,6},{4,0},{6,2},{8,12},{10,14},{12,8},{14,10},{16,20},{18,... | collective-permute-start | bytes 2359304 | tf_op jit(solution)/shard_map/ppermute | solution.py:35
  44.8 7.7 %collective-permute-start.8 = (f32[2,192,128]{2,1,0:T(8,128)S(1)}, f32[2,192,128]{2,1,0:T(8,128)S(1)}, u32[]{:S(2)}, u32[]{:S(2)}) collective-permute-start(f32[2,192,128]{2,1,0:T(8,128)S(1)} %get-tuple-element.47), channel_id=1, source_target_pairs={{0,8},{2,10},{4,12},{6,14},{8,0},{10,2},{12,4},{14,6},{16,24},{18,... | collective-permute-start | bytes 589832 | tf_op jit(solution)/shard_map/ppermute | solution.py:35
  45.4 9.1 %collective-permute-start.9 = (f32[2,192,128]{2,1,0:T(8,128)S(1)}, f32[2,192,128]{2,1,0:T(8,128)S(1)}, u32[]{:S(2)}, u32[]{:S(2)}) collective-permute-start(f32[2,192,128]{2,1,0:T(8,128)S(1)} %get-tuple-element.43), channel_id=1, source_target_pairs={{0,8},{2,10},{4,12},{6,14},{8,0},{10,2},{12,4},{14,6},{16,24},{18,... | collective-permute-start | bytes 589832 | tf_op jit(solution)/shard_map/ppermute | solution.py:35
  62.2 6.0 %collective-permute-start.10 = (f32[16,200,128]{2,1,0:T(8,128)S(1)}, f32[16,200,128]{2,1,0:T(8,128)}, u32[]{:S(2)}, u32[]{:S(2)}) collective-permute-start(f32[16,200,128]{2,1,0:T(8,128)S(1)} %pad_maximum_fusion.a_own), channel_id=1, source_target_pairs={{0,1},{1,0},{2,3},{3,2},{4,5},{5,4},{6,7},{7,6},{8,9},{9,8},{10,11... | collective-permute-start | bytes 4915208 | tf_op jit(solution)/shard_map/ppermute | solution.py:35
  62.9 5.3 %collective-permute-start.13 = (f32[16,192,128]{2,1,0:T(8,128)S(1)}, f32[16,192,128]{2,1,0:T(8,128)}, u32[]{:S(2)}, u32[]{:S(2)}) collective-permute-start(f32[16,192,128]{2,1,0:T(8,128)S(1)} %pad_maximum_fusion.1.b_own), channel_id=1, source_target_pairs={{0,1},{1,0},{2,3},{3,2},{4,5},{5,4},{6,7},{7,6},{8,9},{9,8},{10,11... | collective-permute-start | bytes 4718600 | tf_op jit(solution)/shard_map/ppermute | solution.py:35
  64.5 12.2 %collective-permute-start.14 = (f32[4,192,128]{2,1,0:T(8,128)S(1)}, f32[4,192,128]{2,1,0:T(8,128)S(1)}, u32[]{:S(2)}, u32[]{:S(2)}) collective-permute-start(f32[4,192,128]{2,1,0:T(8,128)S(1)} %copy-done.6), channel_id=1, source_target_pairs={{0,4},{2,6},{4,0},{6,2},{8,12},{10,14},{12,8},{14,10},{16,20},{18,... | collective-permute-start | bytes 1179656 | tf_op jit(solution)/shard_map/ppermute | solution.py:35
  65.0 13.3 %collective-permute-start.16 = (f32[4,192,128]{2,1,0:T(8,128)S(1)}, f32[4,192,128]{2,1,0:T(8,128)S(1)}, u32[]{:S(2)}, u32[]{:S(2)}) collective-permute-start(f32[4,192,128]{2,1,0:T(8,128)S(1)} %copy-done.4), channel_id=1, source_target_pairs={{0,2},{2,0},{4,6},{6,4},{8,10},{10,8},{12,14},{14,12},{16,18},{18,... | collective-permute-start | bytes 1179656 | tf_op jit(solution)/shard_map/ppermute | solution.py:35
  76.8 19.7 %collective-permute-start.15 = (f32[8,192,128]{2,1,0:T(8,128)S(1)}, f32[8,192,128]{2,1,0:T(8,128)S(1)}, u32[]{:S(2)}, u32[]{:S(2)}) collective-permute-start(f32[8,192,128]{2,1,0:T(8,128)S(1)} %pad_maximum_fusion.4), channel_id=1, source_target_pairs={{0,2},{2,0},{4,6},{6,4},{8,10},{10,8},{12,14},{14,12},{16,18},{18,... | collective-permute-start | bytes 2359304 | tf_op jit(solution)/shard_map/ppermute | solution.py:35
  78.4 19.4 %collective-permute-start.17 = (f32[8,192,128]{2,1,0:T(8,128)S(1)}, f32[8,192,128]{2,1,0:T(8,128)S(1)}, u32[]{:S(2)}, u32[]{:S(2)}) collective-permute-start(f32[8,192,128]{2,1,0:T(8,128)S(1)} %pad_maximum_fusion.5), channel_id=1, source_target_pairs={{0,4},{2,6},{4,0},{6,2},{8,12},{10,14},{12,8},{14,10},{16,20},{18,... | collective-permute-start | bytes 2359304 | tf_op jit(solution)/shard_map/ppermute | solution.py:35
  93.6 5.0 %copy-start.13 = (f32[128]{0:T(128)S(1)}, f32[128]{0:T(128)}, u32[]{:S(2)}) copy-start(f32[128]{0:T(128)} %param.20) | copy-start | bytes 1540
  97.9 9.3 %collective-permute-start.18 = (f32[16,192,128]{2,1,0:T(8,128)S(1)}, f32[16,192,128]{2,1,0:T(8,128)S(1)}, u32[]{:S(2)}, u32[]{:S(2)}) collective-permute-start(f32[16,192,128]{2,1,0:T(8,128)S(1)} %constant_dynamic-update-slice_fusion.10.refs_3_), channel_id=1, source_target_pairs={{0,1},{1,0},{2,3},{3,2},{4,5},{5,4},{6,7},{7,6},{8,9},{9,8},{10,11... | collective-permute-start | bytes 4718600 | tf_op jit(solution)/shard_map/ppermute | solution.py:35
  98.0 9.2 %collective-permute-start.19 = (f32[16,192,128]{2,1,0:T(8,128)S(1)}, f32[16,192,128]{2,1,0:T(8,128)S(1)}, u32[]{:S(2)}, u32[]{:S(2)}) collective-permute-start(f32[16,192,128]{2,1,0:T(8,128)S(1)} %constant_dynamic-update-slice_fusion.13.refs_4_), channel_id=1, source_target_pairs={{0,1},{1,0},{2,3},{3,2},{4,5},{5,4},{6,7},{7,6},{8,9},{9,8},{10,11... | collective-permute-start | bytes 4718600 | tf_op jit(solution)/shard_map/ppermute | solution.py:35
  122.7 2.7 %collective-permute-start.20 = (f32[16,128,128]{2,1,0:T(8,128)S(1)}, f32[16,128,128]{2,1,0:T(8,128)S(1)}, u32[]{:S(2)}, u32[]{:S(2)}) collective-permute-start(f32[16,128,128]{2,1,0:T(8,128)S(1)} %get-tuple-element.31), channel_id=1, source_target_pairs={{0,1},{1,0},{2,3},{3,2},{4,5},{5,4},{6,7},{7,6},{8,9},{9,8},{10,11... | collective-permute-start | bytes 3145736 | tf_op jit(solution)/shard_map/ppermute | solution.py:35
  125.6 8.4 %collective-permute-start.23 = (f32[512,128]{1,0:T(8,128)S(1)}, f32[512,128]{1,0:T(8,128)S(1)}, u32[]{:S(2)}, u32[]{:S(2)}) collective-permute-start(f32[512,128]{1,0:T(8,128)S(1)} %bitcast.101), channel_id=1, source_target_pairs={{0,4},{2,6},{4,0},{6,2},{8,12},{10,14},{12,8},{14,10},{16,20},{18,... | collective-permute-start | bytes 786440 | tf_op jit(solution)/shard_map/ppermute | solution.py:35
  126.3 8.4 %collective-permute-start.21 = (f32[520,128]{1,0:T(8,128)S(1)}, f32[520,128]{1,0:T(8,128)S(1)}, u32[]{:S(2)}, u32[]{:S(2)}) collective-permute-start(f32[520,128]{1,0:T(8,128)S(1)} %pad_maximum_fusion.8), channel_id=1, source_target_pairs={{0,2},{2,0},{4,6},{6,4},{8,10},{10,8},{12,14},{14,12},{16,18},{18,... | collective-permute-start | bytes 798728 | tf_op jit(solution)/shard_map/ppermute | solution.py:35
  134.1 5.0 %collective-permute-start.24 = (f32[256,128]{1,0:T(8,128)S(1)}, f32[256,128]{1,0:T(8,128)S(1)}, u32[]{:S(2)}, u32[]{:S(2)}) collective-permute-start(f32[256,128]{1,0:T(8,128)S(1)} %bitcast.103), channel_id=1, source_target_pairs={{0,2},{2,0},{4,6},{6,4},{8,10},{10,8},{12,14},{14,12},{16,18},{18,... | collective-permute-start | bytes 393224 | tf_op jit(solution)/shard_map/ppermute | solution.py:35
  134.8 5.1 %collective-permute-start.22 = (f32[264,128]{1,0:T(8,128)S(1)}, f32[264,128]{1,0:T(8,128)S(1)}, u32[]{:S(2)}, u32[]{:S(2)}) collective-permute-start(f32[264,128]{1,0:T(8,128)S(1)} %pad_maximum_fusion.11), channel_id=1, source_target_pairs={{0,4},{2,6},{4,0},{6,2},{8,12},{10,14},{12,8},{14,10},{16,20},{18,... | collective-permute-start | bytes 405512 | tf_op jit(solution)/shard_map/ppermute | solution.py:35
  140.0 5.1 %collective-permute-start.25 = (f32[264,128]{1,0:T(8,128)S(1)}, f32[264,128]{1,0:T(8,128)S(1)}, u32[]{:S(2)}, u32[]{:S(2)}) collective-permute-start(f32[264,128]{1,0:T(8,128)S(1)} %pad_maximum_fusion.12), channel_id=1, source_target_pairs={{0,8},{2,10},{4,12},{6,14},{8,0},{10,2},{12,4},{14,6},{16,24},{18,... | collective-permute-start | bytes 405512 | tf_op jit(solution)/shard_map/ppermute | solution.py:35
  145.1 5.3 %collective-permute-start.26 = (f32[136,128]{1,0:T(8,128)S(1)}, f32[136,128]{1,0:T(8,128)S(1)}, u32[]{:S(2)}, u32[]{:S(2)}) collective-permute-start(f32[136,128]{1,0:T(8,128)S(1)} %pad_maximum_fusion.14), channel_id=1, source_target_pairs={{0,16},{2,18},{4,20},{6,22},{8,24},{10,26},{12,28},{14,30},{16,0},... | collective-permute-start | bytes 208904 | tf_op jit(solution)/shard_map/ppermute | solution.py:35
  (9 other events, 22.1 us)

commit v6 on v5

--- a/solution.py
+++ b/solution.py
@@ -15,6 +15,7 @@
 MIB = 1024 * 1024
 VMEM_MIX = 16 * MIB
 VMEM_HEAD = 20 * MIB
+LITTLE = pl.CostEstimate(flops=1, bytes_accessed=1, transcendentals=0)
 
 
 def hadamard(length):
@@ -102,23 +103,28 @@
     return (value ^ (value >> 1)) & 1
 
 
-def mix_kernel(rows, begin, group, bits_a, bits_b, me_ref, a_own, a_other, b_own, b_other, emb_ref, lane_ref, block_ref, out_ref, sign_ref, wide_ref, spread_ref):
+def flip(bits):
+    return (1 - 2 * (bits & 1)).astype(jnp.float32)
+
+
+def prepare(bits_a, bits_b, a_own, a_other, b_own, b_other, emb_ref, sign_ref, wide_ref):
     f32 = jnp.float32
     bf16 = jnp.bfloat16
     chunks = a_own.shape[0]
     width = emb_ref.shape[0]
     quarters = width // LANES
     here = LANES // quarters
-    def flip(bits):
-        return (1 - 2 * (bits & 1)).astype(f32)
-
-    for c, ref in enumerate((a_own, a_other)):
-        for p in range(chunks):
-            top = (c * chunks + p) * here
-            for q in range(quarters):
-                sign_ref[top : top + here, q * LANES : (q + 1) * LANES] = ref[
-                    p, q * here : (q + 1) * here, :
-                ].astype(bf16)
+    few = here // 2
+    order = [place_of(distance, bits_a) for distance in range(chunks)]
+
+    for c, pair in enumerate(((a_own, b_own), (a_other, b_other))):
+        for part, (ref, bits) in enumerate(zip(pair, (bits_a, bits_b))):
+            for distance in range(chunks):
+                top = (c * chunks + order[distance]) * here + part * few
+                for q in range(quarters):
+                    sign_ref[top : top + few, q * LANES : (q + 1) * LANES] = ref[
+                        place_of(distance, bits), q * few : (q + 1) * few, :
+                    ].astype(bf16)
     sums = jnp.dot(jnp.ones((16, sign_ref.shape[0]), bf16), sign_ref[...], preferred_element_type=f32)
     odd = 0.5 * sums - 2.0 * jnp.floor(0.25 * sums)
     row = lax.broadcasted_iota(jnp.int32, odd.shape, 0)
@@ -131,22 +137,28 @@
     wide_ref[width:, :] = jnp.zeros((LANES, wide_ref.shape[1]), bf16)
     wide_ref[width : width + 16, :] = jnp.where(row < quarters, high, rest - high).astype(bf16)
 
+
+def first_kernel(rows, begin, group, bits_a, bits_b, me_ref, a_own, a_other, b_own, b_other, *refs):
+    f32 = jnp.float32
+    bf16 = jnp.bfloat16
+    if begin == 0:
+        emb_ref, out_ref, sign_ref, wide_ref = refs
+        prepare(bits_a, bits_b, a_own, a_other, b_own, b_other, emb_ref, sign_ref, wide_ref)
+    else:
+        sign_ref, wide_ref, out_ref = refs
+    here = sign_ref.shape[0] // (2 * a_own.shape[0])
     major_me = me_ref[0] * here
     low = here.bit_length() - 1
-    half = LANES // 2
     lane = lax.broadcasted_iota(jnp.int32, (CHUNK, LANES), 1)
+
     @pl.loop(0, out_ref.shape[0] // group)
     def _(step):
         left = []
-        orders = []
-        gains = []
         for g in range(group):
-            chunk = begin + step * group + g
-            pa = place_of(chunk, bits_a)
-            pb = place_of(chunk, bits_b)
+            pa = place_of(begin + step * group + g, bits_a)
             columns = []
             for ref in (a_own, a_other):
-                source = ref[pa, 3 * half : 3 * half + 1, :].astype(jnp.int32)
+                source = ref[pa, LANES // 2 : LANES // 2 + 1, :].astype(jnp.int32)
                 major = source >> 2
                 code = major & (here - 1)
                 for i, bit in enumerate(bits_a):
@@ -164,66 +176,82 @@
             flip_me, flip_1, flip_2 = flip(code >> 12), flip(code >> 10), flip(code >> 11)
             turns = [flip_me, flip_me * flip_1, flip_me * flip_2, flip_me * flip_1 * flip_2]
             parts = [
-                (jnp.floor(0.25 * sums[:, q * LANES : (q + 1) * LANES]) * turns[q]).astype(bf16) for q in range(4)
+                (jnp.floor(0.25 * sums[:, q * LANES : (q + 1) * LANES]) * turns[q]).astype(bf16)
+                for q in range(4)
             ]
             tail = flip_me * jnp.where((lane & 1) != 0, flip_1, 1.0) * jnp.where((lane & 2) != 0, flip_2, 1.0)
             parts.append(jnp.where(lane < 8, tail, 0.0).astype(bf16))
             left.append(jnp.concatenate(parts, axis=1))
-            orders.append(
-                jnp.concatenate(
-                    [
-                        ref[p, LANES : LANES + half, :]
-                        for ref, p in ((a_own, pa), (b_own, pb), (a_other, pa), (b_other, pb))
-                    ],
-                    axis=0,
-                ).astype(jnp.int32)
-            )
-            gains.append(
-                jnp.concatenate(
-                    [
-                        ref[pb, 0:LANES, :] * (1 - 2 * odd_bits((2 * chunk + c) & me_ref[0])).astype(f32)
-                        for c, ref in enumerate((b_own, b_other))
-                    ],
-                    axis=0,
+        first = jnp.dot(jnp.concatenate(left, axis=0), wide_ref[...], preferred_element_type=f32)
+        for g in range(group):
+            for r in range(rows):
+                out_ref[step * group + g, r] = first[g * CHUNK : (g + 1) * CHUNK, r * LANES : (r + 1) * LANES]
+
+
+def mix_kernel(rows, begin, group, bits_a, bits_b, me_ref, first_ref, *refs):
+    a_refs, b_refs, (lane_ref, block_ref, out_ref, spread_ref) = refs[:4], refs[4:8], refs[8:]
+    f32 = jnp.float32
+    top = max(bits_a[-1], bits_b[-1])
+
+    def piece(refs, core, chunk, within, bits):
+        far = 1 if within & bits[-1] else 0
+        return refs[2 * core + far][place_of(chunk, bits[:-1])]
+
+    @pl.loop(0, out_ref.shape[0] // (2 * top))
+    def _(step):
+        for within in range(0, 2 * top, group):
+            at = step * 2 * top + within
+            orders = []
+            gains = []
+            for g in range(group):
+                chunk = begin + at + g
+                orders += [piece(a_refs, c, chunk, within + g, bits_a) for c in range(2)]
+                gains += [
+                    piece(b_refs, c, chunk, within + g, bits_b)
+                    * (1 - 2 * odd_bits((2 * chunk + c) & me_ref[0])).astype(f32)
+                    for c in range(2)
+                ]
+            order = jnp.concatenate(orders, axis=0).astype(jnp.int32)
+            gain = jnp.concatenate(gains, axis=0)
+            for r in range(rows):
+                columns = slice(r * LANES, (r + 1) * LANES)
+                first = jnp.concatenate([first_ref[at + g, r] for g in range(group)], axis=0)
+                mixed = jnp.take_along_axis(first, order, axis=1) * gain
+                across = jnp.dot(
+                    jnp.concatenate(halves(mixed), axis=1), lane_ref[...], preferred_element_type=f32
                 )
-            )
-        order = jnp.concatenate(orders, axis=0)
-        gain = jnp.concatenate(gains, axis=0)
-        first = jnp.dot(jnp.concatenate(left, axis=0), wide_ref[...], preferred_element_type=f32)
-        for r in range(rows):
-            columns = slice(r * LANES, (r + 1) * LANES)
-            mixed = jnp.take_along_axis(first[:, columns], order, axis=1) * gain
-            across = jnp.dot(
-                jnp.concatenate(halves(mixed), axis=1), lane_ref[...], preferred_element_type=f32
-            )
-            high, low_part = halves(across)
+                high, low = halves(across)
+                for g in range(group):
+                    here = slice(g * CHUNK, (g + 1) * CHUNK)
+                    spread_ref[g, 0:CHUNK, columns] = high[here]
+                    spread_ref[g, CHUNK:, columns] = low[here]
             for g in range(group):
-                here_rows = slice(g * CHUNK, (g + 1) * CHUNK)
-                spread_ref[g, 0:CHUNK, columns] = high[here_rows]
-                spread_ref[g, CHUNK:, columns] = low_part[here_rows]
-        for g in range(group):
-            result = jnp.dot(block_ref[...], spread_ref[g], preferred_element_type=f32)
-            for r in range(rows):
-                out_ref[step * group + g, r] = result[:, r * LANES : (r + 1) * LANES]
-
-
-def turn_cosine_coefficients(degree):
+                result = jnp.dot(block_ref[...], spread_ref[g], preferred_element_type=f32)
+                for r in range(rows):
+                    out_ref[at + g, r] = result[:, r * LANES : (r + 1) * LANES]
+
+
+def turn_sine_coefficients(degree):
     points = np.cos(np.pi * (np.arange(400) + 0.5) / 400)
-    u = 0.5 * points
-    fit = np.polynomial.chebyshev.Chebyshev.fit(u * u, np.cos(2 * np.pi * u), degree, domain=[0, 0.25])
+    v = 0.125 + 0.125 * points
+    fit = np.polynomial.chebyshev.Chebyshev.fit(
+        v * v, np.sin(2 * np.pi * v) / v, degree, domain=[0, 0.0625], w=v
+    )
     return [float(c) for c in fit.convert(kind=np.polynomial.Polynomial).coef]
 
 
 def head_kernel(rows, coefs, grad_scale, bits_a, bits_b, parts, me_ref, target_ref, *refs):
-    y_refs, late_refs, refs = refs[:parts], refs[parts : parts + 4], refs[parts + 4 :]
+    y_refs, late_refs, refs = refs[:parts], refs[parts : parts + 8], refs[parts + 8 :]
     pred_ref, keep_ref, send_ref, feat_ref, acc_ref, scale_ref = refs
     f32 = jnp.float32
     chunks = feat_ref.shape[0]
     cut = LANES // 2
     acc_ref[...] = jnp.zeros_like(acc_ref)
 
-    for part, late_ref in enumerate(late_refs):
+    for part in range(4):
         core, bits = part // 2, (bits_a, bits_b)[part % 2]
+        near = late_refs[2 * part].shape[0]
+        late = [late_refs[2 * part + place // near].at[place % near] for place in range(chunks)]
         turns_me = [
             (1 - 2 * (odd_bits((2 * k + core) & me_ref[0]) ^ odd_bits(me_ref[0]))).astype(f32)
             for k in range(chunks)
@@ -234,7 +262,7 @@
             row = pl.multiple_of(i * 8, 8)
             here = pl.ds(row + part * cut, 8)
             for k in range(chunks):
-                scale_ref[k] = late_ref[place_of(k, bits), pl.ds(row, 8), :] * turns_me[k]
+                scale_ref[k] = late[place_of(k, bits)][pl.ds(row, 8), :] * turns_me[k]
             for r in range(rows):
                 values = [y_ref[k, r, here, :] for y_ref in y_refs for k in range(y_ref.shape[0])]
                 width = 1
@@ -247,14 +275,15 @@
                 acc = acc_ref[r]
                 for k in range(chunks):
                     place = place_of(k, bits)
-                    turns = values[k] * scale_ref[k] + late_ref[place, pl.ds(row + cut, 8), :]
-                    u = turns - jnp.round(turns)
-                    square = u * u
-                    cosine = jnp.full_like(square, coefs[-1])
-                    for c in coefs[-2::-1]:
+                    turns = values[k] * scale_ref[k] + late[place][pl.ds(row + cut, 8), :]
+                    quarter = 0.25 - jnp.abs(turns - jnp.round(turns))
+                    square = quarter * quarter
+                    cosine = square * coefs[-1] + coefs[-2]
+                    for c in coefs[-3::-1]:
                         cosine = cosine * square + c
+                    cosine = cosine * quarter
                     feat_ref[k, r, here, :] = cosine
-                    acc = acc + cosine * late_ref[place, pl.ds(row + 2 * cut, 8), :]
+                    acc = acc + cosine * late[place][pl.ds(row + 2 * cut, 8), :]
                 acc_ref[r] = acc
 
     residuals = []
@@ -333,42 +362,23 @@
         bits_b = bits[:-2] + [1, 2]
     else:
         me = 0
-        bits_a = bits_b = [1 << i for i in range(chunks.bit_length() - 1)]
+        bits_a = bits_b = [1 << i for i in reversed(range(chunks.bit_length() - 1))]
+        from_place = np.argsort([place_of(distance, bits_a) for distance in range(chunks)])
         whole = gather_ordered(jnp.concatenate(everything))
         numbers = whole[:, 6 * mine, :mine].reshape(chunks, 2, 1, LANES)
-        numbers = jnp.broadcast_to(numbers, (chunks, 2, 8, LANES))
-        everything = [whole[:, i * mine : (i + 1) * mine].reshape(chunks, 2, LANES, LANES) for i in range(6)]
+        numbers = jnp.broadcast_to(numbers, (chunks, 2, 8, LANES))[from_place]
+        everything = [whole[:, i * mine : (i + 1) * mine].reshape(chunks, 2, LANES, LANES)[from_place] for i in range(6)]
         everything.append(numbers)
     signs, positions, gains, *late, numbers = everything
 
     per_half = LANES // quarters
+    cut = LANES // 2
     shape = signs.shape
-    signs = jnp.swapaxes(signs.reshape(shape[:-2] + (per_half, quarters, LANES)), -3, -2).reshape(shape)
-    cut = LANES // 2
-    pieces = [
-        jnp.concatenate([signs, positions[..., :cut, :], numbers], axis=-2),
-        jnp.concatenate([gains, positions[..., cut:, :]], axis=-2),
-        jnp.concatenate([x[..., :cut, :] for x in late], axis=-2),
-        jnp.concatenate([x[..., cut:, :] for x in late], axis=-2),
-    ]
-    if direct:
-        early = [x[None] for x in pieces[:2]]
-        late = [x[None] for x in pieces[2:]]
-        for i in range(len(bits)):
-            if i == len(bits) - 2:
-                late = [after(x, *early) for x in late]
-            if i >= len(bits) - 2:
-                late = [doubled(x, bits[i + 2 - len(bits)]) for x in late]
-            early = [doubled(x, b[i]) for x, b in zip(early, (bits_a, bits_b))]
-            if i >= len(bits) - 2:
-                early = [after(x, *late) for x in early]
-        for i in range(2, len(bits) - 2):
-            late = [doubled(x, bits[i]) for x in late]
-        late = [after(x, *early) for x in late]
-        late_got = [swap(x, "feat", b[-2]) for x, b in zip(late, (bits_a, bits_b))]
-        a_pair, b_pair = ((x, swap(x, "rows", 1)) for x in early)
-    else:
-        a_pair, b_pair, c_pair, d_pair = ((x[:, 0], x[:, 1]) for x in pieces)
+    signs = signs.reshape(shape[:-2] + (2, per_half // 2, quarters, LANES))
+    signs = jnp.swapaxes(signs, -3, -2).reshape(shape)
+    early = [jnp.concatenate([signs[..., :cut, :], numbers], axis=-2), signs[..., cut:, :]]
+    middle = [positions, gains]
+    late = [jnp.concatenate([x[..., part, :] for x in late], axis=-2) for part in (slice(0, cut), slice(cut, LANES))]
 
     emb = lax.dynamic_slice_in_dim(embeddings, place * rows, rows, 0)
     lane_signs = hadamard(LANES)
@@ -381,43 +391,126 @@
 
     scalars = pl.BlockSpec(memory_space=pltpu.SMEM)
     vmem = pl.BlockSpec(memory_space=pltpu.VMEM)
-    resident_args = (*a_pair, *b_pair, emb, lane_matrix, block_matrix)
-
-    def mix(begin, count, group=2):
+    group = 2
+
+    def first_of(begin, count, early, ready):
+        shapes = [jax.ShapeDtypeStruct((count, rows, CHUNK, LANES), f32)]
+        if begin == 0:
+            shapes.append(jax.ShapeDtypeStruct((blocks // quarters, width), jnp.bfloat16))
+            shapes.append(jax.ShapeDtypeStruct((width + LANES, rows * LANES), jnp.bfloat16))
+        return pl.pallas_call(
+            functools.partial(first_kernel, rows, begin, group, bits_a, bits_b),
+            in_specs=[scalars] + [vmem] * (4 + len(ready)),
+            out_specs=[vmem] * len(shapes),
+            out_shape=shapes,
+            compiler_params=pltpu.CompilerParams(vmem_limit_bytes=VMEM_MIX),
+            cost_estimate=LITTLE,
+            name="first",
+        )(about_me, *early, *ready)
+
+    def mix(begin, first, middle):
+        count = first.shape[0]
         return pl.pallas_call(
             functools.partial(mix_kernel, rows, begin, group, bits_a, bits_b),
-            in_specs=[scalars] + [vmem] * len(resident_args),
+            in_specs=[scalars] + [vmem] * 11,
             out_specs=vmem,
-            out_shape=jax.ShapeDtypeStruct((count, rows, CHUNK, LANES), f32),
-            scratch_shapes=[
-                pltpu.VMEM((blocks // quarters, width), jnp.bfloat16),
-                pltpu.VMEM((width + LANES, rows * LANES), jnp.bfloat16),
-                pltpu.VMEM((group, 2 * CHUNK, rows * LANES), jnp.bfloat16),
-            ],
+            out_shape=jax.ShapeDtypeStruct(first.shape, f32),
+            input_output_aliases={1: 0},
+            scratch_shapes=[pltpu.VMEM((group, 2 * CHUNK, rows * LANES), jnp.bfloat16)],
             compiler_params=pltpu.CompilerParams(vmem_limit_bytes=VMEM_MIX),
-            cost_estimate=pl.CostEstimate(
-                flops=count * 2 * 256 * 8192 * 256, bytes_accessed=count * rows * CHUNK * LANES * 4, transcendentals=0
-            ),
+            cost_estimate=LITTLE,
             name="mix",
-        )(about_me, *resident_args)
-
-    cuts = (0, chunks // 4, chunks * 3 // 4, chunks)
-    spread = [mix(cuts[0], cuts[1] - cuts[0])]
+        )(about_me, first, *middle, lane_matrix, block_matrix)
+
+    cuts = [chunks * i // 4 for i in range(5)]
     if direct:
-        late = [jnp.concatenate([x, after(y, spread[0])], axis=0) for x, y in zip(late, late_got)]
-        late_got = [swap(x, "feat", b[-1]) for x, b in zip(late, (bits_a, bits_b))]
-    spread.append(mix(cuts[1], cuts[2] - cuts[1]))
-    if direct:
-        late = [jnp.concatenate([x, after(y, spread[1])], axis=0) for x, y in zip(late, late_got)]
-        c_pair, d_pair = ((x, swap(x, "rows", 1)) for x in late)
-    spread.append(mix(cuts[2], cuts[3] - cuts[2]))
+        orders = (bits_a, bits_b)
+
+        def send(values, bit, *others):
+            return swap(after(values, *others) if others else values, "feat", bit)
+
+        def send_pair(pair, step, *others):
+            return [send(x, b[step], *others) for x, b in zip(pair, orders)]
+
+        def join(held, got, *others):
+            return jnp.concatenate([held, after(got, *others) if others else got], axis=0)
+
+        def join_pair(pair, got, *others):
+            return [join(x, y, *others) for x, y in zip(pair, got)]
+
+        def parted(held, pair):
+            size = pair[0].shape[0]
+            return [held[:, :size], held[:, size:]]
+
+        def with_core(pair):
+            return [y for x in pair for y in (x, swap(x, "rows", 1))]
+
+        last = len(bits) - 1
+        s_held, m_held, l_held = (jnp.concatenate(x, axis=0)[None] for x in (early, middle, late))
+        m_step = None
+        for i in range(last - 1):
+            s_step = send(s_held, bits[i])
+            m_next = send(m_held if m_step is None else join(m_held, m_step), bits[i], s_held)
+            s_held = join(s_held, s_step)
+            if m_step is not None:
+                m_held = join(m_held, m_step)
+            m_step = m_next
+        s_pair = parted(s_held, early)
+        s_step = send_pair(s_pair, last - 1)
+        l_step = send(l_held, bits[0], s_held)
+        m_held = join(m_held, m_step)
+        m_pair = parted(m_held, middle)
+        s_pair = join_pair(s_pair, s_step)
+        s_step = send_pair(s_pair, last)
+        m_step = send_pair(m_pair, last - 1, *s_pair)
+        s_pair = join_pair(s_pair, s_step)
+        s_all = with_core(s_pair)
+        for i in range(1, last - 1):
+            l_held = join(l_held, l_step)
+            l_step = send(l_held, bits[i], m_held)
+        m_pair = join_pair(m_pair, m_step)
+        m_step = send_pair(m_pair, last, *s_pair)
+        m_core = [swap(x, "rows", 1) for x in m_pair]
+        first, *ready = first_of(0, cuts[1], s_all, [emb])
+        first = [first]
+        l_held = join(l_held, l_step)
+        l_pair = parted(l_held, late)
+        l_step = send_pair(l_pair, last - 1)
+        s_all[0] = after(s_all[0], *l_pair)
+        first += [first_of(cuts[i], cuts[i + 1] - cuts[i], s_all, ready)[0] for i in (1, 2)]
+        l_pair = join_pair(l_pair, l_step, *first)
+        l_step = send_pair(l_pair, last)
+        l_core = [swap(x, "rows", 1) for x in l_pair]
+        m_step = [after(x, *l_pair) for x in m_step]
+        m_all = []
+        for held, got, core_held in zip(m_pair, m_step, m_core):
+            m_all += [held, got, core_held, swap(got, "rows", 1)]
+        s_all[0] = after(s_all[0], *l_pair, *m_step)
+        first.append(first_of(cuts[3], cuts[4] - cuts[3], s_all, ready)[0])
+        m_all[0] = after(m_all[0], first[3])
+        spread = []
+        for k, x in zip(cuts, first):
+            spread.append(mix(k, x, m_all))
+            m_all[0] = after(m_all[0], spread[-1])
+        l_step = [after(x, spread[-1]) for x in l_step]
+        l_all = []
+        for held, got, core_held in zip(l_pair, l_step, l_core):
+            l_all += [held, got, core_held, swap(got, "rows", 1)]
+    else:
+        low, high = slice(0, chunks // 2), slice(chunks // 2, chunks)
+        s_all = [part[:, c] for part in early for c in range(2)]
+        m_all = [part[half, c] for part in middle for c in range(2) for half in (low, high)]
+        l_all = [part[half, c] for part in late for c in range(2) for half in (low, high)]
+        first, *ready = first_of(0, cuts[1], s_all, [emb])
+        first = [first] + [first_of(cuts[i], cuts[i + 1] - cuts[i], s_all, ready)[0] for i in (1, 2, 3)]
+        spread = [mix(k, x, m_all) for k, x in zip(cuts, first)]
 
     my_targets = lax.dynamic_slice_in_dim(targets, place * rows, rows, 0)
     found, keep, send = pl.pallas_call(
         functools.partial(
-            head_kernel, rows, turn_cosine_coefficients(5), 1.0 / math.sqrt(total_rows), bits_a, bits_b, len(spread)
+            head_kernel, rows, turn_sine_coefficients(3), 1.0 / math.sqrt(total_rows), bits_a, bits_b, len(spread)
         ),
-        in_specs=[scalars, scalars] + [vmem] * (len(spread) + 4),
+        in_specs=[scalars, scalars] + [vmem] * (len(spread) + 8),
         out_specs=[vmem] * 3,
         out_shape=[
             jax.ShapeDtypeStruct((8, LANES), f32),
@@ -431,7 +524,7 @@
         ],
         compiler_params=pltpu.CompilerParams(vmem_limit_bytes=VMEM_HEAD),
         name="head",
-    )(about_me, my_targets, *spread, c_pair[0], d_pair[0], c_pair[1], d_pair[1])
+    )(about_me, my_targets, *spread, *(l_all[i] for i in (0, 1, 4, 5, 2, 3, 6, 7)))
 
     if not direct:
         grads = jnp.stack([keep, send], 1).reshape(feat_size, rows_size, mine, LANES)

time: 152 us -> 139 us (0.914)
  waiting for transfers between devices: 64 us -> 37.7 us
  starting transfers between devices: 29.3 us -> 34.8 us
  other arithmetic: 3.35 us -> 8.2 us
  local copies, waits for them, and re-layouts: 3.21 us -> 5.74 us
    ppermute x27 -> x35, waiting for transfers between devices: 64 us -> 37.7 us  [swap(): return lax.ppermute(values, axis_name, [(i, i ^ bit) for i in range(size)])]
    pallas_call x1 -> x5, Pallas kernels: 15.5 us -> 31.2 us  [the longest x4 16 us: first_of(): pl.pallas_call(functools.partial(first_kernel, rows, begin, group, bits_a...]
    pallas_call x3 -> x4, Pallas kernels: 31.5 us -> 16.7 us  [mix(): pl.pallas_call(functools.partial(mix_kernel, rows, begin, group, bits_a,...]
    ppermute x27 -> x35, starting transfers between devices: 29.3 us -> 34.8 us  [swap(): return lax.ppermute(values, axis_name, [(i, i ^ bit) for i in range(size)])]
    concatenate x10 -> x14, other arithmetic: 0.62 us -> 5.72 us  [join(): jnp.concatenate([held, after(got, *others) if others else got], axis=0)]
    reshape x5, local copies, waits for them, and re-layouts: 0.38 us -> 2.25 us  [half(): values.reshape((rows_size, values.shape[0] // rows_size) + values.shape[1:])]
    slice x3 -> x9, local copies, waits for them, and re-layouts: 0.38 us -> 2.08 us  [the longest x4 1.71 us: parted(): return [held[:, :size], held[:, size:]]]
  transfers between devices with their start and end apart: 27 -> 35, of which waited for: 18 -> 12; matrix products, arithmetic and copies ran while one was open for 2% -> 9% of each run, Pallas kernels for 21% -> 23%
where the time goes in v6:
time: 139 us
  Pallas kernels  47.8 us (34%)
  waiting for transfers between devices  37.7 us (27%)
  starting transfers between devices  34.8 us (25%)
  other arithmetic  8.2 us (6%)
  local copies, waits for them, and re-layouts  5.74 us (4%)
  matrix products  3.36 us (2%)
    ppermute x35, waiting for transfers between devices, swap(): return lax.ppermute(values, axis_name, [(i, i ^ bit) for i in range(size)])  37.7 us
    ppermute x35, starting transfers between devices, swap(): return lax.ppermute(values, axis_name, [(i, i ^ bit) for i in range(size)])  34.8 us
    pallas_call x4, Pallas kernels, mix(): pl.pallas_call(functools.partial(mix_kernel, rows, begin, group, bits_a,...  16.7 us
    pallas_call x4, Pallas kernels, first_of(): pl.pallas_call(functools.partial(first_kernel, rows, begin, group, bits_a...  16 us
    pallas_call x1, Pallas kernels, local(): pl.pallas_call(functools.partial(head_kernel, rows, turn_sine_coefficient...  15.2 us
    concatenate x14, other arithmetic, join(): jnp.concatenate([held, after(got, *others) if others else got], axis=0)  5.72 us
    dot_general x1, matrix products, local(): jnp.einsum('bij,j->bi', half(block_permutations), jnp.arange(LANES).astyp...  3.36 us
  transfers between devices with their start and end apart: 35, of which 12 were waited for; matrix products, arithmetic and copies ran while one was open for 9% of the time, Pallas kernels for 23%

profile of v6, /device:TPU:0, one launch (start us, length us, event | category | flops | bytes accessed | tf_op | source)
XLA Modules:
  0.0 139.0 jit_solution(8127795149765210967)
XLA Ops:
  3.6 4.1 %collective-permute-start = (f32[1,136,128]{2,1,0:T(8,128)S(1)}, f32[1,136,128]{2,1,0:T(8,128)S(1)}, u32[]{:S(2)}, u32[]{:S(2)}) collective-permute-start(f32[1,136,128]{2,1,0:T(8,128)S(1)} %maximum_bitcast_fusion.1), channel_id=1, source_target_pairs={{0,16},{2,18},{4,20},{6,22},{8,24},{10,26},{12,28},{14,30},{16,0},... | collective-permute-start | bytes 208904 | tf_op jit(solution)/shard_map/ppermute | solution.py:36
  7.7 3.4 %fusion = f32[1,128,128]{2,0,1:T(1,128)S(1)} fusion(bf16[2,128,128,128]{3,2,1,0:T(8,128)(2,1)} %bitcast.85, s32[]{:T(128)S(6)} %select_n.17), kind=kOutput, calls=%fused_computation | convolution fusion | flops 4194432 | bytes 4259844 | tf_op jit(solution)/shard_map/bij,j->bi/dot_general | solution.py:345
  12.0 2.0 %collective-permute-start.1 = (f32[2,136,128]{2,1,0:T(8,128)S(1)}, f32[2,136,128]{2,1,0:T(8,128)S(1)}, u32[]{:S(2)}, u32[]{:S(2)}) collective-permute-start(f32[2,136,128]{2,1,0:T(8,128)S(1)} %pad_maximum_fusion.14), channel_id=1, source_target_pairs={{0,8},{2,10},{4,12},{6,14},{8,0},{10,2},{12,4},{14,6},{16,24},{18,... | collective-permute-start | bytes 417800 | tf_op jit(solution)/shard_map/ppermute | solution.py:36
  14.0 5.7 %collective-permute-done.1 = f32[2,136,128]{2,1,0:T(8,128)S(1)} collective-permute-done((f32[2,136,128]{2,1,0:T(8,128)S(1)}, f32[2,136,128]{2,1,0:T(8,128)S(1)}, u32[]{:S(2)}, u32[]{:S(2)}) %collective-permute-start.1) | collective-permute-done | bytes 139296 | tf_op jit(solution)/shard_map/ppermute | solution.py:36
  19.7 1.9 %collective-permute-start.5 = (f32[4,64,128]{2,1,0:T(8,128)S(1)}, f32[4,64,128]{2,1,0:T(8,128)S(1)}, u32[]{:S(2)}, u32[]{:S(2)}) collective-permute-start(f32[4,64,128]{2,1,0:T(8,128)S(1)} %slice.194), channel_id=1, source_target_pairs={{0,2},{2,0},{4,6},{6,4},{8,10},{10,8},{12,14},{14,12},{16,18},{18,... | collective-permute-start | bytes 393224 | tf_op jit(solution)/shard_map/ppermute | solution.py:36
  21.7 1.6 %collective-permute-start.2 = (f32[4,72,128]{2,1,0:T(8,128)S(1)}, f32[4,72,128]{2,1,0:T(8,128)S(1)}, u32[]{:S(2)}, u32[]{:S(2)}) collective-permute-start(f32[4,72,128]{2,1,0:T(8,128)S(1)} %slice.193), channel_id=1, source_target_pairs={{0,4},{2,6},{4,0},{6,2},{8,12},{10,14},{12,8},{14,10},{16,20},{18,... | collective-permute-start | bytes 442376 | tf_op jit(solution)/shard_map/ppermute | solution.py:36
  23.5 4.0 %collective-permute-start.11 = (f32[1,384,128]{2,1,0:T(8,128)S(1)}, f32[1,384,128]{2,1,0:T(8,128)S(1)}, u32[]{:S(2)}, u32[]{:S(2)}) collective-permute-start(f32[1,384,128]{2,1,0:T(8,128)S(1)} %bitcast.88), channel_id=1, source_target_pairs={{0,16},{2,18},{4,20},{6,22},{8,24},{10,26},{12,28},{14,30},{16,0},... | collective-permute-start | bytes 589832 | tf_op jit(solution)/shard_map/ppermute | solution.py:36
  28.8 3.0 %collective-permute-done.9 = f32[2,256,128]{2,1,0:T(8,128)} collective-permute-done((f32[2,256,128]{2,1,0:T(8,128)S(1)}, f32[2,256,128]{2,1,0:T(8,128)}, u32[]{:S(2)}, u32[]{:S(2)}) %collective-permute-start.9) | collective-permute-done | bytes 262176 | tf_op jit(solution)/shard_map/ppermute | solution.py:36
  32.8 2.7 %collective-permute-done.11 = f32[1,384,128]{2,1,0:T(8,128)S(1)} collective-permute-done((f32[1,384,128]{2,1,0:T(8,128)S(1)}, f32[1,384,128]{2,1,0:T(8,128)S(1)}, u32[]{:S(2)}, u32[]{:S(2)}) %collective-permute-start.11) | collective-permute-done | bytes 196640 | tf_op jit(solution)/shard_map/ppermute | solution.py:36
  36.4 1.4 %collective-permute-start.10 = (f32[4,128,128]{2,1,0:T(8,128)}, f32[4,128,128]{2,1,0:T(8,128)}, u32[]{:S(2)}, u32[]{:S(2)}) collective-permute-start(f32[4,128,128]{2,1,0:T(8,128)} %get-tuple-element.31), channel_id=1, source_target_pairs={{0,4},{2,6},{4,0},{6,2},{8,12},{10,14},{12,8},{14,10},{16,20},{18,... | collective-permute-start | bytes 786440 | tf_op jit(solution)/shard_map/ppermute | solution.py:36
  39.1 4.5 %collective-permute-done.12 = f32[2,384,128]{2,1,0:T(8,128)S(1)} collective-permute-done((f32[2,384,128]{2,1,0:T(8,128)S(1)}, f32[2,384,128]{2,1,0:T(8,128)S(1)}, u32[]{:S(2)}, u32[]{:S(2)}) %collective-permute-start.12) | collective-permute-done | bytes 393248 | tf_op jit(solution)/shard_map/ppermute | solution.py:36
  50.7 1.4 collective-permute-start.15
  52.1 4.4 %first.4 = (f32[4,8,256,128]{3,2,1,0:T(8,128)S(1)}, bf16[1024,512]{1,0:T(8,128)(2,1)S(1)}, bf16[640,1024]{1,0:T(8,128)(2,1)S(1)}) custom-call(s32[2]{0:T(128)S(1)} %pad_add_fusion.me_ref, f32[16,72,128]{2,1,0:T(8,128)S(1)} %pad_maximum_fusion.3.a_own, f32[16,72,128]{2,1,0:T(8,128)S(1)} %collective-permute-done.4.a_other, ...), custom_call_target="tpu_custom_call" | custom-call | flops 1 | bytes 1 | tf_op jit(solution)/shard_map/first/pallas_call | solution.py:401
  56.4 3.8 %first.6.first_ref = f32[4,8,256,128]{3,2,1,0:T(8,128)S(1)} custom-call(s32[2]{0:T(128)S(1)} %pad_add_fusion.me_ref, f32[16,72,128]{2,1,0:T(8,128)S(1)} %pad_maximum_fusion.3.a_own, f32[16,72,128]{2,1,0:T(8,128)S(1)} %collective-permute-done.4.a_other, f32[16,64,128]{2,1,0:T(8,128)S(1)} %pad_maximum_fusion.4.b_own, ...), custom_call_target="tpu_custom_call" | custom-call | flops 1 | bytes 1 | tf_op jit(solution)/shard_map/first/pallas_call | solution.py:401
  60.2 3.8 %first.5.first_ref = f32[4,8,256,128]{3,2,1,0:T(8,128)S(1)} custom-call(s32[2]{0:T(128)S(1)} %pad_add_fusion.me_ref, f32[16,72,128]{2,1,0:T(8,128)S(1)} %pad_maximum_fusion.3.a_own, f32[16,72,128]{2,1,0:T(8,128)S(1)} %collective-permute-done.4.a_other, f32[16,64,128]{2,1,0:T(8,128)S(1)} %pad_maximum_fusion.4.b_own, ...), custom_call_target="tpu_custom_call" | custom-call | flops 1 | bytes 1 | tf_op jit(solution)/shard_map/first/pallas_call | solution.py:401
  68.9 4.0 %first.7.first_ref = f32[4,8,256,128]{3,2,1,0:T(8,128)S(1)} custom-call(s32[2]{0:T(128)S(1)} %pad_add_fusion.me_ref, f32[16,72,128]{2,1,0:T(8,128)S(1)} %pad_maximum_fusion.3.a_own, f32[16,72,128]{2,1,0:T(8,128)S(1)} %collective-permute-done.4.a_other, f32[16,64,128]{2,1,0:T(8,128)S(1)} %pad_maximum_fusion.4.b_own, ...), custom_call_target="tpu_custom_call" | custom-call | flops 1 | bytes 1 | tf_op jit(solution)/shard_map/first/pallas_call | solution.py:401
  73.5 4.1 %mix.4.refs_0_ = f32[4,8,256,128]{3,2,1,0:T(8,128)S(1)} custom-call(s32[2]{0:T(128)S(1)} %pad_add_fusion.me_ref, f32[4,8,256,128]{3,2,1,0:T(8,128)S(1)} %get-tuple-element.28.first_ref, f32[8,128,128]{2,1,0:T(8,128)S(1)} %pad_maximum_fusion.6.refs_0_, f32[8,128,128]{2,1,0:T(8,128)S(1)} %collective-permute-done.15.refs_1_, ...), custom_call_target="tpu_custom_call", output_to_operand_aliasing={{}: (1, {})} | custom-call | flops 1 | bytes 1 | tf_op jit(solution)/shard_map/mix/pallas_call | solution.py:413
  77.6 4.1 %mix.5.refs_1_ = f32[4,8,256,128]{3,2,1,0:T(8,128)S(1)} custom-call(s32[2]{0:T(128)S(1)} %pad_add_fusion.me_ref, f32[4,8,256,128]{3,2,1,0:T(8,128)S(1)} %first.5.first_ref, f32[8,128,128]{2,1,0:T(8,128)S(1)} %pad_maximum_fusion.6.refs_0_, f32[8,128,128]{2,1,0:T(8,128)S(1)} %collective-permute-done.15.refs_1_, ...), custom_call_target="tpu_custom_call", output_to_operand_aliasing={{}: (1, {})} | custom-call | flops 1 | bytes 1 | tf_op jit(solution)/shard_map/mix/pallas_call | solution.py:413
  81.7 4.1 %mix.6.refs_2_ = f32[4,8,256,128]{3,2,1,0:T(8,128)S(1)} custom-call(s32[2]{0:T(128)S(1)} %pad_add_fusion.me_ref, f32[4,8,256,128]{3,2,1,0:T(8,128)S(1)} %first.6.first_ref, f32[8,128,128]{2,1,0:T(8,128)S(1)} %pad_maximum_fusion.6.refs_0_, f32[8,128,128]{2,1,0:T(8,128)S(1)} %collective-permute-done.15.refs_1_, ...), custom_call_target="tpu_custom_call", output_to_operand_aliasing={{}: (1, {})} | custom-call | flops 1 | bytes 1 | tf_op jit(solution)/shard_map/mix/pallas_call | solution.py:413
  85.8 4.3 %mix.7.refs_3_ = f32[4,8,256,128]{3,2,1,0:T(8,128)S(1)} custom-call(s32[2]{0:T(128)S(1)} %pad_add_fusion.me_ref, f32[4,8,256,128]{3,2,1,0:T(8,128)S(1)} %first.7.first_ref, f32[8,128,128]{2,1,0:T(8,128)S(1)} %pad_maximum_fusion.6.refs_0_, f32[8,128,128]{2,1,0:T(8,128)S(1)} %collective-permute-done.15.refs_1_, ...), custom_call_target="tpu_custom_call", output_to_operand_aliasing={{}: (1, {})} | custom-call | flops 1 | bytes 1 | tf_op jit(solution)/shard_map/mix/pallas_call | solution.py:413
  90.8 1.7 %collective-permute-done.25.refs_9_ = f32[8,192,128]{2,1,0:T(8,128)S(1)} collective-permute-done((f32[8,192,128]{2,1,0:T(8,128)S(1)}, f32[8,192,128]{2,1,0:T(8,128)S(1)}, u32[]{:S(2)}, u32[]{:S(2)}) %collective-permute-start.25) | collective-permute-done | bytes 786464 | tf_op jit(solution)/shard_map/ppermute | solution.py:36
  93.7 15.2 %head.1 = (f32[8,128]{1,0:T(8,128)S(1)}, f32[16,128,128]{2,1,0:T(8,128)S(1)}, f32[16,128,128]{2,1,0:T(8,128)S(1)}) custom-call(s32[2]{0:T(128)S(1)} %pad_add_fusion.me_ref, f32[8]{0:T(128)S(1)} %dynamic_slice.30.target_ref, f32[4,8,256,128]{3,2,1,0:T(8,128)S(1)} %mix.4.refs_0_, f32[4,8,256,128]{3,2,1,0:T(8,128)S(1)} %mix.5.refs_1_, ...), custom_call_target="tpu_custom_call" | custom-call | tf_op jit(solution)/shard_map/head/pallas_call | solution.py:509
  109.4 2.3 %collective-permute-done.28 = f32[16,128,128]{2,1,0:T(8,128)S(1)} collective-permute-done((f32[16,128,128]{2,1,0:T(8,128)S(1)}, f32[16,128,128]{2,1,0:T(8,128)S(1)}, u32[]{:S(2)}, u32[]{:S(2)}) %collective-permute-start.28) | collective-permute-done | bytes 1048608 | tf_op jit(solution)/shard_map/ppermute | solution.py:36
  113.0 1.5 %collective-permute-start.29 = (f32[520,128]{1,0:T(8,128)S(1)}, f32[520,128]{1,0:T(8,128)S(1)}, u32[]{:S(2)}, u32[]{:S(2)}) collective-permute-start(f32[520,128]{1,0:T(8,128)S(1)} %pad_maximum_fusion.11), channel_id=1, source_target_pairs={{0,2},{2,0},{4,6},{6,4},{8,10},{10,8},{12,14},{14,12},{16,18},{18,... | collective-permute-start | bytes 798728 | tf_op jit(solution)/shard_map/ppermute | solution.py:36
  114.4 6.1 %collective-permute-done.31 = f32[512,128]{1,0:T(8,128)S(1)} collective-permute-done((f32[512,128]{1,0:T(8,128)S(1)}, f32[512,128]{1,0:T(8,128)S(1)}, u32[]{:S(2)}, u32[]{:S(2)}) %collective-permute-start.31) | collective-permute-done | bytes 262176 | tf_op jit(solution)/shard_map/ppermute | solution.py:36
  120.5 1.5 %collective-permute-start.32 = (f32[256,128]{1,0:T(8,128)S(1)}, f32[256,128]{1,0:T(8,128)S(1)}, u32[]{:S(2)}, u32[]{:S(2)}) collective-permute-start(f32[256,128]{1,0:T(8,128)S(1)} %bitcast.103), channel_id=1, source_target_pairs={{0,2},{2,0},{4,6},{6,4},{8,10},{10,8},{12,14},{14,12},{16,18},{18,... | collective-permute-start | bytes 393224 | tf_op jit(solution)/shard_map/ppermute | solution.py:36
  123.2 2.4 %collective-permute-done.32 = f32[256,128]{1,0:T(8,128)S(1)} collective-permute-done((f32[256,128]{1,0:T(8,128)S(1)}, f32[256,128]{1,0:T(8,128)S(1)}, u32[]{:S(2)}, u32[]{:S(2)}) %collective-permute-start.32) | collective-permute-done | bytes 131104 | tf_op jit(solution)/shard_map/ppermute | solution.py:36
  125.6 1.7 %collective-permute-done.30 = f32[264,128]{1,0:T(8,128)S(1)} collective-permute-done((f32[264,128]{1,0:T(8,128)S(1)}, f32[264,128]{1,0:T(8,128)S(1)}, u32[]{:S(2)}, u32[]{:S(2)}) %collective-permute-start.30) | collective-permute-done | bytes 135200 | tf_op jit(solution)/shard_map/ppermute | solution.py:36
  127.4 1.8 %collective-permute-start.33 = (f32[264,128]{1,0:T(8,128)S(1)}, f32[264,128]{1,0:T(8,128)S(1)}, u32[]{:S(2)}, u32[]{:S(2)}) collective-permute-start(f32[264,128]{1,0:T(8,128)S(1)} %pad_maximum_fusion.16), channel_id=1, source_target_pairs={{0,8},{2,10},{4,12},{6,14},{8,0},{10,2},{12,4},{14,6},{16,24},{18,... | collective-permute-start | bytes 405512 | tf_op jit(solution)/shard_map/ppermute | solution.py:36
  129.2 3.3 %collective-permute-done.33 = f32[264,128]{1,0:T(8,128)S(1)} collective-permute-done((f32[264,128]{1,0:T(8,128)S(1)}, f32[264,128]{1,0:T(8,128)S(1)}, u32[]{:S(2)}, u32[]{:S(2)}) %collective-permute-start.33) | collective-permute-done | bytes 135200 | tf_op jit(solution)/shard_map/ppermute | solution.py:36
  132.5 2.1 %collective-permute-start.34 = (f32[136,128]{1,0:T(8,128)S(1)}, f32[136,128]{1,0:T(8,128)S(1)}, u32[]{:S(2)}, u32[]{:S(2)}) collective-permute-start(f32[136,128]{1,0:T(8,128)S(1)} %pad_maximum_fusion.18), channel_id=1, source_target_pairs={{0,16},{2,18},{4,20},{6,22},{8,24},{10,26},{12,28},{14,30},{16,0},... | collective-permute-start | bytes 208904 | tf_op jit(solution)/shard_map/ppermute | solution.py:36
  134.7 3.1 %collective-permute-done.34 = f32[136,128]{1,0:T(8,128)S(1)} collective-permute-done((f32[136,128]{1,0:T(8,128)S(1)}, f32[136,128]{1,0:T(8,128)S(1)}, u32[]{:S(2)}, u32[]{:S(2)}) %collective-permute-start.34) | collective-permute-done | bytes 69664 | tf_op jit(solution)/shard_map/ppermute | solution.py:36
  (141 shorter events, 26.6 us)
Async XLA Ops:
  3.6 8.3 %collective-permute-start = (f32[1,136,128]{2,1,0:T(8,128)S(1)}, f32[1,136,128]{2,1,0:T(8,128)S(1)}, u32[]{:S(2)}, u32[]{:S(2)}) collective-permute-start(f32[1,136,128]{2,1,0:T(8,128)S(1)} %maximum_bitcast_fusion.1), channel_id=1, source_target_pairs={{0,16},{2,18},{4,20},{6,22},{8,24},{10,26},{12,28},{14,30},{16,0},... | collective-permute-start | bytes 208904 | tf_op jit(solution)/shard_map/ppermute | solution.py:36
  11.1 10.5 %collective-permute-start.8 = (f32[1,256,128]{2,1,0:T(8,128)S(1)}, f32[1,256,128]{2,1,0:T(8,128)S(1)}, u32[]{:S(2)}, u32[]{:S(2)}) collective-permute-start(f32[1,256,128]{2,1,0:T(8,128)S(1)} %maximum_bitcast_fusion), channel_id=1, source_target_pairs={{0,16},{2,18},{4,20},{6,22},{8,24},{10,26},{12,28},{14,30},{16,0},... | collective-permute-start | bytes 393224 | tf_op jit(solution)/shard_map/ppermute | solution.py:36
  12.0 7.6 %collective-permute-start.1 = (f32[2,136,128]{2,1,0:T(8,128)S(1)}, f32[2,136,128]{2,1,0:T(8,128)S(1)}, u32[]{:S(2)}, u32[]{:S(2)}) collective-permute-start(f32[2,136,128]{2,1,0:T(8,128)S(1)} %pad_maximum_fusion.14), channel_id=1, source_target_pairs={{0,8},{2,10},{4,12},{6,14},{8,0},{10,2},{12,4},{14,6},{16,24},{18,... | collective-permute-start | bytes 417800 | tf_op jit(solution)/shard_map/ppermute | solution.py:36
  19.7 7.9 %collective-permute-start.5 = (f32[4,64,128]{2,1,0:T(8,128)S(1)}, f32[4,64,128]{2,1,0:T(8,128)S(1)}, u32[]{:S(2)}, u32[]{:S(2)}) collective-permute-start(f32[4,64,128]{2,1,0:T(8,128)S(1)} %slice.194), channel_id=1, source_target_pairs={{0,2},{2,0},{4,6},{6,4},{8,10},{10,8},{12,14},{14,12},{16,18},{18,... | collective-permute-start | bytes 393224 | tf_op jit(solution)/shard_map/ppermute | solution.py:36
  21.6 10.1 %collective-permute-start.9 = (f32[2,256,128]{2,1,0:T(8,128)S(1)}, f32[2,256,128]{2,1,0:T(8,128)}, u32[]{:S(2)}, u32[]{:S(2)}) collective-permute-start(f32[2,256,128]{2,1,0:T(8,128)S(1)} %pad_maximum_fusion.13), channel_id=1, source_target_pairs={{0,8},{2,10},{4,12},{6,14},{8,0},{10,2},{12,4},{14,6},{16,24},{18,... | collective-permute-start | bytes 786440 | tf_op jit(solution)/shard_map/ppermute | solution.py:36
  21.7 6.4 %collective-permute-start.2 = (f32[4,72,128]{2,1,0:T(8,128)S(1)}, f32[4,72,128]{2,1,0:T(8,128)S(1)}, u32[]{:S(2)}, u32[]{:S(2)}) collective-permute-start(f32[4,72,128]{2,1,0:T(8,128)S(1)} %slice.193), channel_id=1, source_target_pairs={{0,4},{2,6},{4,0},{6,2},{8,12},{10,14},{12,8},{14,10},{16,20},{18,... | collective-permute-start | bytes 442376 | tf_op jit(solution)/shard_map/ppermute | solution.py:36
  23.5 12.0 %collective-permute-start.11 = (f32[1,384,128]{2,1,0:T(8,128)S(1)}, f32[1,384,128]{2,1,0:T(8,128)S(1)}, u32[]{:S(2)}, u32[]{:S(2)}) collective-permute-start(f32[1,384,128]{2,1,0:T(8,128)S(1)} %bitcast.88), channel_id=1, source_target_pairs={{0,16},{2,18},{4,20},{6,22},{8,24},{10,26},{12,28},{14,30},{16,0},... | collective-permute-start | bytes 589832 | tf_op jit(solution)/shard_map/ppermute | solution.py:36
  27.6 10.8 %collective-permute-start.6 = (f32[8,64,128]{2,1,0:T(8,128)S(1)}, f32[8,64,128]{2,1,0:T(8,128)S(1)}, u32[]{:S(2)}, u32[]{:S(2)}) collective-permute-start(f32[8,64,128]{2,1,0:T(8,128)S(1)} %pad_maximum_fusion.12), channel_id=1, source_target_pairs={{0,4},{2,6},{4,0},{6,2},{8,12},{10,14},{12,8},{14,10},{16,20},{18,... | collective-permute-start | bytes 786440 | tf_op jit(solution)/shard_map/ppermute | solution.py:36
  28.2 10.3 %collective-permute-start.3 = (f32[8,72,128]{2,1,0:T(8,128)S(1)}, f32[8,72,128]{2,1,0:T(8,128)S(1)}, u32[]{:S(2)}, u32[]{:S(2)}) collective-permute-start(f32[8,72,128]{2,1,0:T(8,128)S(1)} %pad_maximum_fusion.9), channel_id=1, source_target_pairs={{0,2},{2,0},{4,6},{6,4},{8,10},{10,8},{12,14},{14,12},{16,18},{18,... | collective-permute-start | bytes 884744 | tf_op jit(solution)/shard_map/ppermute | solution.py:36
  35.5 8.1 %collective-permute-start.12 = (f32[2,384,128]{2,1,0:T(8,128)S(1)}, f32[2,384,128]{2,1,0:T(8,128)S(1)}, u32[]{:S(2)}, u32[]{:S(2)}) collective-permute-start(f32[2,384,128]{2,1,0:T(8,128)S(1)} %pad_maximum_fusion.8), channel_id=1, source_target_pairs={{0,8},{2,10},{4,12},{6,14},{8,0},{10,2},{12,4},{14,6},{16,24},{18,... | collective-permute-start | bytes 1179656 | tf_op jit(solution)/shard_map/ppermute | solution.py:36
  36.4 12.1 %collective-permute-start.10 = (f32[4,128,128]{2,1,0:T(8,128)}, f32[4,128,128]{2,1,0:T(8,128)}, u32[]{:S(2)}, u32[]{:S(2)}) collective-permute-start(f32[4,128,128]{2,1,0:T(8,128)} %get-tuple-element.31), channel_id=1, source_target_pairs={{0,4},{2,6},{4,0},{6,2},{8,12},{10,14},{12,8},{14,10},{16,20},{18,... | collective-permute-start | bytes 786440 | tf_op jit(solution)/shard_map/ppermute | solution.py:36
  37.8 7.5 %collective-permute-start.16 = (f32[4,128,128]{2,1,0:T(8,128)S(1)}, f32[4,128,128]{2,1,0:T(8,128)}, u32[]{:S(2)}, u32[]{:S(2)}) collective-permute-start(f32[4,128,128]{2,1,0:T(8,128)S(1)} %get-tuple-element.41), channel_id=1, source_target_pairs={{0,2},{2,0},{4,6},{6,4},{8,10},{10,8},{12,14},{14,12},{16,18},{18,... | collective-permute-start | bytes 786440 | tf_op jit(solution)/shard_map/ppermute | solution.py:36
  38.4 11.2 %collective-permute-start.7 = (f32[16,64,128]{2,1,0:T(8,128)S(1)}, f32[16,64,128]{2,1,0:T(8,128)S(1)}, u32[]{:S(2)}, u32[]{:S(2)}) collective-permute-start(f32[16,64,128]{2,1,0:T(8,128)S(1)} %pad_maximum_fusion.4.b_own), channel_id=1, source_target_pairs={{0,1},{1,0},{2,3},{3,2},{4,5},{5,4},{6,7},{7,6},{8,9},{9,8},{10,11... | collective-permute-start | bytes 1572872 | tf_op jit(solution)/shard_map/ppermute | solution.py:36
  38.5 12.1 %collective-permute-start.4 = (f32[16,72,128]{2,1,0:T(8,128)S(1)}, f32[16,72,128]{2,1,0:T(8,128)S(1)}, u32[]{:S(2)}, u32[]{:S(2)}) collective-permute-start(f32[16,72,128]{2,1,0:T(8,128)S(1)} %pad_maximum_fusion.3.a_own), channel_id=1, source_target_pairs={{0,1},{1,0},{2,3},{3,2},{4,5},{5,4},{6,7},{7,6},{8,9},{9,8},{10,11... | collective-permute-start | bytes 1769480 | tf_op jit(solution)/shard_map/ppermute | solution.py:36
  44.6 19.4 %collective-permute-start.14 = (f32[4,192,128]{2,1,0:T(8,128)}, f32[4,192,128]{2,1,0:T(8,128)}, u32[]{:S(2)}, u32[]{:S(2)}) collective-permute-start(f32[4,192,128]{2,1,0:T(8,128)} %get-tuple-element.58), channel_id=1, source_target_pairs={{0,2},{2,0},{4,6},{6,4},{8,10},{10,8},{12,14},{14,12},{16,18},{18,... | collective-permute-start | bytes 1179656 | tf_op jit(solution)/shard_map/ppermute | solution.py:36
  45.3 18.8 %collective-permute-start.13 = (f32[4,192,128]{2,1,0:T(8,128)}, f32[4,192,128]{2,1,0:T(8,128)}, u32[]{:S(2)}, u32[]{:S(2)}) collective-permute-start(f32[4,192,128]{2,1,0:T(8,128)} %get-tuple-element.59), channel_id=1, source_target_pairs={{0,4},{2,6},{4,0},{6,2},{8,12},{10,14},{12,8},{14,10},{16,20},{18,... | collective-permute-start | bytes 1179656 | tf_op jit(solution)/shard_map/ppermute | solution.py:36
  48.4 20.4 %collective-permute-start.20 = (f32[8,128,128]{2,1,0:T(8,128)S(1)}, f32[8,128,128]{2,1,0:T(8,128)S(1)}, u32[]{:S(2)}, u32[]{:S(2)}) collective-permute-start(f32[8,128,128]{2,1,0:T(8,128)S(1)} %pad_maximum_fusion.7.refs_4_), channel_id=1, source_target_pairs={{0,1},{1,0},{2,3},{3,2},{4,5},{5,4},{6,7},{7,6},{8,9},{9,8},{10,11... | collective-permute-start | bytes 1572872 | tf_op jit(solution)/shard_map/ppermute | solution.py:36
  49.6 18.7 %collective-permute-start.17 = (f32[8,128,128]{2,1,0:T(8,128)S(1)}, f32[8,128,128]{2,1,0:T(8,128)S(1)}, u32[]{:S(2)}, u32[]{:S(2)}) collective-permute-start(f32[8,128,128]{2,1,0:T(8,128)S(1)} %pad_maximum_fusion.7.refs_4_), channel_id=1, source_target_pairs={{0,4},{2,6},{4,0},{6,2},{8,12},{10,14},{12,8},{14,10},{16,20},{18,... | collective-permute-start | bytes 1572872 | tf_op jit(solution)/shard_map/ppermute | solution.py:36
  50.7 17.6 %collective-permute-start.15 = (f32[8,128,128]{2,1,0:T(8,128)S(1)}, f32[8,128,128]{2,1,0:T(8,128)S(1)}, u32[]{:S(2)}, u32[]{:S(2)}) collective-permute-start(f32[8,128,128]{2,1,0:T(8,128)S(1)} %pad_maximum_fusion.6.refs_0_), channel_id=1, source_target_pairs={{0,2},{2,0},{4,6},{6,4},{8,10},{10,8},{12,14},{14,12},{16,18},{18,... | collective-permute-start | bytes 1572872 | tf_op jit(solution)/shard_map/ppermute | solution.py:36
  65.3 24.9 %collective-permute-start.22 = (f32[8,192,128]{2,1,0:T(8,128)S(1)}, f32[8,192,128]{2,1,0:T(8,128)S(1)}, u32[]{:S(2)}, u32[]{:S(2)}) collective-permute-start(f32[8,192,128]{2,1,0:T(8,128)S(1)} %pad_maximum_fusion.1.refs_4_), channel_id=1, source_target_pairs={{0,2},{2,0},{4,6},{6,4},{8,10},{10,8},{12,14},{14,12},{16,18},{18,... | collective-permute-start | bytes 2359304 | tf_op jit(solution)/shard_map/ppermute | solution.py:36
  67.2 23.5 %collective-permute-start.23 = (f32[8,192,128]{2,1,0:T(8,128)S(1)}, f32[8,192,128]{2,1,0:T(8,128)S(1)}, u32[]{:S(2)}, u32[]{:S(2)}) collective-permute-start(f32[8,192,128]{2,1,0:T(8,128)S(1)} %pad_maximum_fusion.2.refs_6_), channel_id=1, source_target_pairs={{0,4},{2,6},{4,0},{6,2},{8,12},{10,14},{12,8},{14,10},{16,20},{18,... | collective-permute-start | bytes 2359304 | tf_op jit(solution)/shard_map/ppermute | solution.py:36
  68.3 4.6 %collective-permute-start.18 = (f32[8,128,128]{2,1,0:T(8,128)S(1)}, f32[8,128,128]{2,1,0:T(8,128)S(1)}, u32[]{:S(2)}, u32[]{:S(2)}) collective-permute-start(f32[8,128,128]{2,1,0:T(8,128)S(1)} %pad_maximum_fusion.6.refs_0_), channel_id=1, source_target_pairs={{0,1},{1,0},{2,3},{3,2},{4,5},{5,4},{6,7},{7,6},{8,9},{9,8},{10,11... | collective-permute-start | bytes 1572872 | tf_op jit(solution)/shard_map/ppermute | solution.py:36
  68.3 5.1 %collective-permute-start.19 = (f32[8,128,128]{2,1,0:T(8,128)S(1)}, f32[8,128,128]{2,1,0:T(8,128)S(1)}, u32[]{:S(2)}, u32[]{:S(2)}) collective-permute-start(f32[8,128,128]{2,1,0:T(8,128)S(1)} %collective-permute-done.15.refs_1_), channel_id=1, source_target_pairs={{0,1},{1,0},{2,3},{3,2},{4,5},{5,4},{6,7},{7,6},{8,9},{9,8},{10,11... | collective-permute-start | bytes 1572872 | tf_op jit(solution)/shard_map/ppermute | solution.py:36
  68.8 4.7 %collective-permute-start.21 = (f32[8,128,128]{2,1,0:T(8,128)S(1)}, f32[8,128,128]{2,1,0:T(8,128)S(1)}, u32[]{:S(2)}, u32[]{:S(2)}) collective-permute-start(f32[8,128,128]{2,1,0:T(8,128)S(1)} %collective-permute-done.17.refs_5_), channel_id=1, source_target_pairs={{0,1},{1,0},{2,3},{3,2},{4,5},{5,4},{6,7},{7,6},{8,9},{9,8},{10,11... | collective-permute-start | bytes 1572872 | tf_op jit(solution)/shard_map/ppermute | solution.py:36
  72.9 18.0 %collective-permute-start.24 = (f32[8,192,128]{2,1,0:T(8,128)S(1)}, f32[8,192,128]{2,1,0:T(8,128)S(1)}, u32[]{:S(2)}, u32[]{:S(2)}) collective-permute-start(f32[8,192,128]{2,1,0:T(8,128)S(1)} %pad_maximum_fusion.1.refs_4_), channel_id=1, source_target_pairs={{0,1},{1,0},{2,3},{3,2},{4,5},{5,4},{6,7},{7,6},{8,9},{9,8},{10,11... | collective-permute-start | bytes 2359304 | tf_op jit(solution)/shard_map/ppermute | solution.py:36
  73.4 17.5 %collective-permute-start.26 = (f32[8,192,128]{2,1,0:T(8,128)S(1)}, f32[8,192,128]{2,1,0:T(8,128)S(1)}, u32[]{:S(2)}, u32[]{:S(2)}) collective-permute-start(f32[8,192,128]{2,1,0:T(8,128)S(1)} %pad_maximum_fusion.2.refs_6_), channel_id=1, source_target_pairs={{0,1},{1,0},{2,3},{3,2},{4,5},{5,4},{6,7},{7,6},{8,9},{9,8},{10,11... | collective-permute-start | bytes 2359304 | tf_op jit(solution)/shard_map/ppermute | solution.py:36
  111.8 8.7 %collective-permute-start.31 = (f32[512,128]{1,0:T(8,128)S(1)}, f32[512,128]{1,0:T(8,128)S(1)}, u32[]{:S(2)}, u32[]{:S(2)}) collective-permute-start(f32[512,128]{1,0:T(8,128)S(1)} %bitcast.98), channel_id=1, source_target_pairs={{0,4},{2,6},{4,0},{6,2},{8,12},{10,14},{12,8},{14,10},{16,20},{18,... | collective-permute-start | bytes 786440 | tf_op jit(solution)/shard_map/ppermute | solution.py:36
  113.0 9.1 %collective-permute-start.29 = (f32[520,128]{1,0:T(8,128)S(1)}, f32[520,128]{1,0:T(8,128)S(1)}, u32[]{:S(2)}, u32[]{:S(2)}) collective-permute-start(f32[520,128]{1,0:T(8,128)S(1)} %pad_maximum_fusion.11), channel_id=1, source_target_pairs={{0,2},{2,0},{4,6},{6,4},{8,10},{10,8},{12,14},{14,12},{16,18},{18,... | collective-permute-start | bytes 798728 | tf_op jit(solution)/shard_map/ppermute | solution.py:36
  120.5 5.0 %collective-permute-start.32 = (f32[256,128]{1,0:T(8,128)S(1)}, f32[256,128]{1,0:T(8,128)S(1)}, u32[]{:S(2)}, u32[]{:S(2)}) collective-permute-start(f32[256,128]{1,0:T(8,128)S(1)} %bitcast.103), channel_id=1, source_target_pairs={{0,2},{2,0},{4,6},{6,4},{8,10},{10,8},{12,14},{14,12},{16,18},{18,... | collective-permute-start | bytes 393224 | tf_op jit(solution)/shard_map/ppermute | solution.py:36
  122.2 5.1 %collective-permute-start.30 = (f32[264,128]{1,0:T(8,128)S(1)}, f32[264,128]{1,0:T(8,128)S(1)}, u32[]{:S(2)}, u32[]{:S(2)}) collective-permute-start(f32[264,128]{1,0:T(8,128)S(1)} %pad_maximum_fusion.15), channel_id=1, source_target_pairs={{0,4},{2,6},{4,0},{6,2},{8,12},{10,14},{12,8},{14,10},{16,20},{18,... | collective-permute-start | bytes 405512 | tf_op jit(solution)/shard_map/ppermute | solution.py:36
  127.4 5.1 %collective-permute-start.33 = (f32[264,128]{1,0:T(8,128)S(1)}, f32[264,128]{1,0:T(8,128)S(1)}, u32[]{:S(2)}, u32[]{:S(2)}) collective-permute-start(f32[264,128]{1,0:T(8,128)S(1)} %pad_maximum_fusion.16), channel_id=1, source_target_pairs={{0,8},{2,10},{4,12},{6,14},{8,0},{10,2},{12,4},{14,6},{16,24},{18,... | collective-permute-start | bytes 405512 | tf_op jit(solution)/shard_map/ppermute | solution.py:36
  132.5 5.3 %collective-permute-start.34 = (f32[136,128]{1,0:T(8,128)S(1)}, f32[136,128]{1,0:T(8,128)S(1)}, u32[]{:S(2)}, u32[]{:S(2)}) collective-permute-start(f32[136,128]{1,0:T(8,128)S(1)} %pad_maximum_fusion.18), channel_id=1, source_target_pairs={{0,16},{2,18},{4,20},{6,22},{8,24},{10,26},{12,28},{14,30},{16,0},... | collective-permute-start | bytes 208904 | tf_op jit(solution)/shard_map/ppermute | solution.py:36
  (12 other events, 107.4 us)

commit v7 on v6

--- a/solution.py
+++ b/solution.py
@@ -336,8 +336,8 @@
     per_chunk = CHUNK // mine
 
     def half(values):
-        parts = values.reshape((rows_size, values.shape[0] // rows_size) + values.shape[1:])
-        return lax.dynamic_index_in_dim(parts, core, 0, False)
+        size = values.shape[0] // rows_size
+        return lax.dynamic_slice_in_dim(values, core * size, size, 0)
 
     def rows_of(*vectors):
         return jnp.concatenate([half(v) for v in vectors]).reshape(len(vectors), mine, LANES)
@@ -490,9 +490,11 @@
         m_all[0] = after(m_all[0], first[3])
         spread = []
         for k, x in zip(cuts, first):
+            if k == cuts[3]:
+                l_step = [after(x, spread[-1]) for x in l_step]
+                m_all[0] = after(m_all[0], *l_step)
             spread.append(mix(k, x, m_all))
             m_all[0] = after(m_all[0], spread[-1])
-        l_step = [after(x, spread[-1]) for x in l_step]
         l_all = []
         for held, got, core_held in zip(l_pair, l_step, l_core):
             l_all += [held, got, core_held, swap(got, "rows", 1)]

time: 139 us -> 136 us (0.978)
  starting transfers between devices: 34.8 us -> 33.2 us
    reshape x5 -> x0, local copies, waits for them, and re-layouts: 2.25 us -> none  [half(): values.reshape((rows_size, values.shape[0] // rows_size) + values.shape[1:])]
    ppermute x35, starting transfers between devices: 34.8 us -> 33.2 us  [swap(): return lax.ppermute(values, axis_name, [(i, i ^ bit) for i in range(size)])]
  transfers between devices with their start and end apart: 35 -> 35, of which waited for: 12 -> 12; matrix products, arithmetic and copies ran while one was open for 9% -> 10% of each run, Pallas kernels for 23% -> 24%
where the time goes in v7:
time: 136 us; the launch traced here: 135 us
  Pallas kernels  48 us (35%)
  waiting for transfers between devices  36.6 us (27%)
  starting transfers between devices  33.2 us (24%)
  other arithmetic  8.27 us (6%)
  local copies, waits for them, and re-layouts  4.62 us (3%)
  matrix products  3.37 us (2%)
    ppermute x35, waiting for transfers between devices, swap(): return lax.ppermute(values, axis_name, [(i, i ^ bit) for i in range(size)])  36.6 us
    ppermute x35, starting transfers between devices, swap(): return lax.ppermute(values, axis_name, [(i, i ^ bit) for i in range(size)])  33.2 us
    pallas_call x4, Pallas kernels, mix(): pl.pallas_call(functools.partial(mix_kernel, rows, begin, group, bits_a,...  16.6 us
    pallas_call x4, Pallas kernels, first_of(): pl.pallas_call(functools.partial(first_kernel, rows, begin, group, bits_a...  16.1 us
    pallas_call x1, Pallas kernels, local(): pl.pallas_call(functools.partial(head_kernel, rows, turn_sine_coefficient...  15.2 us
    concatenate x14, other arithmetic, join(): jnp.concatenate([held, after(got, *others) if others else got], axis=0)  5.71 us
    dot_general x1, matrix products, local(): jnp.einsum('bij,j->bi', half(block_permutations), jnp.arange(LANES).astyp...  3.37 us
  transfers between devices with their start and end apart: 35, of which 12 were waited for; matrix products, arithmetic and copies ran while one was open for 10% of the time, Pallas kernels for 24%

profile of v7, /device:TPU:0, one launch (start us, length us, event | category | flops | bytes accessed | tf_op | source)
XLA Modules:
  0.0 135.3 jit_solution(2762485760222622756)
XLA Ops:
  2.4 4.1 %collective-permute-start = (f32[1,136,128]{2,1,0:T(8,128)S(1)}, f32[1,136,128]{2,1,0:T(8,128)S(1)}, u32[]{:S(2)}, u32[]{:S(2)}) collective-permute-start(f32[1,136,128]{2,1,0:T(8,128)S(1)} %maximum_bitcast_fusion.1), channel_id=1, source_target_pairs={{0,16},{2,18},{4,20},{6,22},{8,24},{10,26},{12,28},{14,30},{16,0},... | collective-permute-start | bytes 208904 | tf_op jit(solution)/shard_map/ppermute | solution.py:36
  6.5 3.4 %fusion = f32[1,128,128]{2,0,1:T(1,128)S(1)} fusion(bf16[256,128,128]{2,1,0:T(8,128)(2,1)} %param.18, s32[]{:T(128)S(6)} %select_n.8), kind=kOutput, calls=%fused_computation | convolution fusion | flops 4194432 | bytes 4259844 | tf_op jit(solution)/shard_map/bij,j->bi/dot_general | solution.py:345
  10.3 1.8 %collective-permute-start.1 = (f32[2,136,128]{2,1,0:T(8,128)S(1)}, f32[2,136,128]{2,1,0:T(8,128)S(1)}, u32[]{:S(2)}, u32[]{:S(2)}) collective-permute-start(f32[2,136,128]{2,1,0:T(8,128)S(1)} %pad_maximum_fusion.14), channel_id=1, source_target_pairs={{0,8},{2,10},{4,12},{6,14},{8,0},{10,2},{12,4},{14,6},{16,24},{18,... | collective-permute-start | bytes 417800 | tf_op jit(solution)/shard_map/ppermute | solution.py:36
  12.1 5.2 %collective-permute-done.1 = f32[2,136,128]{2,1,0:T(8,128)S(1)} collective-permute-done((f32[2,136,128]{2,1,0:T(8,128)S(1)}, f32[2,136,128]{2,1,0:T(8,128)S(1)}, u32[]{:S(2)}, u32[]{:S(2)}) %collective-permute-start.1) | collective-permute-done | bytes 139296 | tf_op jit(solution)/shard_map/ppermute | solution.py:36
  17.3 1.6 %collective-permute-start.5 = (f32[4,64,128]{2,1,0:T(8,128)S(1)}, f32[4,64,128]{2,1,0:T(8,128)S(1)}, u32[]{:S(2)}, u32[]{:S(2)}) collective-permute-start(f32[4,64,128]{2,1,0:T(8,128)S(1)} %slice.236), channel_id=1, source_target_pairs={{0,2},{2,0},{4,6},{6,4},{8,10},{10,8},{12,14},{14,12},{16,18},{18,... | collective-permute-start | bytes 393224 | tf_op jit(solution)/shard_map/ppermute | solution.py:36
  20.0 1.6 %collective-permute-start.2 = (f32[4,72,128]{2,1,0:T(8,128)S(1)}, f32[4,72,128]{2,1,0:T(8,128)S(1)}, u32[]{:S(2)}, u32[]{:S(2)}) collective-permute-start(f32[4,72,128]{2,1,0:T(8,128)S(1)} %slice.235), channel_id=1, source_target_pairs={{0,4},{2,6},{4,0},{6,2},{8,12},{10,14},{12,8},{14,10},{16,20},{18,... | collective-permute-start | bytes 442376 | tf_op jit(solution)/shard_map/ppermute | solution.py:36
  22.4 4.1 %collective-permute-start.11 = (f32[1,384,128]{2,1,0:T(8,128)S(1)}, f32[1,384,128]{2,1,0:T(8,128)S(1)}, u32[]{:S(2)}, u32[]{:S(2)}) collective-permute-start(f32[1,384,128]{2,1,0:T(8,128)S(1)} %bitcast.99), channel_id=1, source_target_pairs={{0,16},{2,18},{4,20},{6,22},{8,24},{10,26},{12,28},{14,30},{16,0},... | collective-permute-start | bytes 589832 | tf_op jit(solution)/shard_map/ppermute | solution.py:36
  28.8 5.5 %collective-permute-done.11 = f32[1,384,128]{2,1,0:T(8,128)S(1)} collective-permute-done((f32[1,384,128]{2,1,0:T(8,128)S(1)}, f32[1,384,128]{2,1,0:T(8,128)S(1)}, u32[]{:S(2)}, u32[]{:S(2)}) %collective-permute-start.11) | collective-permute-done | bytes 196640 | tf_op jit(solution)/shard_map/ppermute | solution.py:36
  37.4 5.3 %collective-permute-done.12 = f32[2,384,128]{2,1,0:T(8,128)S(1)} collective-permute-done((f32[2,384,128]{2,1,0:T(8,128)S(1)}, f32[2,384,128]{2,1,0:T(8,128)S(1)}, u32[]{:S(2)}, u32[]{:S(2)}) %collective-permute-start.12) | collective-permute-done | bytes 393248 | tf_op jit(solution)/shard_map/ppermute | solution.py:36
  47.7 1.9 %collective-permute-start.17 = (f32[8,128,128]{2,1,0:T(8,128)S(1)}, f32[8,128,128]{2,1,0:T(8,128)S(1)}, u32[]{:S(2)}, u32[]{:S(2)}) collective-permute-start(f32[8,128,128]{2,1,0:T(8,128)S(1)} %pad_maximum_fusion.7.refs_4_), channel_id=1, source_target_pairs={{0,4},{2,6},{4,0},{6,2},{8,12},{10,14},{12,8},{14,10},{16,20},{18,... | collective-permute-start | bytes 1572872 | tf_op jit(solution)/shard_map/ppermute | solution.py:36
  49.6 1.4 %collective-permute-start.15 = (f32[8,128,128]{2,1,0:T(8,128)S(1)}, f32[8,128,128]{2,1,0:T(8,128)S(1)}, u32[]{:S(2)}, u32[]{:S(2)}) collective-permute-start(f32[8,128,128]{2,1,0:T(8,128)S(1)} %pad_maximum_fusion.6.refs_0_), channel_id=1, source_target_pairs={{0,2},{2,0},{4,6},{6,4},{8,10},{10,8},{12,14},{14,12},{16,18},{18,... | collective-permute-start | bytes 1572872 | tf_op jit(solution)/shard_map/ppermute | solution.py:36
  51.1 4.4 %first.4 = (f32[4,8,256,128]{3,2,1,0:T(8,128)S(1)}, bf16[1024,512]{1,0:T(8,128)(2,1)S(1)}, bf16[640,1024]{1,0:T(8,128)(2,1)S(1)}) custom-call(s32[2]{0:T(128)S(1)} %pad_add_fusion.me_ref, f32[16,72,128]{2,1,0:T(8,128)S(1)} %pad_maximum_fusion.3.a_own, f32[16,72,128]{2,1,0:T(8,128)S(1)} %collective-permute-done.4.a_other, ...), custom_call_target="tpu_custom_call" | custom-call | flops 1 | bytes 1 | tf_op jit(solution)/shard_map/first/pallas_call | solution.py:401
  55.5 3.9 %first.6.first_ref = f32[4,8,256,128]{3,2,1,0:T(8,128)S(1)} custom-call(s32[2]{0:T(128)S(1)} %pad_add_fusion.me_ref, f32[16,72,128]{2,1,0:T(8,128)S(1)} %pad_maximum_fusion.3.a_own, f32[16,72,128]{2,1,0:T(8,128)S(1)} %collective-permute-done.4.a_other, f32[16,64,128]{2,1,0:T(8,128)S(1)} %pad_maximum_fusion.4.b_own, ...), custom_call_target="tpu_custom_call" | custom-call | flops 1 | bytes 1 | tf_op jit(solution)/shard_map/first/pallas_call | solution.py:401
  59.3 3.9 %first.5.first_ref = f32[4,8,256,128]{3,2,1,0:T(8,128)S(1)} custom-call(s32[2]{0:T(128)S(1)} %pad_add_fusion.me_ref, f32[16,72,128]{2,1,0:T(8,128)S(1)} %pad_maximum_fusion.3.a_own, f32[16,72,128]{2,1,0:T(8,128)S(1)} %collective-permute-done.4.a_other, f32[16,64,128]{2,1,0:T(8,128)S(1)} %pad_maximum_fusion.4.b_own, ...), custom_call_target="tpu_custom_call" | custom-call | flops 1 | bytes 1 | tf_op jit(solution)/shard_map/first/pallas_call | solution.py:401
  63.2 1.2 pad_maximum_fusion.2.refs_6_
  64.6 1.2 pad_maximum_fusion.1.refs_4_
  67.1 4.0 %first.7.first_ref = f32[4,8,256,128]{3,2,1,0:T(8,128)S(1)} custom-call(s32[2]{0:T(128)S(1)} %pad_add_fusion.me_ref, f32[16,72,128]{2,1,0:T(8,128)S(1)} %pad_maximum_fusion.3.a_own, f32[16,72,128]{2,1,0:T(8,128)S(1)} %collective-permute-done.4.a_other, f32[16,64,128]{2,1,0:T(8,128)S(1)} %pad_maximum_fusion.4.b_own, ...), custom_call_target="tpu_custom_call" | custom-call | flops 1 | bytes 1 | tf_op jit(solution)/shard_map/first/pallas_call | solution.py:401
  71.7 4.1 %mix.4.refs_0_ = f32[4,8,256,128]{3,2,1,0:T(8,128)S(1)} custom-call(s32[2]{0:T(128)S(1)} %pad_add_fusion.me_ref, f32[4,8,256,128]{3,2,1,0:T(8,128)S(1)} %get-tuple-element.29.first_ref, f32[8,128,128]{2,1,0:T(8,128)S(1)} %pad_maximum_fusion.6.refs_0_, f32[8,128,128]{2,1,0:T(8,128)S(1)} %collective-permute-done.15.refs_1_, ...), custom_call_target="tpu_custom_call", output_to_operand_aliasing={{}: (1, {})} | custom-call | flops 1 | bytes 1 | tf_op jit(solution)/shard_map/mix/pallas_call | solution.py:413
  75.8 4.1 %mix.5.refs_1_ = f32[4,8,256,128]{3,2,1,0:T(8,128)S(1)} custom-call(s32[2]{0:T(128)S(1)} %pad_add_fusion.me_ref, f32[4,8,256,128]{3,2,1,0:T(8,128)S(1)} %first.5.first_ref, f32[8,128,128]{2,1,0:T(8,128)S(1)} %pad_maximum_fusion.6.refs_0_, f32[8,128,128]{2,1,0:T(8,128)S(1)} %collective-permute-done.15.refs_1_, ...), custom_call_target="tpu_custom_call", output_to_operand_aliasing={{}: (1, {})} | custom-call | flops 1 | bytes 1 | tf_op jit(solution)/shard_map/mix/pallas_call | solution.py:413
  79.9 4.1 %mix.6.refs_2_ = f32[4,8,256,128]{3,2,1,0:T(8,128)S(1)} custom-call(s32[2]{0:T(128)S(1)} %pad_add_fusion.me_ref, f32[4,8,256,128]{3,2,1,0:T(8,128)S(1)} %first.6.first_ref, f32[8,128,128]{2,1,0:T(8,128)S(1)} %pad_maximum_fusion.6.refs_0_, f32[8,128,128]{2,1,0:T(8,128)S(1)} %collective-permute-done.15.refs_1_, ...), custom_call_target="tpu_custom_call", output_to_operand_aliasing={{}: (1, {})} | custom-call | flops 1 | bytes 1 | tf_op jit(solution)/shard_map/mix/pallas_call | solution.py:413
  84.1 1.2 collective-permute-done.22.refs_5_
  85.8 4.3 %mix.7.refs_3_ = f32[4,8,256,128]{3,2,1,0:T(8,128)S(1)} custom-call(s32[2]{0:T(128)S(1)} %pad_add_fusion.me_ref, f32[4,8,256,128]{3,2,1,0:T(8,128)S(1)} %first.7.first_ref, f32[8,128,128]{2,1,0:T(8,128)S(1)} %pad_maximum_fusion.6.refs_0_, f32[8,128,128]{2,1,0:T(8,128)S(1)} %collective-permute-done.15.refs_1_, ...), custom_call_target="tpu_custom_call", output_to_operand_aliasing={{}: (1, {})} | custom-call | flops 1 | bytes 1 | tf_op jit(solution)/shard_map/mix/pallas_call | solution.py:413
  90.2 15.2 %head.1 = (f32[8,128]{1,0:T(8,128)S(1)}, f32[16,128,128]{2,1,0:T(8,128)S(1)}, f32[16,128,128]{2,1,0:T(8,128)S(1)}) custom-call(s32[2]{0:T(128)S(1)} %pad_add_fusion.me_ref, f32[8]{0:T(128)S(1)} %dynamic_slice.27.target_ref, f32[4,8,256,128]{3,2,1,0:T(8,128)S(1)} %mix.4.refs_0_, f32[4,8,256,128]{3,2,1,0:T(8,128)S(1)} %mix.5.refs_1_, ...), custom_call_target="tpu_custom_call" | custom-call | tf_op jit(solution)/shard_map/head/pallas_call | solution.py:511
  105.5 2.6 %collective-permute-done.28 = f32[16,128,128]{2,1,0:T(8,128)S(1)} collective-permute-done((f32[16,128,128]{2,1,0:T(8,128)S(1)}, f32[16,128,128]{2,1,0:T(8,128)S(1)}, u32[]{:S(2)}, u32[]{:S(2)}) %collective-permute-start.28) | collective-permute-done | bytes 1048608 | tf_op jit(solution)/shard_map/ppermute | solution.py:36
  108.3 1.7 %collective-permute-start.31 = (f32[512,128]{1,0:T(8,128)S(1)}, f32[512,128]{1,0:T(8,128)S(1)}, u32[]{:S(2)}, u32[]{:S(2)}) collective-permute-start(f32[512,128]{1,0:T(8,128)S(1)} %bitcast.109), channel_id=1, source_target_pairs={{0,4},{2,6},{4,0},{6,2},{8,12},{10,14},{12,8},{14,10},{16,20},{18,... | collective-permute-start | bytes 786440 | tf_op jit(solution)/shard_map/ppermute | solution.py:36
  110.8 5.9 %collective-permute-done.31 = f32[512,128]{1,0:T(8,128)S(1)} collective-permute-done((f32[512,128]{1,0:T(8,128)S(1)}, f32[512,128]{1,0:T(8,128)S(1)}, u32[]{:S(2)}, u32[]{:S(2)}) %collective-permute-start.31) | collective-permute-done | bytes 262176 | tf_op jit(solution)/shard_map/ppermute | solution.py:36
  119.6 2.3 %collective-permute-done.32 = f32[256,128]{1,0:T(8,128)S(1)} collective-permute-done((f32[256,128]{1,0:T(8,128)S(1)}, f32[256,128]{1,0:T(8,128)S(1)}, u32[]{:S(2)}, u32[]{:S(2)}) %collective-permute-start.32) | collective-permute-done | bytes 131104 | tf_op jit(solution)/shard_map/ppermute | solution.py:36
  121.9 1.7 %collective-permute-done.30 = f32[264,128]{1,0:T(8,128)S(1)} collective-permute-done((f32[264,128]{1,0:T(8,128)S(1)}, f32[264,128]{1,0:T(8,128)S(1)}, u32[]{:S(2)}, u32[]{:S(2)}) %collective-permute-start.30) | collective-permute-done | bytes 135200 | tf_op jit(solution)/shard_map/ppermute | solution.py:36
  123.6 1.2 collective-permute-start.33
  124.8 3.9 %collective-permute-done.33 = f32[264,128]{1,0:T(8,128)S(1)} collective-permute-done((f32[264,128]{1,0:T(8,128)S(1)}, f32[264,128]{1,0:T(8,128)S(1)}, u32[]{:S(2)}, u32[]{:S(2)}) %collective-permute-start.33) | collective-permute-done | bytes 135200 | tf_op jit(solution)/shard_map/ppermute | solution.py:36
  128.8 3.1 %collective-permute-start.34 = (f32[136,128]{1,0:T(8,128)S(1)}, f32[136,128]{1,0:T(8,128)S(1)}, u32[]{:S(2)}, u32[]{:S(2)}) collective-permute-start(f32[136,128]{1,0:T(8,128)S(1)} %pad_maximum_fusion.18), channel_id=1, source_target_pairs={{0,16},{2,18},{4,20},{6,22},{8,24},{10,26},{12,28},{14,30},{16,0},... | collective-permute-start | bytes 208904 | tf_op jit(solution)/shard_map/ppermute | solution.py:36
  131.9 2.3 %collective-permute-done.34 = f32[136,128]{1,0:T(8,128)S(1)} collective-permute-done((f32[136,128]{1,0:T(8,128)S(1)}, f32[136,128]{1,0:T(8,128)S(1)}, u32[]{:S(2)}, u32[]{:S(2)}) %collective-permute-start.34) | collective-permute-done | bytes 69664 | tf_op jit(solution)/shard_map/ppermute | solution.py:36
  (134 shorter events, 22.1 us)
Async XLA Ops:
  2.4 7.9 %collective-permute-start = (f32[1,136,128]{2,1,0:T(8,128)S(1)}, f32[1,136,128]{2,1,0:T(8,128)S(1)}, u32[]{:S(2)}, u32[]{:S(2)}) collective-permute-start(f32[1,136,128]{2,1,0:T(8,128)S(1)} %maximum_bitcast_fusion.1), channel_id=1, source_target_pairs={{0,16},{2,18},{4,20},{6,22},{8,24},{10,26},{12,28},{14,30},{16,0},... | collective-permute-start | bytes 208904 | tf_op jit(solution)/shard_map/ppermute | solution.py:36
  9.9 9.0 %collective-permute-start.8 = (f32[1,256,128]{2,1,0:T(8,128)S(1)}, f32[1,256,128]{2,1,0:T(8,128)S(1)}, u32[]{:S(2)}, u32[]{:S(2)}) collective-permute-start(f32[1,256,128]{2,1,0:T(8,128)S(1)} %maximum_bitcast_fusion), channel_id=1, source_target_pairs={{0,16},{2,18},{4,20},{6,22},{8,24},{10,26},{12,28},{14,30},{16,0},... | collective-permute-start | bytes 393224 | tf_op jit(solution)/shard_map/ppermute | solution.py:36
  10.3 7.0 %collective-permute-start.1 = (f32[2,136,128]{2,1,0:T(8,128)S(1)}, f32[2,136,128]{2,1,0:T(8,128)S(1)}, u32[]{:S(2)}, u32[]{:S(2)}) collective-permute-start(f32[2,136,128]{2,1,0:T(8,128)S(1)} %pad_maximum_fusion.14), channel_id=1, source_target_pairs={{0,8},{2,10},{4,12},{6,14},{8,0},{10,2},{12,4},{14,6},{16,24},{18,... | collective-permute-start | bytes 417800 | tf_op jit(solution)/shard_map/ppermute | solution.py:36
  17.3 9.2 %collective-permute-start.5 = (f32[4,64,128]{2,1,0:T(8,128)S(1)}, f32[4,64,128]{2,1,0:T(8,128)S(1)}, u32[]{:S(2)}, u32[]{:S(2)}) collective-permute-start(f32[4,64,128]{2,1,0:T(8,128)S(1)} %slice.236), channel_id=1, source_target_pairs={{0,2},{2,0},{4,6},{6,4},{8,10},{10,8},{12,14},{14,12},{16,18},{18,... | collective-permute-start | bytes 393224 | tf_op jit(solution)/shard_map/ppermute | solution.py:36
  19.0 8.9 %collective-permute-start.9 = (f32[2,256,128]{2,1,0:T(8,128)S(1)}, f32[2,256,128]{2,1,0:T(8,128)}, u32[]{:S(2)}, u32[]{:S(2)}) collective-permute-start(f32[2,256,128]{2,1,0:T(8,128)S(1)} %pad_maximum_fusion.13), channel_id=1, source_target_pairs={{0,8},{2,10},{4,12},{6,14},{8,0},{10,2},{12,4},{14,6},{16,24},{18,... | collective-permute-start | bytes 786440 | tf_op jit(solution)/shard_map/ppermute | solution.py:36
  20.0 7.1 %collective-permute-start.2 = (f32[4,72,128]{2,1,0:T(8,128)S(1)}, f32[4,72,128]{2,1,0:T(8,128)S(1)}, u32[]{:S(2)}, u32[]{:S(2)}) collective-permute-start(f32[4,72,128]{2,1,0:T(8,128)S(1)} %slice.235), channel_id=1, source_target_pairs={{0,4},{2,6},{4,0},{6,2},{8,12},{10,14},{12,8},{14,10},{16,20},{18,... | collective-permute-start | bytes 442376 | tf_op jit(solution)/shard_map/ppermute | solution.py:36
  22.4 11.8 %collective-permute-start.11 = (f32[1,384,128]{2,1,0:T(8,128)S(1)}, f32[1,384,128]{2,1,0:T(8,128)S(1)}, u32[]{:S(2)}, u32[]{:S(2)}) collective-permute-start(f32[1,384,128]{2,1,0:T(8,128)S(1)} %bitcast.99), channel_id=1, source_target_pairs={{0,16},{2,18},{4,20},{6,22},{8,24},{10,26},{12,28},{14,30},{16,0},... | collective-permute-start | bytes 589832 | tf_op jit(solution)/shard_map/ppermute | solution.py:36
  26.5 10.1 %collective-permute-start.6 = (f32[8,64,128]{2,1,0:T(8,128)S(1)}, f32[8,64,128]{2,1,0:T(8,128)S(1)}, u32[]{:S(2)}, u32[]{:S(2)}) collective-permute-start(f32[8,64,128]{2,1,0:T(8,128)S(1)} %pad_maximum_fusion.12), channel_id=1, source_target_pairs={{0,4},{2,6},{4,0},{6,2},{8,12},{10,14},{12,8},{14,10},{16,20},{18,... | collective-permute-start | bytes 786440 | tf_op jit(solution)/shard_map/ppermute | solution.py:36
  27.2 9.6 %collective-permute-start.3 = (f32[8,72,128]{2,1,0:T(8,128)S(1)}, f32[8,72,128]{2,1,0:T(8,128)S(1)}, u32[]{:S(2)}, u32[]{:S(2)}) collective-permute-start(f32[8,72,128]{2,1,0:T(8,128)S(1)} %pad_maximum_fusion.9), channel_id=1, source_target_pairs={{0,2},{2,0},{4,6},{6,4},{8,10},{10,8},{12,14},{14,12},{16,18},{18,... | collective-permute-start | bytes 884744 | tf_op jit(solution)/shard_map/ppermute | solution.py:36
  34.3 8.3 %collective-permute-start.12 = (f32[2,384,128]{2,1,0:T(8,128)S(1)}, f32[2,384,128]{2,1,0:T(8,128)S(1)}, u32[]{:S(2)}, u32[]{:S(2)}) collective-permute-start(f32[2,384,128]{2,1,0:T(8,128)S(1)} %pad_maximum_fusion.8), channel_id=1, source_target_pairs={{0,8},{2,10},{4,12},{6,14},{8,0},{10,2},{12,4},{14,6},{16,24},{18,... | collective-permute-start | bytes 1179656 | tf_op jit(solution)/shard_map/ppermute | solution.py:36
  35.1 11.4 %collective-permute-start.16 = (f32[4,128,128]{2,1,0:T(8,128)}, f32[4,128,128]{2,1,0:T(8,128)}, u32[]{:S(2)}, u32[]{:S(2)}) collective-permute-start(f32[4,128,128]{2,1,0:T(8,128)} %get-tuple-element.42), channel_id=1, source_target_pairs={{0,2},{2,0},{4,6},{6,4},{8,10},{10,8},{12,14},{14,12},{16,18},{18,... | collective-permute-start | bytes 786440 | tf_op jit(solution)/shard_map/ppermute | solution.py:36
  35.7 8.5 %collective-permute-start.10 = (f32[4,128,128]{2,1,0:T(8,128)S(1)}, f32[4,128,128]{2,1,0:T(8,128)}, u32[]{:S(2)}, u32[]{:S(2)}) collective-permute-start(f32[4,128,128]{2,1,0:T(8,128)S(1)} %get-tuple-element.32), channel_id=1, source_target_pairs={{0,4},{2,6},{4,0},{6,2},{8,12},{10,14},{12,8},{14,10},{16,20},{18,... | collective-permute-start | bytes 786440 | tf_op jit(solution)/shard_map/ppermute | solution.py:36
  36.7 11.0 %collective-permute-start.7 = (f32[16,64,128]{2,1,0:T(8,128)S(1)}, f32[16,64,128]{2,1,0:T(8,128)S(1)}, u32[]{:S(2)}, u32[]{:S(2)}) collective-permute-start(f32[16,64,128]{2,1,0:T(8,128)S(1)} %pad_maximum_fusion.4.b_own), channel_id=1, source_target_pairs={{0,1},{1,0},{2,3},{3,2},{4,5},{5,4},{6,7},{7,6},{8,9},{9,8},{10,11... | collective-permute-start | bytes 1572872 | tf_op jit(solution)/shard_map/ppermute | solution.py:36
  36.8 12.8 %collective-permute-start.4 = (f32[16,72,128]{2,1,0:T(8,128)S(1)}, f32[16,72,128]{2,1,0:T(8,128)S(1)}, u32[]{:S(2)}, u32[]{:S(2)}) collective-permute-start(f32[16,72,128]{2,1,0:T(8,128)S(1)} %pad_maximum_fusion.3.a_own), channel_id=1, source_target_pairs={{0,1},{1,0},{2,3},{3,2},{4,5},{5,4},{6,7},{7,6},{8,9},{9,8},{10,11... | collective-permute-start | bytes 1769480 | tf_op jit(solution)/shard_map/ppermute | solution.py:36
  43.6 19.6 %collective-permute-start.14 = (f32[4,192,128]{2,1,0:T(8,128)}, f32[4,192,128]{2,1,0:T(8,128)}, u32[]{:S(2)}, u32[]{:S(2)}) collective-permute-start(f32[4,192,128]{2,1,0:T(8,128)} %get-tuple-element.60), channel_id=1, source_target_pairs={{0,2},{2,0},{4,6},{6,4},{8,10},{10,8},{12,14},{14,12},{16,18},{18,... | collective-permute-start | bytes 1179656 | tf_op jit(solution)/shard_map/ppermute | solution.py:36
  44.2 19.0 %collective-permute-start.13 = (f32[4,192,128]{2,1,0:T(8,128)}, f32[4,192,128]{2,1,0:T(8,128)}, u32[]{:S(2)}, u32[]{:S(2)}) collective-permute-start(f32[4,192,128]{2,1,0:T(8,128)} %get-tuple-element.61), channel_id=1, source_target_pairs={{0,4},{2,6},{4,0},{6,2},{8,12},{10,14},{12,8},{14,10},{16,20},{18,... | collective-permute-start | bytes 1179656 | tf_op jit(solution)/shard_map/ppermute | solution.py:36
  46.5 20.5 %collective-permute-start.18 = (f32[8,128,128]{2,1,0:T(8,128)S(1)}, f32[8,128,128]{2,1,0:T(8,128)S(1)}, u32[]{:S(2)}, u32[]{:S(2)}) collective-permute-start(f32[8,128,128]{2,1,0:T(8,128)S(1)} %pad_maximum_fusion.6.refs_0_), channel_id=1, source_target_pairs={{0,1},{1,0},{2,3},{3,2},{4,5},{5,4},{6,7},{7,6},{8,9},{9,8},{10,11... | collective-permute-start | bytes 1572872 | tf_op jit(solution)/shard_map/ppermute | solution.py:36
  47.7 18.8 %collective-permute-start.17 = (f32[8,128,128]{2,1,0:T(8,128)S(1)}, f32[8,128,128]{2,1,0:T(8,128)S(1)}, u32[]{:S(2)}, u32[]{:S(2)}) collective-permute-start(f32[8,128,128]{2,1,0:T(8,128)S(1)} %pad_maximum_fusion.7.refs_4_), channel_id=1, source_target_pairs={{0,4},{2,6},{4,0},{6,2},{8,12},{10,14},{12,8},{14,10},{16,20},{18,... | collective-permute-start | bytes 1572872 | tf_op jit(solution)/shard_map/ppermute | solution.py:36
  49.6 16.9 %collective-permute-start.15 = (f32[8,128,128]{2,1,0:T(8,128)S(1)}, f32[8,128,128]{2,1,0:T(8,128)S(1)}, u32[]{:S(2)}, u32[]{:S(2)}) collective-permute-start(f32[8,128,128]{2,1,0:T(8,128)S(1)} %pad_maximum_fusion.6.refs_0_), channel_id=1, source_target_pairs={{0,2},{2,0},{4,6},{6,4},{8,10},{10,8},{12,14},{14,12},{16,18},{18,... | collective-permute-start | bytes 1572872 | tf_op jit(solution)/shard_map/ppermute | solution.py:36
  64.4 19.7 %collective-permute-start.23 = (f32[8,192,128]{2,1,0:T(8,128)S(1)}, f32[8,192,128]{2,1,0:T(8,128)S(1)}, u32[]{:S(2)}, u32[]{:S(2)}) collective-permute-start(f32[8,192,128]{2,1,0:T(8,128)S(1)} %pad_maximum_fusion.2.refs_6_), channel_id=1, source_target_pairs={{0,4},{2,6},{4,0},{6,2},{8,12},{10,14},{12,8},{14,10},{16,20},{18,... | collective-permute-start | bytes 2359304 | tf_op jit(solution)/shard_map/ppermute | solution.py:36
  65.8 19.4 %collective-permute-start.22 = (f32[8,192,128]{2,1,0:T(8,128)S(1)}, f32[8,192,128]{2,1,0:T(8,128)S(1)}, u32[]{:S(2)}, u32[]{:S(2)}) collective-permute-start(f32[8,192,128]{2,1,0:T(8,128)S(1)} %pad_maximum_fusion.1.refs_4_), channel_id=1, source_target_pairs={{0,2},{2,0},{4,6},{6,4},{8,10},{10,8},{12,14},{14,12},{16,18},{18,... | collective-permute-start | bytes 2359304 | tf_op jit(solution)/shard_map/ppermute | solution.py:36
  66.5 5.1 %collective-permute-start.21 = (f32[8,128,128]{2,1,0:T(8,128)S(1)}, f32[8,128,128]{2,1,0:T(8,128)S(1)}, u32[]{:S(2)}, u32[]{:S(2)}) collective-permute-start(f32[8,128,128]{2,1,0:T(8,128)S(1)} %collective-permute-done.17.refs_5_), channel_id=1, source_target_pairs={{0,1},{1,0},{2,3},{3,2},{4,5},{5,4},{6,7},{7,6},{8,9},{9,8},{10,11... | collective-permute-start | bytes 1572872 | tf_op jit(solution)/shard_map/ppermute | solution.py:36
  71.1 19.0 %collective-permute-start.26 = (f32[8,192,128]{2,1,0:T(8,128)S(1)}, f32[8,192,128]{2,1,0:T(8,128)S(1)}, u32[]{:S(2)}, u32[]{:S(2)}) collective-permute-start(f32[8,192,128]{2,1,0:T(8,128)S(1)} %pad_maximum_fusion.2.refs_6_), channel_id=1, source_target_pairs={{0,1},{1,0},{2,3},{3,2},{4,5},{5,4},{6,7},{7,6},{8,9},{9,8},{10,11... | collective-permute-start | bytes 2359304 | tf_op jit(solution)/shard_map/ppermute | solution.py:36
  71.6 18.5 %collective-permute-start.24 = (f32[8,192,128]{2,1,0:T(8,128)S(1)}, f32[8,192,128]{2,1,0:T(8,128)S(1)}, u32[]{:S(2)}, u32[]{:S(2)}) collective-permute-start(f32[8,192,128]{2,1,0:T(8,128)S(1)} %pad_maximum_fusion.1.refs_4_), channel_id=1, source_target_pairs={{0,1},{1,0},{2,3},{3,2},{4,5},{5,4},{6,7},{7,6},{8,9},{9,8},{10,11... | collective-permute-start | bytes 2359304 | tf_op jit(solution)/shard_map/ppermute | solution.py:36
  85.2 5.0 %collective-permute-start.27 = (f32[8,192,128]{2,1,0:T(8,128)S(1)}, f32[8,192,128]{2,1,0:T(8,128)S(1)}, u32[]{:S(2)}, u32[]{:S(2)}) collective-permute-start(f32[8,192,128]{2,1,0:T(8,128)S(1)} %collective-permute-done.23.refs_7_), channel_id=1, source_target_pairs={{0,1},{1,0},{2,3},{3,2},{4,5},{5,4},{6,7},{7,6},{8,9},{9,8},{10,11... | collective-permute-start | bytes 2359304 | tf_op jit(solution)/shard_map/ppermute | solution.py:36
  85.2 5.0 %collective-permute-start.25 = (f32[8,192,128]{2,1,0:T(8,128)S(1)}, f32[8,192,128]{2,1,0:T(8,128)S(1)}, u32[]{:S(2)}, u32[]{:S(2)}) collective-permute-start(f32[8,192,128]{2,1,0:T(8,128)S(1)} %collective-permute-done.22.refs_5_), channel_id=1, source_target_pairs={{0,1},{1,0},{2,3},{3,2},{4,5},{5,4},{6,7},{7,6},{8,9},{9,8},{10,11... | collective-permute-start | bytes 2359304 | tf_op jit(solution)/shard_map/ppermute | solution.py:36
  108.3 8.4 %collective-permute-start.31 = (f32[512,128]{1,0:T(8,128)S(1)}, f32[512,128]{1,0:T(8,128)S(1)}, u32[]{:S(2)}, u32[]{:S(2)}) collective-permute-start(f32[512,128]{1,0:T(8,128)S(1)} %bitcast.109), channel_id=1, source_target_pairs={{0,4},{2,6},{4,0},{6,2},{8,12},{10,14},{12,8},{14,10},{16,20},{18,... | collective-permute-start | bytes 786440 | tf_op jit(solution)/shard_map/ppermute | solution.py:36
  110.1 8.2 %collective-permute-start.29 = (f32[520,128]{1,0:T(8,128)S(1)}, f32[520,128]{1,0:T(8,128)S(1)}, u32[]{:S(2)}, u32[]{:S(2)}) collective-permute-start(f32[520,128]{1,0:T(8,128)S(1)} %pad_maximum_fusion.11), channel_id=1, source_target_pairs={{0,2},{2,0},{4,6},{6,4},{8,10},{10,8},{12,14},{14,12},{16,18},{18,... | collective-permute-start | bytes 798728 | tf_op jit(solution)/shard_map/ppermute | solution.py:36
  116.8 5.0 %collective-permute-start.32 = (f32[256,128]{1,0:T(8,128)S(1)}, f32[256,128]{1,0:T(8,128)S(1)}, u32[]{:S(2)}, u32[]{:S(2)}) collective-permute-start(f32[256,128]{1,0:T(8,128)S(1)} %bitcast.113), channel_id=1, source_target_pairs={{0,2},{2,0},{4,6},{6,4},{8,10},{10,8},{12,14},{14,12},{16,18},{18,... | collective-permute-start | bytes 393224 | tf_op jit(solution)/shard_map/ppermute | solution.py:36
  118.5 5.1 %collective-permute-start.30 = (f32[264,128]{1,0:T(8,128)S(1)}, f32[264,128]{1,0:T(8,128)S(1)}, u32[]{:S(2)}, u32[]{:S(2)}) collective-permute-start(f32[264,128]{1,0:T(8,128)S(1)} %pad_maximum_fusion.15), channel_id=1, source_target_pairs={{0,4},{2,6},{4,0},{6,2},{8,12},{10,14},{12,8},{14,10},{16,20},{18,... | collective-permute-start | bytes 405512 | tf_op jit(solution)/shard_map/ppermute | solution.py:36
  123.6 5.1 %collective-permute-start.33 = (f32[264,128]{1,0:T(8,128)S(1)}, f32[264,128]{1,0:T(8,128)S(1)}, u32[]{:S(2)}, u32[]{:S(2)}) collective-permute-start(f32[264,128]{1,0:T(8,128)S(1)} %pad_maximum_fusion.16), channel_id=1, source_target_pairs={{0,8},{2,10},{4,12},{6,14},{8,0},{10,2},{12,4},{14,6},{16,24},{18,... | collective-permute-start | bytes 405512 | tf_op jit(solution)/shard_map/ppermute | solution.py:36
  128.8 5.4 %collective-permute-start.34 = (f32[136,128]{1,0:T(8,128)S(1)}, f32[136,128]{1,0:T(8,128)S(1)}, u32[]{:S(2)}, u32[]{:S(2)}) collective-permute-start(f32[136,128]{1,0:T(8,128)S(1)} %pad_maximum_fusion.18), channel_id=1, source_target_pairs={{0,16},{2,18},{4,20},{6,22},{8,24},{10,26},{12,28},{14,30},{16,0},... | collective-permute-start | bytes 208904 | tf_op jit(solution)/shard_map/ppermute | solution.py:36
  (12 other events, 90.0 us)

commit v8 on v7

--- a/solution.py
+++ b/solution.py
@@ -272,7 +272,7 @@
                             a, b = values[k], values[k | width]
                             values[k], values[k | width] = a + b, a - b
                     width *= 2
-                acc = acc_ref[r]
+                accs = [acc_ref[r], None, None, None]
                 for k in range(chunks):
                     place = place_of(k, bits)
                     turns = values[k] * scale_ref[k] + late[place][pl.ds(row + cut, 8), :]
@@ -283,8 +283,9 @@
                         cosine = cosine * square + c
                     cosine = cosine * quarter
                     feat_ref[k, r, here, :] = cosine
-                    acc = acc + cosine * late[place][pl.ds(row + 2 * cut, 8), :]
-                acc_ref[r] = acc
+                    term = cosine * late[place][pl.ds(row + 2 * cut, 8), :]
+                    accs[k % 4] = term if accs[k % 4] is None else accs[k % 4] + term
+                acc_ref[r] = (accs[0] + accs[1]) + (accs[2] + accs[3])
 
     residuals = []
     lane = lax.broadcasted_iota(jnp.int32, (1, LANES), 1)
@@ -462,7 +463,7 @@
         m_pair = parted(m_held, middle)
         s_pair = join_pair(s_pair, s_step)
         s_step = send_pair(s_pair, last)
-        m_step = send_pair(m_pair, last - 1, *s_pair)
+        m_step = send_pair(m_pair, last - 1)
         s_pair = join_pair(s_pair, s_step)
         s_all = with_core(s_pair)
         for i in range(1, last - 1):

time: 136 us -> 135 us (level)
  no operation moved by 1% of the time
where the time goes in v8:
time: 135 us
  Pallas kernels  47.8 us (35%)
  waiting for transfers between devices  36.6 us (27%)
  starting transfers between devices  33.2 us (25%)
  other arithmetic  8.27 us (6%)
  local copies, waits for them, and re-layouts  4.62 us (3%)
  matrix products  3.37 us (2%)
    ppermute x35, waiting for transfers between devices, swap(): return lax.ppermute(values, axis_name, [(i, i ^ bit) for i in range(size)])  36.6 us
    ppermute x35, starting transfers between devices, swap(): return lax.ppermute(values, axis_name, [(i, i ^ bit) for i in range(size)])  33.2 us
    pallas_call x4, Pallas kernels, mix(): pl.pallas_call(functools.partial(mix_kernel, rows, begin, group, bits_a,...  16.6 us
    pallas_call x4, Pallas kernels, first_of(): pl.pallas_call(functools.partial(first_kernel, rows, begin, group, bits_a...  16.1 us
    pallas_call x1, Pallas kernels, local(): pl.pallas_call(functools.partial(head_kernel, rows, turn_sine_coefficient...  15 us
    concatenate x14, other arithmetic, join(): jnp.concatenate([held, after(got, *others) if others else got], axis=0)  5.71 us
    dot_general x1, matrix products, local(): jnp.einsum('bij,j->bi', half(block_permutations), jnp.arange(LANES).astyp...  3.37 us
  transfers between devices with their start and end apart: 35, of which 12 were waited for; matrix products, arithmetic and copies ran while one was open for 10% of the time, Pallas kernels for 24%

profile of v8, /device:TPU:0, one launch (start us, length us, event | category | flops | bytes accessed | tf_op | source)
XLA Modules:
  0.0 135.1 jit_solution(8236042659938789248)
XLA Ops:
  2.4 4.1 %collective-permute-start = (f32[1,136,128]{2,1,0:T(8,128)S(1)}, f32[1,136,128]{2,1,0:T(8,128)S(1)}, u32[]{:S(2)}, u32[]{:S(2)}) collective-permute-start(f32[1,136,128]{2,1,0:T(8,128)S(1)} %maximum_bitcast_fusion.1), channel_id=1, source_target_pairs={{0,16},{2,18},{4,20},{6,22},{8,24},{10,26},{12,28},{14,30},{16,0},... | collective-permute-start | bytes 208904 | tf_op jit(solution)/shard_map/ppermute | solution.py:36
  6.5 3.4 %fusion = f32[1,128,128]{2,0,1:T(1,128)S(1)} fusion(bf16[256,128,128]{2,1,0:T(8,128)(2,1)} %param.18, s32[]{:T(128)S(6)} %select_n.8), kind=kOutput, calls=%fused_computation | convolution fusion | flops 4194432 | bytes 4259844 | tf_op jit(solution)/shard_map/bij,j->bi/dot_general | solution.py:346
  10.3 1.8 %collective-permute-start.1 = (f32[2,136,128]{2,1,0:T(8,128)S(1)}, f32[2,136,128]{2,1,0:T(8,128)S(1)}, u32[]{:S(2)}, u32[]{:S(2)}) collective-permute-start(f32[2,136,128]{2,1,0:T(8,128)S(1)} %pad_maximum_fusion.14), channel_id=1, source_target_pairs={{0,8},{2,10},{4,12},{6,14},{8,0},{10,2},{12,4},{14,6},{16,24},{18,... | collective-permute-start | bytes 417800 | tf_op jit(solution)/shard_map/ppermute | solution.py:36
  12.1 5.2 %collective-permute-done.1 = f32[2,136,128]{2,1,0:T(8,128)S(1)} collective-permute-done((f32[2,136,128]{2,1,0:T(8,128)S(1)}, f32[2,136,128]{2,1,0:T(8,128)S(1)}, u32[]{:S(2)}, u32[]{:S(2)}) %collective-permute-start.1) | collective-permute-done | bytes 139296 | tf_op jit(solution)/shard_map/ppermute | solution.py:36
  17.3 1.6 %collective-permute-start.5 = (f32[4,64,128]{2,1,0:T(8,128)S(1)}, f32[4,64,128]{2,1,0:T(8,128)S(1)}, u32[]{:S(2)}, u32[]{:S(2)}) collective-permute-start(f32[4,64,128]{2,1,0:T(8,128)S(1)} %slice.236), channel_id=1, source_target_pairs={{0,2},{2,0},{4,6},{6,4},{8,10},{10,8},{12,14},{14,12},{16,18},{18,... | collective-permute-start | bytes 393224 | tf_op jit(solution)/shard_map/ppermute | solution.py:36
  20.0 1.6 %collective-permute-start.2 = (f32[4,72,128]{2,1,0:T(8,128)S(1)}, f32[4,72,128]{2,1,0:T(8,128)S(1)}, u32[]{:S(2)}, u32[]{:S(2)}) collective-permute-start(f32[4,72,128]{2,1,0:T(8,128)S(1)} %slice.235), channel_id=1, source_target_pairs={{0,4},{2,6},{4,0},{6,2},{8,12},{10,14},{12,8},{14,10},{16,20},{18,... | collective-permute-start | bytes 442376 | tf_op jit(solution)/shard_map/ppermute | solution.py:36
  22.4 4.1 %collective-permute-start.11 = (f32[1,384,128]{2,1,0:T(8,128)S(1)}, f32[1,384,128]{2,1,0:T(8,128)S(1)}, u32[]{:S(2)}, u32[]{:S(2)}) collective-permute-start(f32[1,384,128]{2,1,0:T(8,128)S(1)} %bitcast.99), channel_id=1, source_target_pairs={{0,16},{2,18},{4,20},{6,22},{8,24},{10,26},{12,28},{14,30},{16,0},... | collective-permute-start | bytes 589832 | tf_op jit(solution)/shard_map/ppermute | solution.py:36
  28.8 5.5 %collective-permute-done.11 = f32[1,384,128]{2,1,0:T(8,128)S(1)} collective-permute-done((f32[1,384,128]{2,1,0:T(8,128)S(1)}, f32[1,384,128]{2,1,0:T(8,128)S(1)}, u32[]{:S(2)}, u32[]{:S(2)}) %collective-permute-start.11) | collective-permute-done | bytes 196640 | tf_op jit(solution)/shard_map/ppermute | solution.py:36
  37.4 5.3 %collective-permute-done.12 = f32[2,384,128]{2,1,0:T(8,128)S(1)} collective-permute-done((f32[2,384,128]{2,1,0:T(8,128)S(1)}, f32[2,384,128]{2,1,0:T(8,128)S(1)}, u32[]{:S(2)}, u32[]{:S(2)}) %collective-permute-start.12) | collective-permute-done | bytes 393248 | tf_op jit(solution)/shard_map/ppermute | solution.py:36
  47.7 1.9 %collective-permute-start.17 = (f32[8,128,128]{2,1,0:T(8,128)S(1)}, f32[8,128,128]{2,1,0:T(8,128)S(1)}, u32[]{:S(2)}, u32[]{:S(2)}) collective-permute-start(f32[8,128,128]{2,1,0:T(8,128)S(1)} %pad_maximum_fusion.7.refs_4_), channel_id=1, source_target_pairs={{0,4},{2,6},{4,0},{6,2},{8,12},{10,14},{12,8},{14,10},{16,20},{18,... | collective-permute-start | bytes 1572872 | tf_op jit(solution)/shard_map/ppermute | solution.py:36
  49.6 1.4 %collective-permute-start.15 = (f32[8,128,128]{2,1,0:T(8,128)S(1)}, f32[8,128,128]{2,1,0:T(8,128)S(1)}, u32[]{:S(2)}, u32[]{:S(2)}) collective-permute-start(f32[8,128,128]{2,1,0:T(8,128)S(1)} %pad_maximum_fusion.6.refs_0_), channel_id=1, source_target_pairs={{0,2},{2,0},{4,6},{6,4},{8,10},{10,8},{12,14},{14,12},{16,18},{18,... | collective-permute-start | bytes 1572872 | tf_op jit(solution)/shard_map/ppermute | solution.py:36
  51.1 4.4 %first.4 = (f32[4,8,256,128]{3,2,1,0:T(8,128)S(1)}, bf16[1024,512]{1,0:T(8,128)(2,1)S(1)}, bf16[640,1024]{1,0:T(8,128)(2,1)S(1)}) custom-call(s32[2]{0:T(128)S(1)} %pad_add_fusion.me_ref, f32[16,72,128]{2,1,0:T(8,128)S(1)} %pad_maximum_fusion.3.a_own, f32[16,72,128]{2,1,0:T(8,128)S(1)} %collective-permute-done.4.a_other, ...), custom_call_target="tpu_custom_call" | custom-call | flops 1 | bytes 1 | tf_op jit(solution)/shard_map/first/pallas_call | solution.py:402
  55.5 3.9 %first.6.first_ref = f32[4,8,256,128]{3,2,1,0:T(8,128)S(1)} custom-call(s32[2]{0:T(128)S(1)} %pad_add_fusion.me_ref, f32[16,72,128]{2,1,0:T(8,128)S(1)} %pad_maximum_fusion.3.a_own, f32[16,72,128]{2,1,0:T(8,128)S(1)} %collective-permute-done.4.a_other, f32[16,64,128]{2,1,0:T(8,128)S(1)} %pad_maximum_fusion.4.b_own, ...), custom_call_target="tpu_custom_call" | custom-call | flops 1 | bytes 1 | tf_op jit(solution)/shard_map/first/pallas_call | solution.py:402
  59.3 3.9 %first.5.first_ref = f32[4,8,256,128]{3,2,1,0:T(8,128)S(1)} custom-call(s32[2]{0:T(128)S(1)} %pad_add_fusion.me_ref, f32[16,72,128]{2,1,0:T(8,128)S(1)} %pad_maximum_fusion.3.a_own, f32[16,72,128]{2,1,0:T(8,128)S(1)} %collective-permute-done.4.a_other, f32[16,64,128]{2,1,0:T(8,128)S(1)} %pad_maximum_fusion.4.b_own, ...), custom_call_target="tpu_custom_call" | custom-call | flops 1 | bytes 1 | tf_op jit(solution)/shard_map/first/pallas_call | solution.py:402
  63.2 1.2 pad_maximum_fusion.2.refs_6_
  64.6 1.2 pad_maximum_fusion.1.refs_4_
  67.1 4.0 %first.7.first_ref = f32[4,8,256,128]{3,2,1,0:T(8,128)S(1)} custom-call(s32[2]{0:T(128)S(1)} %pad_add_fusion.me_ref, f32[16,72,128]{2,1,0:T(8,128)S(1)} %pad_maximum_fusion.3.a_own, f32[16,72,128]{2,1,0:T(8,128)S(1)} %collective-permute-done.4.a_other, f32[16,64,128]{2,1,0:T(8,128)S(1)} %pad_maximum_fusion.4.b_own, ...), custom_call_target="tpu_custom_call" | custom-call | flops 1 | bytes 1 | tf_op jit(solution)/shard_map/first/pallas_call | solution.py:402
  71.7 4.1 %mix.4.refs_0_ = f32[4,8,256,128]{3,2,1,0:T(8,128)S(1)} custom-call(s32[2]{0:T(128)S(1)} %pad_add_fusion.me_ref, f32[4,8,256,128]{3,2,1,0:T(8,128)S(1)} %get-tuple-element.27.first_ref, f32[8,128,128]{2,1,0:T(8,128)S(1)} %pad_maximum_fusion.6.refs_0_, f32[8,128,128]{2,1,0:T(8,128)S(1)} %collective-permute-done.15.refs_1_, ...), custom_call_target="tpu_custom_call", output_to_operand_aliasing={{}: (1, {})} | custom-call | flops 1 | bytes 1 | tf_op jit(solution)/shard_map/mix/pallas_call | solution.py:414
  75.8 4.1 %mix.5.refs_1_ = f32[4,8,256,128]{3,2,1,0:T(8,128)S(1)} custom-call(s32[2]{0:T(128)S(1)} %pad_add_fusion.me_ref, f32[4,8,256,128]{3,2,1,0:T(8,128)S(1)} %first.5.first_ref, f32[8,128,128]{2,1,0:T(8,128)S(1)} %pad_maximum_fusion.6.refs_0_, f32[8,128,128]{2,1,0:T(8,128)S(1)} %collective-permute-done.15.refs_1_, ...), custom_call_target="tpu_custom_call", output_to_operand_aliasing={{}: (1, {})} | custom-call | flops 1 | bytes 1 | tf_op jit(solution)/shard_map/mix/pallas_call | solution.py:414
  79.9 4.1 %mix.6.refs_2_ = f32[4,8,256,128]{3,2,1,0:T(8,128)S(1)} custom-call(s32[2]{0:T(128)S(1)} %pad_add_fusion.me_ref, f32[4,8,256,128]{3,2,1,0:T(8,128)S(1)} %first.6.first_ref, f32[8,128,128]{2,1,0:T(8,128)S(1)} %pad_maximum_fusion.6.refs_0_, f32[8,128,128]{2,1,0:T(8,128)S(1)} %collective-permute-done.15.refs_1_, ...), custom_call_target="tpu_custom_call", output_to_operand_aliasing={{}: (1, {})} | custom-call | flops 1 | bytes 1 | tf_op jit(solution)/shard_map/mix/pallas_call | solution.py:414
  84.1 1.2 collective-permute-done.22.refs_5_
  85.8 4.3 %mix.7.refs_3_ = f32[4,8,256,128]{3,2,1,0:T(8,128)S(1)} custom-call(s32[2]{0:T(128)S(1)} %pad_add_fusion.me_ref, f32[4,8,256,128]{3,2,1,0:T(8,128)S(1)} %first.7.first_ref, f32[8,128,128]{2,1,0:T(8,128)S(1)} %pad_maximum_fusion.6.refs_0_, f32[8,128,128]{2,1,0:T(8,128)S(1)} %collective-permute-done.15.refs_1_, ...), custom_call_target="tpu_custom_call", output_to_operand_aliasing={{}: (1, {})} | custom-call | flops 1 | bytes 1 | tf_op jit(solution)/shard_map/mix/pallas_call | solution.py:414
  90.2 15.0 %head.1 = (f32[8,128]{1,0:T(8,128)S(1)}, f32[16,128,128]{2,1,0:T(8,128)S(1)}, f32[16,128,128]{2,1,0:T(8,128)S(1)}) custom-call(s32[2]{0:T(128)S(1)} %pad_add_fusion.me_ref, f32[8]{0:T(128)S(1)} %dynamic_slice.27.target_ref, f32[4,8,256,128]{3,2,1,0:T(8,128)S(1)} %mix.4.refs_0_, f32[4,8,256,128]{3,2,1,0:T(8,128)S(1)} %mix.5.refs_1_, ...), custom_call_target="tpu_custom_call" | custom-call | tf_op jit(solution)/shard_map/head/pallas_call | solution.py:512
  105.3 2.6 %collective-permute-done.28 = f32[16,128,128]{2,1,0:T(8,128)S(1)} collective-permute-done((f32[16,128,128]{2,1,0:T(8,128)S(1)}, f32[16,128,128]{2,1,0:T(8,128)S(1)}, u32[]{:S(2)}, u32[]{:S(2)}) %collective-permute-start.28) | collective-permute-done | bytes 1048608 | tf_op jit(solution)/shard_map/ppermute | solution.py:36
  108.1 1.7 %collective-permute-start.31 = (f32[512,128]{1,0:T(8,128)S(1)}, f32[512,128]{1,0:T(8,128)S(1)}, u32[]{:S(2)}, u32[]{:S(2)}) collective-permute-start(f32[512,128]{1,0:T(8,128)S(1)} %bitcast.109), channel_id=1, source_target_pairs={{0,4},{2,6},{4,0},{6,2},{8,12},{10,14},{12,8},{14,10},{16,20},{18,... | collective-permute-start | bytes 786440 | tf_op jit(solution)/shard_map/ppermute | solution.py:36
  110.6 5.9 %collective-permute-done.31 = f32[512,128]{1,0:T(8,128)S(1)} collective-permute-done((f32[512,128]{1,0:T(8,128)S(1)}, f32[512,128]{1,0:T(8,128)S(1)}, u32[]{:S(2)}, u32[]{:S(2)}) %collective-permute-start.31) | collective-permute-done | bytes 262176 | tf_op jit(solution)/shard_map/ppermute | solution.py:36
  119.4 2.3 %collective-permute-done.32 = f32[256,128]{1,0:T(8,128)S(1)} collective-permute-done((f32[256,128]{1,0:T(8,128)S(1)}, f32[256,128]{1,0:T(8,128)S(1)}, u32[]{:S(2)}, u32[]{:S(2)}) %collective-permute-start.32) | collective-permute-done | bytes 131104 | tf_op jit(solution)/shard_map/ppermute | solution.py:36
  121.6 1.7 %collective-permute-done.30 = f32[264,128]{1,0:T(8,128)S(1)} collective-permute-done((f32[264,128]{1,0:T(8,128)S(1)}, f32[264,128]{1,0:T(8,128)S(1)}, u32[]{:S(2)}, u32[]{:S(2)}) %collective-permute-start.30) | collective-permute-done | bytes 135200 | tf_op jit(solution)/shard_map/ppermute | solution.py:36
  123.4 1.2 collective-permute-start.33
  124.6 3.9 %collective-permute-done.33 = f32[264,128]{1,0:T(8,128)S(1)} collective-permute-done((f32[264,128]{1,0:T(8,128)S(1)}, f32[264,128]{1,0:T(8,128)S(1)}, u32[]{:S(2)}, u32[]{:S(2)}) %collective-permute-start.33) | collective-permute-done | bytes 135200 | tf_op jit(solution)/shard_map/ppermute | solution.py:36
  128.6 3.1 %collective-permute-start.34 = (f32[136,128]{1,0:T(8,128)S(1)}, f32[136,128]{1,0:T(8,128)S(1)}, u32[]{:S(2)}, u32[]{:S(2)}) collective-permute-start(f32[136,128]{1,0:T(8,128)S(1)} %pad_maximum_fusion.18), channel_id=1, source_target_pairs={{0,16},{2,18},{4,20},{6,22},{8,24},{10,26},{12,28},{14,30},{16,0},... | collective-permute-start | bytes 208904 | tf_op jit(solution)/shard_map/ppermute | solution.py:36
  131.6 2.3 %collective-permute-done.34 = f32[136,128]{1,0:T(8,128)S(1)} collective-permute-done((f32[136,128]{1,0:T(8,128)S(1)}, f32[136,128]{1,0:T(8,128)S(1)}, u32[]{:S(2)}, u32[]{:S(2)}) %collective-permute-start.34) | collective-permute-done | bytes 69664 | tf_op jit(solution)/shard_map/ppermute | solution.py:36
  (134 shorter events, 22.1 us)
Async XLA Ops:
  2.4 7.9 %collective-permute-start = (f32[1,136,128]{2,1,0:T(8,128)S(1)}, f32[1,136,128]{2,1,0:T(8,128)S(1)}, u32[]{:S(2)}, u32[]{:S(2)}) collective-permute-start(f32[1,136,128]{2,1,0:T(8,128)S(1)} %maximum_bitcast_fusion.1), channel_id=1, source_target_pairs={{0,16},{2,18},{4,20},{6,22},{8,24},{10,26},{12,28},{14,30},{16,0},... | collective-permute-start | bytes 208904 | tf_op jit(solution)/shard_map/ppermute | solution.py:36
  9.9 9.0 %collective-permute-start.8 = (f32[1,256,128]{2,1,0:T(8,128)S(1)}, f32[1,256,128]{2,1,0:T(8,128)S(1)}, u32[]{:S(2)}, u32[]{:S(2)}) collective-permute-start(f32[1,256,128]{2,1,0:T(8,128)S(1)} %maximum_bitcast_fusion), channel_id=1, source_target_pairs={{0,16},{2,18},{4,20},{6,22},{8,24},{10,26},{12,28},{14,30},{16,0},... | collective-permute-start | bytes 393224 | tf_op jit(solution)/shard_map/ppermute | solution.py:36
  10.3 7.0 %collective-permute-start.1 = (f32[2,136,128]{2,1,0:T(8,128)S(1)}, f32[2,136,128]{2,1,0:T(8,128)S(1)}, u32[]{:S(2)}, u32[]{:S(2)}) collective-permute-start(f32[2,136,128]{2,1,0:T(8,128)S(1)} %pad_maximum_fusion.14), channel_id=1, source_target_pairs={{0,8},{2,10},{4,12},{6,14},{8,0},{10,2},{12,4},{14,6},{16,24},{18,... | collective-permute-start | bytes 417800 | tf_op jit(solution)/shard_map/ppermute | solution.py:36
  17.3 9.2 %collective-permute-start.5 = (f32[4,64,128]{2,1,0:T(8,128)S(1)}, f32[4,64,128]{2,1,0:T(8,128)S(1)}, u32[]{:S(2)}, u32[]{:S(2)}) collective-permute-start(f32[4,64,128]{2,1,0:T(8,128)S(1)} %slice.236), channel_id=1, source_target_pairs={{0,2},{2,0},{4,6},{6,4},{8,10},{10,8},{12,14},{14,12},{16,18},{18,... | collective-permute-start | bytes 393224 | tf_op jit(solution)/shard_map/ppermute | solution.py:36
  19.0 8.9 %collective-permute-start.9 = (f32[2,256,128]{2,1,0:T(8,128)S(1)}, f32[2,256,128]{2,1,0:T(8,128)}, u32[]{:S(2)}, u32[]{:S(2)}) collective-permute-start(f32[2,256,128]{2,1,0:T(8,128)S(1)} %pad_maximum_fusion.13), channel_id=1, source_target_pairs={{0,8},{2,10},{4,12},{6,14},{8,0},{10,2},{12,4},{14,6},{16,24},{18,... | collective-permute-start | bytes 786440 | tf_op jit(solution)/shard_map/ppermute | solution.py:36
  20.0 7.1 %collective-permute-start.2 = (f32[4,72,128]{2,1,0:T(8,128)S(1)}, f32[4,72,128]{2,1,0:T(8,128)S(1)}, u32[]{:S(2)}, u32[]{:S(2)}) collective-permute-start(f32[4,72,128]{2,1,0:T(8,128)S(1)} %slice.235), channel_id=1, source_target_pairs={{0,4},{2,6},{4,0},{6,2},{8,12},{10,14},{12,8},{14,10},{16,20},{18,... | collective-permute-start | bytes 442376 | tf_op jit(solution)/shard_map/ppermute | solution.py:36
  22.4 11.8 %collective-permute-start.11 = (f32[1,384,128]{2,1,0:T(8,128)S(1)}, f32[1,384,128]{2,1,0:T(8,128)S(1)}, u32[]{:S(2)}, u32[]{:S(2)}) collective-permute-start(f32[1,384,128]{2,1,0:T(8,128)S(1)} %bitcast.99), channel_id=1, source_target_pairs={{0,16},{2,18},{4,20},{6,22},{8,24},{10,26},{12,28},{14,30},{16,0},... | collective-permute-start | bytes 589832 | tf_op jit(solution)/shard_map/ppermute | solution.py:36
  26.5 10.1 %collective-permute-start.6 = (f32[8,64,128]{2,1,0:T(8,128)S(1)}, f32[8,64,128]{2,1,0:T(8,128)S(1)}, u32[]{:S(2)}, u32[]{:S(2)}) collective-permute-start(f32[8,64,128]{2,1,0:T(8,128)S(1)} %pad_maximum_fusion.12), channel_id=1, source_target_pairs={{0,4},{2,6},{4,0},{6,2},{8,12},{10,14},{12,8},{14,10},{16,20},{18,... | collective-permute-start | bytes 786440 | tf_op jit(solution)/shard_map/ppermute | solution.py:36
  27.2 9.6 %collective-permute-start.3 = (f32[8,72,128]{2,1,0:T(8,128)S(1)}, f32[8,72,128]{2,1,0:T(8,128)S(1)}, u32[]{:S(2)}, u32[]{:S(2)}) collective-permute-start(f32[8,72,128]{2,1,0:T(8,128)S(1)} %pad_maximum_fusion.9), channel_id=1, source_target_pairs={{0,2},{2,0},{4,6},{6,4},{8,10},{10,8},{12,14},{14,12},{16,18},{18,... | collective-permute-start | bytes 884744 | tf_op jit(solution)/shard_map/ppermute | solution.py:36
  34.3 8.3 %collective-permute-start.12 = (f32[2,384,128]{2,1,0:T(8,128)S(1)}, f32[2,384,128]{2,1,0:T(8,128)S(1)}, u32[]{:S(2)}, u32[]{:S(2)}) collective-permute-start(f32[2,384,128]{2,1,0:T(8,128)S(1)} %pad_maximum_fusion.8), channel_id=1, source_target_pairs={{0,8},{2,10},{4,12},{6,14},{8,0},{10,2},{12,4},{14,6},{16,24},{18,... | collective-permute-start | bytes 1179656 | tf_op jit(solution)/shard_map/ppermute | solution.py:36
  35.1 11.4 %collective-permute-start.16 = (f32[4,128,128]{2,1,0:T(8,128)}, f32[4,128,128]{2,1,0:T(8,128)}, u32[]{:S(2)}, u32[]{:S(2)}) collective-permute-start(f32[4,128,128]{2,1,0:T(8,128)} %get-tuple-element.58), channel_id=1, source_target_pairs={{0,2},{2,0},{4,6},{6,4},{8,10},{10,8},{12,14},{14,12},{16,18},{18,... | collective-permute-start | bytes 786440 | tf_op jit(solution)/shard_map/ppermute | solution.py:36
  35.7 8.5 %collective-permute-start.10 = (f32[4,128,128]{2,1,0:T(8,128)S(1)}, f32[4,128,128]{2,1,0:T(8,128)}, u32[]{:S(2)}, u32[]{:S(2)}) collective-permute-start(f32[4,128,128]{2,1,0:T(8,128)S(1)} %get-tuple-element.59), channel_id=1, source_target_pairs={{0,4},{2,6},{4,0},{6,2},{8,12},{10,14},{12,8},{14,10},{16,20},{18,... | collective-permute-start | bytes 786440 | tf_op jit(solution)/shard_map/ppermute | solution.py:36
  36.7 11.0 %collective-permute-start.7 = (f32[16,64,128]{2,1,0:T(8,128)S(1)}, f32[16,64,128]{2,1,0:T(8,128)S(1)}, u32[]{:S(2)}, u32[]{:S(2)}) collective-permute-start(f32[16,64,128]{2,1,0:T(8,128)S(1)} %pad_maximum_fusion.4.b_own), channel_id=1, source_target_pairs={{0,1},{1,0},{2,3},{3,2},{4,5},{5,4},{6,7},{7,6},{8,9},{9,8},{10,11... | collective-permute-start | bytes 1572872 | tf_op jit(solution)/shard_map/ppermute | solution.py:36
  36.8 12.8 %collective-permute-start.4 = (f32[16,72,128]{2,1,0:T(8,128)S(1)}, f32[16,72,128]{2,1,0:T(8,128)S(1)}, u32[]{:S(2)}, u32[]{:S(2)}) collective-permute-start(f32[16,72,128]{2,1,0:T(8,128)S(1)} %pad_maximum_fusion.3.a_own), channel_id=1, source_target_pairs={{0,1},{1,0},{2,3},{3,2},{4,5},{5,4},{6,7},{7,6},{8,9},{9,8},{10,11... | collective-permute-start | bytes 1769480 | tf_op jit(solution)/shard_map/ppermute | solution.py:36
  43.6 19.6 %collective-permute-start.14 = (f32[4,192,128]{2,1,0:T(8,128)}, f32[4,192,128]{2,1,0:T(8,128)}, u32[]{:S(2)}, u32[]{:S(2)}) collective-permute-start(f32[4,192,128]{2,1,0:T(8,128)} %get-tuple-element.56), channel_id=1, source_target_pairs={{0,2},{2,0},{4,6},{6,4},{8,10},{10,8},{12,14},{14,12},{16,18},{18,... | collective-permute-start | bytes 1179656 | tf_op jit(solution)/shard_map/ppermute | solution.py:36
  44.2 19.0 %collective-permute-start.13 = (f32[4,192,128]{2,1,0:T(8,128)}, f32[4,192,128]{2,1,0:T(8,128)}, u32[]{:S(2)}, u32[]{:S(2)}) collective-permute-start(f32[4,192,128]{2,1,0:T(8,128)} %get-tuple-element.57), channel_id=1, source_target_pairs={{0,4},{2,6},{4,0},{6,2},{8,12},{10,14},{12,8},{14,10},{16,20},{18,... | collective-permute-start | bytes 1179656 | tf_op jit(solution)/shard_map/ppermute | solution.py:36
  46.5 20.5 %collective-permute-start.18 = (f32[8,128,128]{2,1,0:T(8,128)S(1)}, f32[8,128,128]{2,1,0:T(8,128)S(1)}, u32[]{:S(2)}, u32[]{:S(2)}) collective-permute-start(f32[8,128,128]{2,1,0:T(8,128)S(1)} %pad_maximum_fusion.6.refs_0_), channel_id=1, source_target_pairs={{0,1},{1,0},{2,3},{3,2},{4,5},{5,4},{6,7},{7,6},{8,9},{9,8},{10,11... | collective-permute-start | bytes 1572872 | tf_op jit(solution)/shard_map/ppermute | solution.py:36
  47.7 18.8 %collective-permute-start.17 = (f32[8,128,128]{2,1,0:T(8,128)S(1)}, f32[8,128,128]{2,1,0:T(8,128)S(1)}, u32[]{:S(2)}, u32[]{:S(2)}) collective-permute-start(f32[8,128,128]{2,1,0:T(8,128)S(1)} %pad_maximum_fusion.7.refs_4_), channel_id=1, source_target_pairs={{0,4},{2,6},{4,0},{6,2},{8,12},{10,14},{12,8},{14,10},{16,20},{18,... | collective-permute-start | bytes 1572872 | tf_op jit(solution)/shard_map/ppermute | solution.py:36
  49.6 16.9 %collective-permute-start.15 = (f32[8,128,128]{2,1,0:T(8,128)S(1)}, f32[8,128,128]{2,1,0:T(8,128)S(1)}, u32[]{:S(2)}, u32[]{:S(2)}) collective-permute-start(f32[8,128,128]{2,1,0:T(8,128)S(1)} %pad_maximum_fusion.6.refs_0_), channel_id=1, source_target_pairs={{0,2},{2,0},{4,6},{6,4},{8,10},{10,8},{12,14},{14,12},{16,18},{18,... | collective-permute-start | bytes 1572872 | tf_op jit(solution)/shard_map/ppermute | solution.py:36
  64.4 19.7 %collective-permute-start.23 = (f32[8,192,128]{2,1,0:T(8,128)S(1)}, f32[8,192,128]{2,1,0:T(8,128)S(1)}, u32[]{:S(2)}, u32[]{:S(2)}) collective-permute-start(f32[8,192,128]{2,1,0:T(8,128)S(1)} %pad_maximum_fusion.2.refs_6_), channel_id=1, source_target_pairs={{0,4},{2,6},{4,0},{6,2},{8,12},{10,14},{12,8},{14,10},{16,20},{18,... | collective-permute-start | bytes 2359304 | tf_op jit(solution)/shard_map/ppermute | solution.py:36
  65.8 19.4 %collective-permute-start.22 = (f32[8,192,128]{2,1,0:T(8,128)S(1)}, f32[8,192,128]{2,1,0:T(8,128)S(1)}, u32[]{:S(2)}, u32[]{:S(2)}) collective-permute-start(f32[8,192,128]{2,1,0:T(8,128)S(1)} %pad_maximum_fusion.1.refs_4_), channel_id=1, source_target_pairs={{0,2},{2,0},{4,6},{6,4},{8,10},{10,8},{12,14},{14,12},{16,18},{18,... | collective-permute-start | bytes 2359304 | tf_op jit(solution)/shard_map/ppermute | solution.py:36
  66.5 5.1 %collective-permute-start.21 = (f32[8,128,128]{2,1,0:T(8,128)S(1)}, f32[8,128,128]{2,1,0:T(8,128)S(1)}, u32[]{:S(2)}, u32[]{:S(2)}) collective-permute-start(f32[8,128,128]{2,1,0:T(8,128)S(1)} %collective-permute-done.17.refs_5_), channel_id=1, source_target_pairs={{0,1},{1,0},{2,3},{3,2},{4,5},{5,4},{6,7},{7,6},{8,9},{9,8},{10,11... | collective-permute-start | bytes 1572872 | tf_op jit(solution)/shard_map/ppermute | solution.py:36
  71.1 19.0 %collective-permute-start.26 = (f32[8,192,128]{2,1,0:T(8,128)S(1)}, f32[8,192,128]{2,1,0:T(8,128)S(1)}, u32[]{:S(2)}, u32[]{:S(2)}) collective-permute-start(f32[8,192,128]{2,1,0:T(8,128)S(1)} %pad_maximum_fusion.2.refs_6_), channel_id=1, source_target_pairs={{0,1},{1,0},{2,3},{3,2},{4,5},{5,4},{6,7},{7,6},{8,9},{9,8},{10,11... | collective-permute-start | bytes 2359304 | tf_op jit(solution)/shard_map/ppermute | solution.py:36
  71.6 18.5 %collective-permute-start.24 = (f32[8,192,128]{2,1,0:T(8,128)S(1)}, f32[8,192,128]{2,1,0:T(8,128)S(1)}, u32[]{:S(2)}, u32[]{:S(2)}) collective-permute-start(f32[8,192,128]{2,1,0:T(8,128)S(1)} %pad_maximum_fusion.1.refs_4_), channel_id=1, source_target_pairs={{0,1},{1,0},{2,3},{3,2},{4,5},{5,4},{6,7},{7,6},{8,9},{9,8},{10,11... | collective-permute-start | bytes 2359304 | tf_op jit(solution)/shard_map/ppermute | solution.py:36
  85.2 5.0 %collective-permute-start.27 = (f32[8,192,128]{2,1,0:T(8,128)S(1)}, f32[8,192,128]{2,1,0:T(8,128)S(1)}, u32[]{:S(2)}, u32[]{:S(2)}) collective-permute-start(f32[8,192,128]{2,1,0:T(8,128)S(1)} %collective-permute-done.23.refs_7_), channel_id=1, source_target_pairs={{0,1},{1,0},{2,3},{3,2},{4,5},{5,4},{6,7},{7,6},{8,9},{9,8},{10,11... | collective-permute-start | bytes 2359304 | tf_op jit(solution)/shard_map/ppermute | solution.py:36
  85.2 5.0 %collective-permute-start.25 = (f32[8,192,128]{2,1,0:T(8,128)S(1)}, f32[8,192,128]{2,1,0:T(8,128)S(1)}, u32[]{:S(2)}, u32[]{:S(2)}) collective-permute-start(f32[8,192,128]{2,1,0:T(8,128)S(1)} %collective-permute-done.22.refs_5_), channel_id=1, source_target_pairs={{0,1},{1,0},{2,3},{3,2},{4,5},{5,4},{6,7},{7,6},{8,9},{9,8},{10,11... | collective-permute-start | bytes 2359304 | tf_op jit(solution)/shard_map/ppermute | solution.py:36
  108.1 8.4 %collective-permute-start.31 = (f32[512,128]{1,0:T(8,128)S(1)}, f32[512,128]{1,0:T(8,128)S(1)}, u32[]{:S(2)}, u32[]{:S(2)}) collective-permute-start(f32[512,128]{1,0:T(8,128)S(1)} %bitcast.109), channel_id=1, source_target_pairs={{0,4},{2,6},{4,0},{6,2},{8,12},{10,14},{12,8},{14,10},{16,20},{18,... | collective-permute-start | bytes 786440 | tf_op jit(solution)/shard_map/ppermute | solution.py:36
  109.9 8.2 %collective-permute-start.29 = (f32[520,128]{1,0:T(8,128)S(1)}, f32[520,128]{1,0:T(8,128)S(1)}, u32[]{:S(2)}, u32[]{:S(2)}) collective-permute-start(f32[520,128]{1,0:T(8,128)S(1)} %pad_maximum_fusion.11), channel_id=1, source_target_pairs={{0,2},{2,0},{4,6},{6,4},{8,10},{10,8},{12,14},{14,12},{16,18},{18,... | collective-permute-start | bytes 798728 | tf_op jit(solution)/shard_map/ppermute | solution.py:36
  116.6 5.0 %collective-permute-start.32 = (f32[256,128]{1,0:T(8,128)S(1)}, f32[256,128]{1,0:T(8,128)S(1)}, u32[]{:S(2)}, u32[]{:S(2)}) collective-permute-start(f32[256,128]{1,0:T(8,128)S(1)} %bitcast.113), channel_id=1, source_target_pairs={{0,2},{2,0},{4,6},{6,4},{8,10},{10,8},{12,14},{14,12},{16,18},{18,... | collective-permute-start | bytes 393224 | tf_op jit(solution)/shard_map/ppermute | solution.py:36
  118.2 5.1 %collective-permute-start.30 = (f32[264,128]{1,0:T(8,128)S(1)}, f32[264,128]{1,0:T(8,128)S(1)}, u32[]{:S(2)}, u32[]{:S(2)}) collective-permute-start(f32[264,128]{1,0:T(8,128)S(1)} %pad_maximum_fusion.15), channel_id=1, source_target_pairs={{0,4},{2,6},{4,0},{6,2},{8,12},{10,14},{12,8},{14,10},{16,20},{18,... | collective-permute-start | bytes 405512 | tf_op jit(solution)/shard_map/ppermute | solution.py:36
  123.4 5.1 %collective-permute-start.33 = (f32[264,128]{1,0:T(8,128)S(1)}, f32[264,128]{1,0:T(8,128)S(1)}, u32[]{:S(2)}, u32[]{:S(2)}) collective-permute-start(f32[264,128]{1,0:T(8,128)S(1)} %pad_maximum_fusion.16), channel_id=1, source_target_pairs={{0,8},{2,10},{4,12},{6,14},{8,0},{10,2},{12,4},{14,6},{16,24},{18,... | collective-permute-start | bytes 405512 | tf_op jit(solution)/shard_map/ppermute | solution.py:36
  128.6 5.4 %collective-permute-start.34 = (f32[136,128]{1,0:T(8,128)S(1)}, f32[136,128]{1,0:T(8,128)S(1)}, u32[]{:S(2)}, u32[]{:S(2)}) collective-permute-start(f32[136,128]{1,0:T(8,128)S(1)} %pad_maximum_fusion.18), channel_id=1, source_target_pairs={{0,16},{2,18},{4,20},{6,22},{8,24},{10,26},{12,28},{14,30},{16,0},... | collective-permute-start | bytes 208904 | tf_op jit(solution)/shard_map/ppermute | solution.py:36
  (12 other events, 90.0 us)
